TPU v7x, 32 devices: a whole 2x2x4 slice. The times are simulated.
32 devices in a mesh: dp: 4 (over y, x), seq: 8 (over z, core).
Axes of the slice: x: 2, y: 2, z: 4, core: 2. Of those that a mesh axis runs over, the one named last changes fastest.
Arguments:
- block_in: bfloat16 [4, 4, 2048, 512], P('dp', None, 'seq'), may hold values from -6 to 6
- cotangent: bfloat16 [4, 4, 2048, 512], P('dp', None, 'seq'), may hold values from -6 to 6
- bucket_id: int32 [4, 4, 16], P('dp'), may hold values from 0 to 2, as said below
- assignment: int32 [4, 4], P('dp'), may hold values from 0 to 3, each once within a row
- norm_gain: float32 [512], replicated, may hold values from 0.25 to 1.75
- b_proj: bfloat16 [512, 512], replicated, may hold values from -0.25 to 0.25
- gamma_log: float32 [256], replicated, may hold values from -7 to -0.8
- nu_log: float32 [256], replicated
- theta_log: float32 [256], replicated, may hold values from -6.9 to 1.1
- c_proj: bfloat16 [512, 512], replicated, may hold values from -0.375 to 0.375
- d_skip: float32 [512], replicated, may hold values from -4 to 4
- glu_weight: bfloat16 [512, 1024], replicated, may hold values from -0.25 to 0.25
Outputs:
- block_out: bfloat16 [4, 4, 2048, 512], P('dp', None, 'seq')
- grad_in: bfloat16 [4, 4, 2048, 512], P('dp', None, 'seq')
- grad_norm_gain: float32 [512], replicated
- grad_b_proj: float32 [512, 512], replicated
- grad_gamma_log: float32 [256], replicated
- grad_nu_log: float32 [256], replicated
- grad_theta_log: float32 [256], replicated
- grad_c_proj: float32 [512, 512], replicated
- grad_d_skip: float32 [512], replicated
- grad_glu_weight: float32 [512, 1024], replicated
Inputs may be any that keep to these rules, and one draw needn't show every extreme that they name: `bucket_id`: bucket 0 is 128 tokens, bucket 1 is 512 tokens, bucket 2 is 2048 tokens; a run of equal ids covers whole aligned runs of that bucket's length; pattern 0 of every group is bucket 2 throughout, the others hold buckets 0 and 1. `assignment`: in each group every pattern is held by exactly one lane.
All inputs are finite; a program needn't handle non-finite values.
Results may differ from a plain program's by a relative error of at most 0.012.
Values sent between devices are 32-bit elements; how exact they have to be, the bound alone decides.
No kernel may reach another device: no remote copies, remote signals or barrier semaphores. Data moves between devices by JAX's collectives and lax.ppermute only.
A program may use at most 128 MiB of HBM per device.

v0:
```python
import functools

import jax
import jax.numpy as jnp
from jax import lax
from jax.experimental import pallas as pl
from jax.experimental.pallas import tpu as pltpu
from jax.sharding import PartitionSpec as P

EPS = 1e-05
CHUNKS = 8
LANE = 128
GELU_A = 0.044715
GELU_K = 0.7978845608028654
F32 = jnp.float32
BF16 = jnp.bfloat16


def dot_nt(left, right):
    return lax.dot_general(left, right, (((1,), (1,)), ((), ())), preferred_element_type=F32)


def dot_tn(left, right):
    return lax.dot_general(left, right, (((0,), (0,)), ((), ())), preferred_element_type=F32)


def dot_nn(left, right):
    return jnp.dot(left, right, preferred_element_type=F32)


def cmul(x, y):
    return x[0] * y[0] - x[1] * y[1], x[0] * y[1] + x[1] * y[0]


def cadd(x, y):
    return x[0] + y[0], x[1] + y[1]


def fma(a, x, y):
    return (y[0] - a[1] * x[1]) + a[0] * x[0], (y[1] + a[1] * x[0]) + a[0] * x[1]


def conj(x):
    return x[0], -x[1]


def cload(ref, first, count=1):
    n = ref.shape[-1] // 2
    return ref[first : first + count, :n], ref[first : first + count, n:]


def cstore(ref, first, value):
    n = ref.shape[-1] // 2
    rows = value[0].shape[0]
    ref[first : first + rows, :n], ref[first : first + rows, n:] = value


def kept(ref, row, value):
    keep = cload(ref, row)
    return value[0] * keep[0], value[1] * keep[1]


def scan_order(seg, back=False):
    row = lax.broadcasted_iota(jnp.int32, (seg, seg), 0)
    column = lax.broadcasted_iota(jnp.int32, (seg, seg), 1)
    if back:
        row, column = column, row
    span = seg // CHUNKS
    hit = (row % CHUNKS == column // span) & (row // CHUNKS == column % span)
    return jnp.where(hit, 1.0, 0.0).astype(BF16)


def fill_keeps(bucket, assign, keep_ref, lanes, seg, short):
    own = lax.axis_index("seq")
    for lane in range(lanes):
        pattern = assign[0, lane]
        for chunk in range(CHUNKS):
            token = own * seg + chunk * (seg // CHUNKS)
            here = bucket[pattern, lax.div(token, short)]
            span = jnp.where(here == 0, short, jnp.where(here == 1, 4 * short, 16 * short))
            keep = jnp.where(lax.rem(token, span) == 0, 0.0, 1.0).astype(F32)
            row = lane * CHUNKS + chunk
            keep_ref[row : row + 1, :] = jnp.full((1, keep_ref.shape[1]), keep)


def norm_stats(rows):
    mean = jnp.mean(rows, axis=-1, keepdims=True)
    centred = rows - mean
    var = jnp.mean(centred * centred, axis=-1, keepdims=True)
    scale = lax.rsqrt(var + EPS)
    return centred * scale, scale


def cost(micros):
    return pl.CostEstimate(flops=int(micros * 1.1e9), bytes_accessed=int(micros * 3e6), transcendentals=0)


def put_halves(value, keep, send):
    rows = value.shape[0] // 2
    first = lax.rem(lax.axis_index("seq"), 2) == 0
    top, bottom = value[:rows], value[rows:]
    keep[...] = jnp.where(first, top, bottom)
    send[...] = jnp.where(first, bottom, top)


class Copies:
    def __init__(self, sems):
        self.sems, self.all = sems, []

    def start(self, source, target):
        copy = pltpu.make_async_copy(source, target, self.sems.at[len(self.all)])
        copy.start()
        self.all.append(copy)
        return copy

    def lanes(self, lanes, *pairs):
        return [
            [self.start(lane_of(source, lane, lanes), lane_of(target, lane, lanes)) for source, target in pairs]
            for lane in range(lanes)
        ]


def lane_of(ref, lane, lanes):
    if len(ref.shape) == 3:
        return ref.at[lane]
    rows = ref.shape[0] // lanes
    return ref.at[pl.ds(lane * rows, rows)]


def wait(copies):
    for copy in copies:
        copy.wait()


def first_kernel(
    short, bucket_hbm, assign_hbm, x_hbm, gain_hbm, b_hbm, gamma_hbm, nu_hbm, th_hbm,
    xs_hbm, normed_hbm, loc_hbm, pair_ref, pow_ref, keep_ref,
    bucket, assign, x_ref, gain_ref, b_ref, gamma_ref, nu_ref, th_ref, xs_ref, normed_ref, loc_ref, sems,
):
    lanes, seg, width = x_ref.shape
    span = seg // CHUNKS
    copies = Copies(sems)
    x_here = copies.lanes(lanes, (x_hbm, x_ref))
    nu_here, th_here = copies.start(nu_hbm, nu_ref), copies.start(th_hbm, th_ref)
    gain_here, gamma_here = copies.start(gain_hbm, gain_ref), copies.start(gamma_hbm, gamma_ref)
    b_here = copies.start(b_hbm, b_ref)
    tables = copies.start(bucket_hbm, bucket), copies.start(assign_hbm, assign)
    leaving = []

    order = scan_order(seg)
    nu_here.wait(), th_here.wait()
    modulus = jnp.exp(-jnp.exp(nu_ref[...]))
    phase = jnp.exp(th_ref[...])
    cstore(pow_ref, 0, (modulus * jnp.cos(phase), modulus * jnp.sin(phase)))
    size = 1
    while size < span:
        cstore(pow_ref, size, cmul(cload(pow_ref, 0, size), cload(pow_ref, size - 1)))
        size *= 2

    gain_here.wait(), gamma_here.wait()
    factor = jnp.exp(gamma_ref[...])
    factor = jnp.concatenate([factor, factor], 1)
    for lane in range(lanes):
        rows = pl.ds(lane * seg, seg)
        wait(x_here[lane])
        x = dot_nn(order, x_ref[lane])
        xs_ref[rows, :] = x.astype(BF16)
        xhat, _ = norm_stats(x)
        low = (xhat * gain_ref[...]).astype(BF16)
        normed_ref[rows, :] = low
        if lane == 0:
            b_here.wait()
        loc_ref[rows, :] = dot_nn(low, b_ref[...]) * factor
        for source, target in ((xs_ref, xs_hbm), (normed_ref, normed_hbm)):
            leaving.append(copies.start(source.at[rows], target.at[rows]))

    for table in tables:
        table.wait()
    fill_keeps(bucket, assign, keep_ref, lanes, seg, short)
    lam = cload(pow_ref, 0)
    lam_span = cload(pow_ref, span - 1)
    for lane in range(lanes):
        h = cload(loc_ref, lane * seg, CHUNKS)
        for step in range(1, span):
            at = lane * seg + step * CHUNKS
            h = fma(lam, h, cload(loc_ref, at, CHUNKS))
            cstore(loc_ref, at, h)
        rows = pl.ds(lane * seg, seg)
        leaving.append(copies.start(loc_ref.at[rows], loc_hbm.at[rows]))
        state = h[0][0:1], h[1][0:1]
        decay = kept(keep_ref, lane * CHUNKS, lam_span)
        for chunk in range(1, CHUNKS):
            step = kept(keep_ref, lane * CHUNKS + chunk, lam_span)
            state = fma(step, state, (h[0][chunk : chunk + 1], h[1][chunk : chunk + 1]))
            decay = cmul(step, decay)
        cstore(pair_ref, lane, state)
        cstore(pair_ref, lanes + lane, decay)
    wait(leaving)


def block_kernel(
    ct_hbm, c_hbm, d_hbm, w_hbm, xs_hbm, normed_hbm, loc_hbm, enter_ref, pow_ref, keep_ref,
    out_hbm, cts_hbm, h_hbm, carry_ref, states_ref, slope_ref, pre_ref, go_ref, send_ref,
    ct_ref, c_ref, d_ref, w_ref, xs_ref, normed_ref, h_ref, out_ref, cts_ref, gelu_ref, sems,
):
    lanes, seg, width = ct_ref.shape
    copies = Copies(sems)
    loc_here = copies.lanes(lanes, (loc_hbm, h_ref))
    c_here, d_here = copies.start(c_hbm, c_ref), copies.start(d_hbm, d_ref)
    normed_here = copies.lanes(lanes, (normed_hbm, normed_ref))
    w_here = copies.start(w_hbm, w_ref)
    rest_here = copies.lanes(lanes, (xs_hbm, xs_ref), (ct_hbm, ct_ref))
    leaving = []
    span = seg // CHUNKS
    lam_span = cload(pow_ref, span - 1)
    order, order_back = scan_order(seg), scan_order(seg, True)
    for lane in range(lanes):
        first = lane * seg
        rows = pl.ds(first, seg)
        wait(loc_here[lane])
        last = first + (span - 1) * CHUNKS
        state = kept(keep_ref, lane * CHUNKS, cload(enter_ref, lane))
        cstore(carry_ref, lane * CHUNKS, state)
        for chunk in range(1, CHUNKS):
            state = fma(lam_span, state, cload(h_ref, last + chunk - 1))
            state = kept(keep_ref, lane * CHUNKS + chunk, state)
            cstore(carry_ref, lane * CHUNKS + chunk, state)
        carry = cload(carry_ref, lane * CHUNKS, CHUNKS)
        for step in range(span):
            at = first + step * CHUNKS
            cstore(h_ref, at, fma(cload(pow_ref, step), carry, cload(h_ref, at, CHUNKS)))
        leaving.append(copies.start(h_ref.at[rows], h_hbm.at[rows]))

        states = h_ref[rows, :].astype(BF16)
        states_ref[rows, :] = states
        if lane == 0:
            c_here.wait(), d_here.wait()
        wait(normed_here[lane])
        mixed = dot_nn(states, c_ref[...]) + d_ref[...] * normed_ref[rows, :].astype(F32)
        square = mixed * mixed
        tanh = jnp.tanh(GELU_K * mixed * (1.0 + GELU_A * square))
        half_up = 0.5 * (1.0 + tanh)
        gelu = (mixed * half_up).astype(BF16)
        gelu_ref[rows, :] = gelu
        slope_ref[rows, :] = half_up + 0.5 * GELU_K * mixed * (1.0 - tanh * tanh) * (
            1.0 + 3.0 * GELU_A * square
        )
        if lane == 0:
            w_here.wait()
        pre = dot_nn(gelu, w_ref[...])
        value = pre[:, :width]
        sig = jax.nn.sigmoid(pre[:, width:])
        gated = value * sig
        wait(rest_here[lane])
        out = (xs_ref[rows, :].astype(F32) + gated).astype(BF16)
        out_ref[lane] = dot_nn(order_back, out).astype(BF16)
        leaving.append(copies.start(out_ref.at[lane], out_hbm.at[lane]))
        cot = dot_nn(order, ct_ref[lane])
        cts_ref[rows, :] = cot.astype(BF16)
        leaving.append(copies.start(cts_ref.at[rows], cts_hbm.at[rows]))
        grad_value = cot * sig
        pre_ref[rows, :width] = grad_value.astype(BF16)
        pre_ref[rows, width:] = (grad_value * (value - gated)).astype(BF16)
    put_halves(dot_tn(gelu_ref[...], pre_ref[...]), go_ref, send_ref)
    wait(leaving)


def adjoint_kernel(
    w_hbm, c_hbm, normed_hbm, pre_ref, slope_ref, states_ref, pow_ref, keep_ref,
    mixed_hbm, adj_hbm, back_ref, g_d_ref, go_ref, send_ref,
    w_ref, c_ref, normed_ref, mixed_ref, adj_ref, low_ref, sems,
):
    copies = Copies(sems)
    w_here, c_here = copies.start(w_hbm, w_ref), copies.start(c_hbm, c_ref)
    normed_here = copies.lanes(back_ref.shape[0], (normed_hbm, normed_ref))
    leaving = []
    lanes = back_ref.shape[0]
    seg = pre_ref.shape[0] // lanes
    span = seg // CHUNKS
    lam, lam_span = conj(cload(pow_ref, 0)), conj(cload(pow_ref, span - 1))
    total = None
    w_here.wait()
    for lane in range(lanes):
        rows = pl.ds(lane * seg, seg)
        grad_mixed = dot_nt(pre_ref[rows, :], w_ref[...]) * slope_ref[rows, :]
        mixed_ref[rows, :] = grad_mixed
        leaving.append(copies.start(mixed_ref.at[rows], mixed_hbm.at[rows]))
        wait(normed_here[lane])
        add = jnp.sum(grad_mixed * normed_ref[rows, :].astype(F32), axis=0, keepdims=True)
        total = add if total is None else total + add
        low = grad_mixed.astype(BF16)
        low_ref[rows, :] = low
        if lane == 0:
            c_here.wait()
        adj_ref[rows, :] = dot_nt(low, c_ref[...])
    g_d_ref[...] = total
    for lane in range(lanes):
        adj = cload(adj_ref, (lane + 1) * seg - CHUNKS, CHUNKS)
        for step in reversed(range(span - 1)):
            at = lane * seg + step * CHUNKS
            adj = fma(lam, adj, cload(adj_ref, at, CHUNKS))
            cstore(adj_ref, at, adj)
        rows = pl.ds(lane * seg, seg)
        leaving.append(copies.start(adj_ref.at[rows], adj_hbm.at[rows]))
        state = None
        for chunk in reversed(range(CHUNKS)):
            here = adj[0][chunk : chunk + 1], adj[1][chunk : chunk + 1]
            state = here if state is None else fma(lam_span, state, here)
            state = kept(keep_ref, lane * CHUNKS + chunk, state)
        cstore(back_ref, lane, state)
    put_halves(dot_tn(states_ref[...], low_ref[...]), go_ref, send_ref)
    wait(leaving)


def states_kernel(
    b_hbm, gamma_hbm, d_hbm, normed_hbm, h_hbm, adj_hbm, leave_ref, carry_ref, pow_ref, keep_ref, g_d_ref,
    low_hbm, go_ref, send_ref, small_ref,
    b_ref, gamma_ref, d_ref, normed_ref, h_ref, adj_ref, low_ref, after_ref, sems,
):
    copies = Copies(sems)
    lanes_here = copies.lanes(leave_ref.shape[0], (adj_hbm, adj_ref), (h_hbm, h_ref))
    normed_here = copies.start(normed_hbm, normed_ref)
    leaving = []
    b_here, gamma_here, d_here = (
        copies.start(a, b) for a, b in ((b_hbm, b_ref), (gamma_hbm, gamma_ref), (d_hbm, d_ref))
    )
    lanes = leave_ref.shape[0]
    seg = normed_ref.shape[0] // lanes
    span = seg // CHUNKS
    back = conj(cload(pow_ref, span - 1))
    gamma_here.wait()
    factor = jnp.exp(gamma_ref[...])
    sums = None
    for lane in range(lanes):
        first = lane * seg
        state = cload(leave_ref, lane)
        wait(lanes_here[lane])
        cstore(after_ref, CHUNKS - 1, state)
        for chunk in reversed(range(1, CHUNKS)):
            state = fma(back, state, cload(adj_ref, first + chunk))
            state = kept(keep_ref, lane * CHUNKS + chunk, state)
            cstore(after_ref, chunk - 1, state)
        after = cload(after_ref, 0, CHUNKS)
        before = cload(carry_ref, lane * CHUNKS, CHUNKS)
        for step in range(span):
            at = first + step * CHUNKS
            full = fma(conj(cload(pow_ref, span - 1 - step)), after, cload(adj_ref, at, CHUNKS))
            add = cmul(conj(before), full)
            sums = add if sums is None else cadd(sums, add)
            cstore(low_ref, at, ((full[0] * factor).astype(BF16), (full[1] * factor).astype(BF16)))
            before = cload(h_ref, at, CHUNKS)
        rows = pl.ds(first, seg)
        leaving.append(copies.start(low_ref.at[rows], low_hbm.at[rows]))
    normed_here.wait()
    grad_b = dot_tn(normed_ref[...], low_ref[...])
    put_halves(grad_b, go_ref, send_ref)
    b_here.wait(), d_here.wait()
    prod = grad_b * b_ref[...].astype(F32)
    small_ref[...] = jnp.zeros_like(small_ref)
    n = gamma_ref.shape[1]
    small_ref[0:1, :n] = jnp.sum(sums[0], axis=0, keepdims=True)
    small_ref[0:1, n:] = jnp.sum(sums[1], axis=0, keepdims=True)
    small_ref[1:2, :] = jnp.sum(prod, axis=0, keepdims=True)
    small_ref[2:3, :] = jnp.sum(prod.T, axis=0, keepdims=True) + d_ref[...] * g_d_ref[...]
    small_ref[3:4, :] = g_d_ref[...]
    wait(leaving)


def input_kernel(
    gain_hbm, b_hbm, d_hbm, xs_hbm, cts_hbm, low_hbm, mixed_hbm,
    in_hbm, gain_ref, b_ref, d_ref, xs_ref, cts_ref, low_ref, mixed_ref, in_ref, sems,
):
    lanes, seg, width = in_ref.shape
    copies = Copies(sems)
    params = [copies.start(a, b) for a, b in ((gain_hbm, gain_ref), (b_hbm, b_ref), (d_hbm, d_ref))]
    here = copies.lanes(
        lanes, (low_hbm, low_ref), (mixed_hbm, mixed_ref), (xs_hbm, xs_ref), (cts_hbm, cts_ref)
    )
    wait(params)
    leaving = []
    order_back = scan_order(seg, True)
    for lane in range(lanes):
        rows = pl.ds(lane * seg, seg)
        wait(here[lane])
        grad_normed = dot_nt(low_ref[rows, :], b_ref[...]) + mixed_ref[rows, :] * d_ref[...]
        xhat, scale = norm_stats(xs_ref[rows, :].astype(F32))
        dxhat = grad_normed * gain_ref[...]
        one = jnp.mean(dxhat, axis=-1, keepdims=True)
        two = jnp.mean(dxhat * xhat, axis=-1, keepdims=True)
        grad = (cts_ref[rows, :].astype(F32) + (dxhat - one - xhat * two) * scale).astype(BF16)
        in_ref[lane] = dot_nn(order_back, grad).astype(BF16)
        leaving.append(copies.start(in_ref.at[lane], in_hbm.at[lane]))
    wait(leaving)


def finish_kernel(
    nu_hbm, th_hbm, gain_hbm, small_ref, pow_ref, gain_out, gamma_out, nu_out, th_out, d_out,
    nu_ref, th_ref, gain_ref, sems,
):
    n = nu_ref.shape[1]
    copies = Copies(sems)
    for copy in [copies.start(a, b) for a, b in ((nu_hbm, nu_ref), (th_hbm, th_ref), (gain_hbm, gain_ref))]:
        copy.wait()
    lam = cload(pow_ref, 0)
    p, q = small_ref[0:1, :n], small_ref[0:1, n:]
    nu_out[...] = -jnp.exp(nu_ref[...]) * (p * lam[0] + q * lam[1])
    th_out[...] = -jnp.exp(th_ref[...]) * (p * lam[1] - q * lam[0])
    gamma_out[...] = small_ref[1:2, :n] + small_ref[1:2, n:]
    gain_out[...] = small_ref[2:3, :] / gain_ref[...]
    d_out[...] = small_ref[3:4, :]


def swap(value, axis, bit):
    count = lax.axis_size(axis)
    return lax.ppermute(value, axis, [(i, i ^ (1 << bit)) for i in range(count)])


def entering(pair, backward, beside=None):
    lanes, n = pair.shape[0] // 2, pair.shape[1] // 2

    def mul(x, y):
        return jnp.concatenate(
            [x[:, :n] * y[:, :n] - x[:, n:] * y[:, n:], x[:, :n] * y[:, n:] + x[:, n:] * y[:, :n]], 1
        )

    count, mine = lax.axis_size("seq"), lax.axis_index("seq")
    total, decay = pair[:lanes], pair[lanes:]
    prefix = through = None
    for bit in range(count.bit_length() - 1):
        sent = jnp.concatenate([total, decay], 0)
        if beside is not None and bit == 1:
            sent, beside = tie(sent, beside)
        got = swap(sent, "seq", bit)
        other, other_decay = got[:lanes], got[lanes:]
        later = (lax.div(mine, 1 << bit) % 2 == 1) != backward
        if prefix is None:
            unit = jnp.concatenate([jnp.ones_like(pair[:lanes, :n]), jnp.zeros_like(pair[:lanes, n:])], 1)
            prefix = jnp.where(later, other, 0.0)
            through = jnp.where(later, other_decay, unit)
        else:
            prefix = jnp.where(later, prefix + mul(through, other), prefix)
            through = jnp.where(later, mul(through, other_decay), through)
        total = jnp.where(later, total + mul(decay, other), other + mul(other_decay, total))
        decay = mul(decay, other_decay)
    return prefix, beside


def bit_of(dim):
    axis, bit = dim
    return lax.axis_index(axis) // (1 << bit) % 2


def cut_rows(value, which):
    rows = value.shape[0] // 2
    return lax.dynamic_slice(value, (which * rows, 0), (rows, value.shape[1]))


def scatter(value, dim, extra=None):
    mine = bit_of(dim)
    send, keep = cut_rows(value, 1 - mine), cut_rows(value, mine)
    if extra is None:
        return keep + swap(send, *dim), None
    rows = send.shape[0]
    got = swap(jnp.concatenate([send, extra], 0), *dim)
    return keep + got[:rows], extra + got[rows:]


def gather(value, dim):
    mine, got = bit_of(dim), swap(value, *dim)
    return jnp.where(
        mine == 0, jnp.concatenate([value, got], 0), jnp.concatenate([got, value], 0)
    )


def bits(axis, first=0):
    return [(axis, bit) for bit in range(first, lax.axis_size(axis).bit_length() - 1)]


def tie(*values):
    return lax.optimization_barrier(values)


def dp_orders():
    return [bits("dp"), bits("dp")[::-1]]


def scatter_dp(parts, position, extra=None):
    orders = dp_orders()
    first, _ = scatter(parts[0], orders[0][position])
    second, extra = scatter(parts[1], orders[1][position], extra)
    return [first, second], extra


def gather_dp(parts, position):
    return [gather(part, order[position]) for part, order in zip(parts, dp_orders())]


def double(value, dim, extra=None):
    if extra is None:
        return value + swap(value, *dim), None
    rows = value.shape[0]
    both = jnp.concatenate([value, extra], 0)
    both = both + swap(both, *dim)
    return both[:rows], both[rows:]


def assemble_kernel(*refs):
    count = (len(refs) - 1) // 3
    mine, other, whole, sems = refs[:count], refs[count : 2 * count], refs[2 * count : -1], refs[-1]
    copies = Copies(sems)
    core = lax.rem(lax.axis_index("seq"), 2)
    for a, b, c in zip(mine, other, whole):
        rows = a.shape[0]
        first = pl.multiple_of(core * rows, rows)
        copies.start(a, c.at[pl.ds(first, rows)])
        copies.start(b, c.at[pl.ds(pl.multiple_of(rows - first, rows), rows)])
    for copy in copies.all:
        copy.wait()


def on_device(
    block_in, cotangent, bucket_id, assignment, norm_gain, b_proj, gamma_log, nu_log, theta_log,
    c_proj, d_skip, glu_weight,
):
    _, lanes, seg, width = block_in.shape
    n = nu_log.shape[0]
    two = 2 * n
    tokens = lanes * seg
    span = seg // CHUNKS
    short = seg * lax.axis_size("seq") // bucket_id.shape[2]
    gain, gamma, nu, theta, skip = (
        v.reshape(1, -1) for v in (norm_gain, gamma_log, nu_log, theta_log, d_skip)
    )
    hbm, vmem = pl.BlockSpec(memory_space=pltpu.HBM), pl.BlockSpec(memory_space=pltpu.VMEM)

    def call(kernel, name, micros, outs, far, near, fetched=None, scratch=(), sems=0, far_outs=0, limit=4, pin=False):
        fetched = far if fetched is None else fetched
        far = [pltpu.with_memory_space_constraint(v, pltpu.HBM) for v in far]
        if pin:
            near = [pltpu.with_memory_space_constraint(v, pltpu.VMEM) for v in near]
        shapes = [
            pltpu.HBM(shape, kind) if k < far_outs else jax.ShapeDtypeStruct(shape, kind)
            for k, (shape, kind) in enumerate(outs)
        ]
        room = [(pltpu.SMEM if v.dtype == jnp.int32 else pltpu.VMEM)(v.shape, v.dtype) for v in fetched]
        return pl.pallas_call(
            kernel,
            in_specs=[hbm] * len(far) + [vmem] * len(near),
            out_specs=[hbm] * far_outs + [vmem] * (len(outs) - far_outs),
            out_shape=shapes,
            scratch_shapes=room
            + [pltpu.VMEM(shape, kind) for shape, kind in scratch]
            + [pltpu.SemaphoreType.DMA((sems,))],
            compiler_params=pltpu.CompilerParams(vmem_limit_bytes=limit * 1024 * 1024),
            cost_estimate=cost(micros),
            name=name,
        )(*far, *near)

    low_rows, full_rows = ((tokens, width), BF16), ((tokens, two), F32)
    lane_rows = ((lanes, seg, width), BF16)
    xs, normed, loc, pair, powers, keep = call(
        functools.partial(first_kernel, short), "forward_local", 4,
        [
            low_rows, low_rows, full_rows, ((2 * lanes, two), F32), ((span, two), F32),
            ((lanes * CHUNKS, two), F32),
        ],
        [bucket_id[0], assignment, block_in[0], gain, b_proj, gamma, nu, theta], [],
        scratch=[low_rows, low_rows, full_rows], sems=4 * lanes + 7, far_outs=3, limit=12,
    )
    enter, _ = entering(pair, False)

    block_out, cts, h, carry, states, slope, pre, w_keep, w_send = call(
        block_kernel, "block", 7,
        [
            lane_rows, low_rows, full_rows, ((lanes * CHUNKS, two), F32), low_rows, full_rows,
            ((tokens, 2 * width), BF16), ((n, 2 * width), F32), ((n, 2 * width), F32),
        ],
        [cotangent[0], c_proj, skip, glu_weight, xs, normed, loc], [enter, powers, keep],
        scratch=[lane_rows, low_rows, low_rows], sems=7 * lanes + 3, far_outs=3, limit=20,
    )
    grad_mixed, adj, back_total, grad_d, c_keep, c_send = call(
        adjoint_kernel, "adjoint_local", 4,
        [
            full_rows, full_rows, ((lanes, two), F32), ((1, width), F32), ((n, width), F32),
            ((n, width), F32),
        ],
        [glu_weight, c_proj, normed], [pre, slope, states, powers, keep],
        scratch=[full_rows, full_rows, low_rows], sems=3 * lanes + 2, far_outs=2, limit=16,
    )

    decay = pair[lanes:]
    back_pair = jnp.concatenate(
        [back_total, jnp.concatenate([decay[:, :n], -decay[:, n:]], 1)], 0
    )
    w = w_keep + swap(w_send, "seq", 0)
    c = c_keep + swap(c_send, "seq", 0)
    wc = jnp.concatenate([w, c], 1)
    leave, wc = entering(back_pair, True, wc)
    half = wc.shape[1] // 2
    wc, _ = scatter_dp([wc[:, :half], wc[:, half:]], 0)

    back_low, b_keep, b_send, small = call(
        states_kernel, "adjoint_states", 3,
        [low_rows, ((n, two), F32), ((n, two), F32), ((8, two), F32)],
        [b_proj, gamma, skip, normed, h, adj], [leave, carry, powers, keep, grad_d],
        scratch=[low_rows, ((CHUNKS, two), F32)], sems=3 * lanes + 4, far_outs=1, limit=12,
    )

    b_send, *wc = tie(b_send, *wc)
    b = b_keep + swap(b_send, "seq", 0)
    small = small + swap(small, "seq", 0)
    b = [b[:, :n], b[:, n:]]
    small = small.reshape(-1, n)
    more = bits("seq", 1)
    steps = len(bits("dp"))
    for position in range(1, steps):
        wc, _ = scatter_dp(wc, position)
    for position in range(steps):
        b, small = scatter_dp(b, position, small)
    wc, b = jnp.concatenate(wc, 1), jnp.concatenate(b, 1)
    small = small.reshape(-1, two)
    for dim in more[:-1]:
        wc, _ = scatter(wc, dim)
        b, small = scatter(b, dim, small)
    wc, _ = double(wc, more[-1])
    b, small = double(b, more[-1], small)

    (grad_in,) = call(
        input_kernel, "back_input", 4, [lane_rows],
        [gain, b_proj, skip, xs, cts, back_low, grad_mixed], [],
        scratch=[lane_rows], sems=5 * lanes + 3, far_outs=1, limit=12,
    )
    finished = call(
        finish_kernel, "finish", 1, [((1, v), F32) for v in (width, n, n, n, width)],
        [nu, theta, gain], [small.reshape(8, two), powers], sems=3,
    )
    wc, b, grad_in, *finished = tie(wc, b, grad_in, *finished)
    grad_gain, grad_gamma, grad_nu, grad_theta, grad_d = finished

    for dim in more[:-1][::-1]:
        wc, b = gather(wc, dim), gather(b, dim)
    half = wc.shape[1] // 2
    wc, b = [wc[:, :half], wc[:, half:]], [b[:, :n], b[:, n:]]
    for position in reversed(range(steps)):
        wc, b = gather_dp(wc, position), gather_dp(b, position)
    wc, b = jnp.concatenate(wc, 1), jnp.concatenate(b, 1)
    mine = [wc[:, : 2 * width], wc[:, 2 * width :], b]
    other = [swap(v, "seq", 0) for v in mine]
    grad_w, grad_c, grad_b = call(
        assemble_kernel, "assemble", 2, [((2 * v.shape[0], v.shape[1]), F32) for v in mine],
        [], mine + other, sems=6, far_outs=3, pin=True,
    )
    return (
        block_out[None], grad_in[None], grad_gain[0], grad_b, grad_gamma[0], grad_nu[0], grad_theta[0],
        grad_c, grad_d[0], grad_w,
    )


def solution(mesh):
    rows = P("dp", None, "seq", None)
    in_specs = (rows, rows, P("dp", None, None), P("dp", None)) + (P(),) * 8
    out_specs = (rows, rows) + (P(),) * 8
    return jax.shard_map(
        on_device, mesh=mesh, in_specs=in_specs, out_specs=out_specs, check_vma=False
    )
```

profile of v0, /device:TPU:0, one launch (start us, length us, event | category | flops | bytes accessed | tf_op | source)
XLA Modules:
  0.0 123.5 jit_solution(8341365950864791336)
XLA Ops:
  0.7 5.6 %forward_local.1 = (bf16[1024,512]{1,0:T(8,128)(2,1)}, bf16[1024,512]{1,0:T(8,128)(2,1)}, f32[1024,512]{1,0:T(8,128)}, f32[8,512]{1,0:T(8,128)S(1)}, f32[32,512]{1,0:T(8,128)S(1)}, /*index=5*/f32[32,512]{1,0:T(8,128)S(1)}) custom-call(s32[4,16]{1,0:T(4,128)} %bitcast.17, s32[1,4]{1,0:T(1,128)} %assign_hbm.1, bf16[4,256,512]{2,1,0:T(8,128)(2,1)} %bitcast.15, ...), custom_call_target="tpu_custom_call" | custom-call | flops 4400000000 | bytes 12000000 | tf_op jit(solution)/shard_map/forward_local/pallas_call | solution.py:546
  6.8 0.8 collective-permute-done
  7.7 3.0 %collective-permute-start.1 = (f32[8,512]{1,0:T(8,128)S(1)}, f32[8,512]{1,0:T(8,128)S(1)}, u32[]{:S(2)}, u32[]{:S(2)}) collective-permute-start(f32[8,512]{1,0:T(8,128)S(1)} %maximum_maximum_fusion), channel_id=1, source_target_pairs={{0,2},{1,3},{2,0},{3,1},{4,6},{5,7},{6,4},{7,5},{8,10},{9,11},{10,... | collective-permute-start | bytes 49160 | tf_op jit(solution)/shard_map/ppermute | solution.py:415
  10.7 1.7 %collective-permute-done.1 = f32[8,512]{1,0:T(8,128)S(1)} collective-permute-done((f32[8,512]{1,0:T(8,128)S(1)}, f32[8,512]{1,0:T(8,128)S(1)}, u32[]{:S(2)}, u32[]{:S(2)}) %collective-permute-start.1) | collective-permute-done | bytes 16416 | tf_op jit(solution)/shard_map/ppermute | solution.py:415
  12.5 3.1 %collective-permute-start.2 = (f32[8,512]{1,0:T(8,128)S(1)}, f32[8,512]{1,0:T(8,128)S(1)}, u32[]{:S(2)}, u32[]{:S(2)}) collective-permute-start(f32[8,512]{1,0:T(8,128)S(1)} %maximum_maximum_fusion.1), channel_id=1, source_target_pairs={{0,4},{1,5},{2,6},{3,7},{4,0},{5,1},{6,2},{7,3},{8,12},{9,13},{10,... | collective-permute-start | bytes 49160 | tf_op jit(solution)/shard_map/ppermute | solution.py:415
  15.6 1.7 %collective-permute-done.2 = f32[8,512]{1,0:T(8,128)S(1)} collective-permute-done((f32[8,512]{1,0:T(8,128)S(1)}, f32[8,512]{1,0:T(8,128)S(1)}, u32[]{:S(2)}, u32[]{:S(2)}) %collective-permute-start.2) | collective-permute-done | bytes 16416 | tf_op jit(solution)/shard_map/ppermute | solution.py:415
  17.3 9.2 %block.1 = (bf16[4,256,512]{2,1,0:T(8,128)(2,1)}, bf16[1024,512]{1,0:T(8,128)(2,1)}, f32[1024,512]{1,0:T(8,128)}, f32[32,512]{1,0:T(8,128)S(1)}, bf16[1024,512]{...) custom-call(bf16[4,256,512]{2,1,0:T(8,128)(2,1)} %bitcast.16, ...), custom_call_target="tpu_custom_call" | custom-call | flops 7699999744 | bytes 21000000 | tf_op jit(solution)/shard_map/block/pallas_call | solution.py:546
  26.6 5.5 %adjoint_local.1 = (f32[1024,512]{1,0:T(8,128)}, f32[1024,512]{1,0:T(8,128)}, f32[4,512]{1,0:T(4,128)S(1)}, f32[1,512]{1,0:T(1,128)S(1)}, f32[256,512]{1,0:T(8,128)S(1)}, /*index=5*/f32[256,512]{1,0:T(8,128)S(1)}) custom-call(bf16[512,1024]{1,0:T(8,128)(2,1)} %w_hbm.3, bf16[512,512]{1,0:T(8,128)(2,1)} %c_hbm.3, ...), custom_call_target="tpu_custom_call" | custom-call | flops 4400000000 | bytes 12000000 | tf_op jit(solution)/shard_map/adjoint_local/pallas_call | solution.py:546
  32.8 0.7 collective-permute-done.3
  33.6 1.0 collective-permute-done.5
  34.9 1.4 %add.252 = f32[256,1024]{1,0:T(8,128)S(1)} add(f32[256,1024]{1,0:T(8,128)S(1)} %get-tuple-element.69, f32[256,1024]{1,0:T(8,128)} %collective-permute-done.4) | non-fusion elementwise | flops 262144 | bytes 3145728 | tf_op jit(solution)/shard_map/add | solution.py:595
  36.5 1.9 %collective-permute-start.9 = (f32[128,768]{1,0:T(8,128)S(1)}, f32[128,768]{1,0:T(8,128)S(1)}, u32[]{:S(2)}, u32[]{:S(2)}) collective-permute-start(f32[128,768]{1,0:T(8,128)S(1)} %constant_dynamic-slice_fusion.6), channel_id=1, source_target_pairs={{0,16},{8,24},{16,0},{24,8},{1,17},{9,25},{17,1},{25,9},{2,18},{10... | collective-permute-start | bytes 1179656 | tf_op jit(solution)/shard_map/ppermute | solution.py:415
  38.4 1.6 %collective-permute-start.6 = (f32[8,512]{1,0:T(8,128)S(1)}, f32[8,512]{1,0:T(8,128)S(1)}, u32[]{:S(2)}, u32[]{:S(2)}) collective-permute-start(f32[8,512]{1,0:T(8,128)S(1)} %maximum_maximum_fusion.3), channel_id=1, source_target_pairs={{0,2},{1,3},{2,0},{3,1},{4,6},{5,7},{6,4},{7,5},{8,10},{9,11},{10,... | collective-permute-start | bytes 49160 | tf_op jit(solution)/shard_map/ppermute | solution.py:415
  40.0 1.6 %collective-permute-start.8 = (f32[128,768]{1,0:T(8,128)S(1)}, f32[128,768]{1,0:T(8,128)S(1)}, u32[]{:S(2)}, u32[]{:S(2)}) collective-permute-start(f32[128,768]{1,0:T(8,128)S(1)} %constant_dynamic-slice_fusion.7), channel_id=1, source_target_pairs={{0,8},{8,0},{16,24},{24,16},{1,9},{9,1},{17,25},{25,17},{2,10},{10... | collective-permute-start | bytes 1179656 | tf_op jit(solution)/shard_map/ppermute | solution.py:415
  41.6 0.6 collective-permute-done.6
  42.2 2.6 %collective-permute-start.7 = (f32[8,512]{1,0:T(8,128)S(1)}, f32[8,512]{1,0:T(8,128)S(1)}, u32[]{:S(2)}, u32[]{:S(2)}) collective-permute-start(f32[8,512]{1,0:T(8,128)S(1)} %maximum_maximum_fusion.4), channel_id=1, source_target_pairs={{0,4},{1,5},{2,6},{3,7},{4,0},{5,1},{6,2},{7,3},{8,12},{9,13},{10,... | collective-permute-start | bytes 49160 | tf_op jit(solution)/shard_map/ppermute | solution.py:415
  44.9 2.0 %collective-permute-done.7 = f32[8,512]{1,0:T(8,128)S(1)} collective-permute-done((f32[8,512]{1,0:T(8,128)S(1)}, f32[8,512]{1,0:T(8,128)S(1)}, u32[]{:S(2)}, u32[]{:S(2)}) %collective-permute-start.7) | collective-permute-done | bytes 16416 | tf_op jit(solution)/shard_map/ppermute | solution.py:415
  46.9 4.6 %adjoint_states.1 = (bf16[1024,512]{1,0:T(8,128)(2,1)}, f32[256,512]{1,0:T(8,128)S(1)}, f32[256,512]{1,0:T(8,128)S(1)}, f32[8,512]{1,0:T(8,128)S(1)}) custom-call(bf16[512,512]{1,0:T(8,128)(2,1)} %b_hbm.5, f32[1,256]{1,0:T(1,128)} %bitcast.25, f32[1,512]{1,0:T(1,128)} %bitcast.19, bf16[1024,512]{1,0:T(8,128)(2,1)} %get-tuple-element.57.normed_hbm, ...), custom_call_target="tpu_custom_call" | custom-call | flops 3300000000 | bytes 9000000 | tf_op jit(solution)/shard_map/adjoint_states/pallas_call | solution.py:546
  51.7 1.6 %collective-permute-start.11 = (f32[64,768]{1,0:T(8,128)S(1)}, f32[64,768]{1,0:T(8,128)S(1)}, u32[]{:S(2)}, u32[]{:S(2)}) collective-permute-start(f32[64,768]{1,0:T(8,128)S(1)} %constant_dynamic-slice_fusion.4), channel_id=1, source_target_pairs={{0,8},{8,0},{16,24},{24,16},{1,9},{9,1},{17,25},{25,17},{2,10},{10... | collective-permute-start | bytes 589832 | tf_op jit(solution)/shard_map/ppermute | solution.py:415
  53.3 1.2 collective-permute-done.17
  55.3 2.2 %collective-permute-done.11 = f32[64,768]{1,0:T(8,128)S(1)} collective-permute-done((f32[64,768]{1,0:T(8,128)S(1)}, f32[64,768]{1,0:T(8,128)S(1)}, u32[]{:S(2)}, u32[]{:S(2)}) %collective-permute-start.11) | collective-permute-done | bytes 196640 | tf_op jit(solution)/shard_map/ppermute | solution.py:415
  57.5 4.5 %collective-permute-done.10 = f32[64,768]{1,0:T(8,128)S(1)} collective-permute-done((f32[64,768]{1,0:T(8,128)S(1)}, f32[64,768]{1,0:T(8,128)S(1)}, u32[]{:S(2)}, u32[]{:S(2)}) %collective-permute-start.10) | collective-permute-done | bytes 196640 | tf_op jit(solution)/shard_map/ppermute | solution.py:415
  62.0 1.6 %collective-permute-start.12 = (f32[32,1536]{1,0:T(8,128)S(1)}, f32[32,1536]{1,0:T(8,128)S(1)}, u32[]{:S(2)}, u32[]{:S(2)}) collective-permute-start(f32[32,1536]{1,0:T(8,128)S(1)} %fusion), channel_id=1, source_target_pairs={{0,2},{1,3},{2,0},{3,1},{4,6},{5,7},{6,4},{7,5},{8,10},{9,11},{10,... | collective-permute-start | bytes 589832 | tf_op jit(solution)/shard_map/ppermute | solution.py:415
  63.8 0.6 collective-permute-start.15
  65.0 3.8 %collective-permute-done.15 = f32[128,256]{1,0:T(8,128)S(1)} collective-permute-done((f32[128,256]{1,0:T(8,128)S(1)}, f32[128,256]{1,0:T(8,128)S(1)}, u32[]{:S(2)}, u32[]{:S(2)}) %collective-permute-start.15) | collective-permute-done | bytes 131104 | tf_op jit(solution)/shard_map/ppermute | solution.py:415
  69.7 2.2 %collective-permute-start.19 = (f32[80,256]{1,0:T(8,128)S(1)}, f32[80,256]{1,0:T(8,128)S(1)}, u32[]{:S(2)}, u32[]{:S(2)}) collective-permute-start(f32[80,256]{1,0:T(8,128)S(1)} %pad_maximum_fusion.4), channel_id=1, source_target_pairs={{0,8},{8,0},{16,24},{24,16},{1,9},{9,1},{17,25},{25,17},{2,10},{10... | collective-permute-start | bytes 245768 | tf_op jit(solution)/shard_map/ppermute | solution.py:415
  72.0 1.3 %collective-permute-done.16 = f32[64,256]{1,0:T(8,128)S(1)} collective-permute-done((f32[64,256]{1,0:T(8,128)S(1)}, f32[64,256]{1,0:T(8,128)S(1)}, u32[]{:S(2)}, u32[]{:S(2)}) %collective-permute-start.16) | collective-permute-done | bytes 65568 | tf_op jit(solution)/shard_map/ppermute | solution.py:415
  73.2 1.1 collective-permute-done.19
  75.0 2.7 %collective-permute-start.13 = (f32[32,1536]{1,0:T(8,128)S(1)}, f32[32,1536]{1,0:T(8,128)S(1)}, u32[]{:S(2)}, u32[]{:S(2)}) collective-permute-start(f32[32,1536]{1,0:T(8,128)S(1)} %fusion.2), channel_id=1, source_target_pairs={{0,4},{1,5},{2,6},{3,7},{4,0},{5,1},{6,2},{7,3},{8,12},{9,13},{10,... | collective-permute-start | bytes 589832 | tf_op jit(solution)/shard_map/ppermute | solution.py:415
  77.7 1.3 %collective-permute-done.20 = f32[40,512]{1,0:T(8,128)S(1)} collective-permute-done((f32[40,512]{1,0:T(8,128)S(1)}, f32[40,512]{1,0:T(8,128)S(1)}, u32[]{:S(2)}, u32[]{:S(2)}) %collective-permute-start.20) | collective-permute-done | bytes 81952 | tf_op jit(solution)/shard_map/ppermute | solution.py:415
  79.0 2.8 %collective-permute-start.21 = (f32[40,512]{1,0:T(8,128)S(1)}, f32[40,512]{1,0:T(8,128)S(1)}, u32[]{:S(2)}, u32[]{:S(2)}) collective-permute-start(f32[40,512]{1,0:T(8,128)S(1)} %pad_maximum_fusion.6), channel_id=1, source_target_pairs={{0,4},{1,5},{2,6},{3,7},{4,0},{5,1},{6,2},{7,3},{8,12},{9,13},{10,... | collective-permute-start | bytes 245768 | tf_op jit(solution)/shard_map/ppermute | solution.py:415
  81.8 5.2 %back_input.1 = bf16[4,256,512]{2,1,0:T(8,128)(2,1)} custom-call(f32[1,512]{1,0:T(1,128)} %bitcast.22, bf16[512,512]{1,0:T(8,128)(2,1)} %b_hbm.5, f32[1,512]{1,0:T(1,128)} %bitcast.20, bf16[1024,512]{1,0:T(8,128)(2,1)} %get-tuple-element.56.xs_hbm, bf16[1024,512]{1,0:T(8,128)(2,1)} %get-tuple-element.83.cts_hbm, ...), custom_call_target="tpu_custom_call" | custom-call | flops 4400000000 | bytes 12000000 | tf_op jit(solution)/shard_map/back_input/pallas_call | solution.py:546
  87.1 1.3 %finish.1 = (f32[1,512]{1,0:T(1,128)}, f32[1,256]{1,0:T(1,128)}, f32[1,256]{1,0:T(1,128)}, f32[1,256]{1,0:T(1,128)}, f32[1,512]{1,0:T(1,128)}) custom-call(f32[1,256]{1,0:T(1,128)} %bitcast.27, f32[1,256]{1,0:T(1,128)} %bitcast.29, f32[1,512]{1,0:T(1,128)} %bitcast.23, f32[8,512]{1,0:T(8,128)S(1)} %slice.414.small_ref, f32[32,512]{1,0:T(8,128)S(1)} %get-tuple-element.60.pow_ref), custom_call_target="tpu_custom_call" | custom-call | flops 1100000000 | bytes 3000000 | tf_op jit(solution)/shard_map/finish/pallas_call | solution.py:546
  88.5 1.5 %collective-permute-start.22 = (f32[32,1536]{1,0:T(8,128)S(1)}, f32[32,1536]{1,0:T(8,128)S(1)}, u32[]{:S(2)}, u32[]{:S(2)}) collective-permute-start(f32[32,1536]{1,0:T(8,128)S(1)} %add.282), channel_id=1, source_target_pairs={{0,2},{1,3},{2,0},{3,1},{4,6},{5,7},{6,4},{7,5},{8,10},{9,11},{10,... | collective-permute-start | bytes 589832 | tf_op jit(solution)/shard_map/ppermute | solution.py:415
  89.9 4.3 %collective-permute-done.22 = f32[32,1536]{1,0:T(8,128)S(1)} collective-permute-done((f32[32,1536]{1,0:T(8,128)S(1)}, f32[32,1536]{1,0:T(8,128)S(1)}, u32[]{:S(2)}, u32[]{:S(2)}) %collective-permute-start.22) | collective-permute-done | bytes 196640 | tf_op jit(solution)/shard_map/ppermute | solution.py:415
  94.3 1.4 %collective-permute-start.23 = (f32[64,768]{1,0:T(8,128)S(1)}, f32[64,768]{1,0:T(8,128)S(1)}, u32[]{:S(2)}, u32[]{:S(2)}) collective-permute-start(f32[64,768]{1,0:T(8,128)S(1)} %get-tuple-element.106), channel_id=1, source_target_pairs={{0,16},{8,24},{16,0},{24,8},{1,17},{9,25},{17,1},{25,9},{2,18},{10... | collective-permute-start | bytes 589832 | tf_op jit(solution)/shard_map/ppermute | solution.py:415
  95.7 1.1 collective-permute-start.25
  96.7 1.5 %collective-permute-start.27 = (f32[32,512]{1,0:T(8,128)S(1)}, f32[32,512]{1,0:T(8,128)S(1)}, u32[]{:S(2)}, u32[]{:S(2)}) collective-permute-start(f32[32,512]{1,0:T(8,128)S(1)} %slice.413), channel_id=1, source_target_pairs={{0,2},{1,3},{2,0},{3,1},{4,6},{5,7},{6,4},{7,5},{8,10},{9,11},{10,... | collective-permute-start | bytes 196616 | tf_op jit(solution)/shard_map/ppermute | solution.py:415
  98.2 2.1 %collective-permute-done.23 = f32[64,768]{1,0:T(8,128)S(1)} collective-permute-done((f32[64,768]{1,0:T(8,128)S(1)}, f32[64,768]{1,0:T(8,128)S(1)}, u32[]{:S(2)}, u32[]{:S(2)}) %collective-permute-start.23) | collective-permute-done | bytes 196640 | tf_op jit(solution)/shard_map/ppermute | solution.py:415
  100.4 3.7 %collective-permute-start.24 = (f32[128,768]{1,0:T(8,128)S(1)}, f32[128,768]{1,0:T(8,128)S(1)}, u32[]{:S(2)}, u32[]{:S(2)}) collective-permute-start(f32[128,768]{1,0:T(8,128)S(1)} %maximum_select_fusion.3), channel_id=1, source_target_pairs={{0,8},{8,0},{16,24},{24,16},{1,9},{9,1},{17,25},{25,17},{2,10},{10... | collective-permute-start | bytes 1179656 | tf_op jit(solution)/shard_map/ppermute | solution.py:415
  104.3 2.0 %collective-permute-start.28 = (f32[64,256]{1,0:T(8,128)S(1)}, f32[64,256]{1,0:T(8,128)S(1)}, u32[]{:S(2)}, u32[]{:S(2)}) collective-permute-start(f32[64,256]{1,0:T(8,128)S(1)} %get-tuple-element.108), channel_id=1, source_target_pairs={{0,16},{8,24},{16,0},{24,8},{1,17},{9,25},{17,1},{25,9},{2,18},{10... | collective-permute-start | bytes 196616 | tf_op jit(solution)/shard_map/ppermute | solution.py:415
  106.7 3.1 %collective-permute-done.24 = f32[128,768]{1,0:T(8,128)S(1)} collective-permute-done((f32[128,768]{1,0:T(8,128)S(1)}, f32[128,768]{1,0:T(8,128)S(1)}, u32[]{:S(2)}, u32[]{:S(2)}) %collective-permute-start.24) | collective-permute-done | bytes 393248 | tf_op jit(solution)/shard_map/ppermute | solution.py:415
  109.9 2.1 %collective-permute-done.26 = f32[128,768]{1,0:T(8,128)S(1)} collective-permute-done((f32[128,768]{1,0:T(8,128)S(1)}, f32[128,768]{1,0:T(8,128)S(1)}, u32[]{:S(2)}, u32[]{:S(2)}) %collective-permute-start.26) | collective-permute-done | bytes 393248 | tf_op jit(solution)/shard_map/ppermute | solution.py:415
  113.2 1.7 %collective-permute-start.31 = (f32[128,256]{1,0:T(8,128)S(1)}, f32[128,256]{1,0:T(8,128)S(1)}, u32[]{:S(2)}, u32[]{:S(2)}) collective-permute-start(f32[128,256]{1,0:T(8,128)S(1)} %maximum_select_fusion.9), channel_id=1, source_target_pairs={{0,16},{8,24},{16,0},{24,8},{1,17},{9,25},{17,1},{25,9},{2,18},{10... | collective-permute-start | bytes 393224 | tf_op jit(solution)/shard_map/ppermute | solution.py:415
  114.9 3.3 %collective-permute-done.29 = f32[128,256]{1,0:T(8,128)S(1)} collective-permute-done((f32[128,256]{1,0:T(8,128)S(1)}, f32[128,256]{1,0:T(8,128)S(1)}, u32[]{:S(2)}, u32[]{:S(2)}) %collective-permute-start.29) | collective-permute-done | bytes 131104 | tf_op jit(solution)/shard_map/ppermute | solution.py:415
  119.2 1.3 %collective-permute-done.34.refs_5_ = f32[256,512]{1,0:T(8,128)S(1)} collective-permute-done((f32[256,512]{1,0:T(8,128)S(1)}, f32[256,512]{1,0:T(8,128)S(1)}, u32[]{:S(2)}, u32[]{:S(2)}) %collective-permute-start.34) | collective-permute-done | bytes 524320 | tf_op jit(solution)/shard_map/ppermute | solution.py:415
  120.5 0.7 collective-permute-done.33.refs_4_
  121.3 2.1 %assemble.1 = (f32[512,1024]{1,0:T(8,128)}, f32[512,512]{1,0:T(8,128)}, f32[512,512]{1,0:T(8,128)}) custom-call(f32[256,1024]{1,0:T(8,128)S(1)} %pad_maximum_fusion.1.refs_0_, f32[256,512]{1,0:T(8,128)S(1)} %slice.417.refs_1_, f32[256,512]{1,0:T(8,128)S(1)} %pad_maximum_fusion.2.refs_2_, f32[256,1024]{1,0:T(8,128)S(1)} %collective-permute-done.32.refs_3_, ...), custom_call_target="tpu_custom_call" | custom-call | flops 2200000000 | bytes 6000000 | tf_op jit(solution)/shard_map/assemble/pallas_call | solution.py:546
  (109 shorter events, 8.2 us)
Async XLA Ops:
  0.6 7.0 %copy-start = (f32[4,512]{1,0:T(4,128)S(1)}, f32[4,512]{1,0:T(4,128)}, u32[]{:S(2)}) copy-start(f32[4,512]{1,0:T(4,128)} %constant.152.clone.1) | copy-start | bytes 24580
  6.3 1.4 %collective-permute-start = (f32[8,512]{1,0:T(8,128)S(1)}, f32[8,512]{1,0:T(8,128)S(1)}, u32[]{:S(2)}, u32[]{:S(2)}) collective-permute-start(f32[8,512]{1,0:T(8,128)S(1)} %get-tuple-element.59), channel_id=1, source_target_pairs={{0,1},{1,0},{2,3},{3,2},{4,5},{5,4},{6,7},{7,6},{8,9},{9,8},{10,11... | collective-permute-start | bytes 49160 | tf_op jit(solution)/shard_map/ppermute | solution.py:415
  7.7 4.7 %collective-permute-start.1 = (f32[8,512]{1,0:T(8,128)S(1)}, f32[8,512]{1,0:T(8,128)S(1)}, u32[]{:S(2)}, u32[]{:S(2)}) collective-permute-start(f32[8,512]{1,0:T(8,128)S(1)} %maximum_maximum_fusion), channel_id=1, source_target_pairs={{0,2},{1,3},{2,0},{3,1},{4,6},{5,7},{6,4},{7,5},{8,10},{9,11},{10,... | collective-permute-start | bytes 49160 | tf_op jit(solution)/shard_map/ppermute | solution.py:415
  12.5 4.8 %collective-permute-start.2 = (f32[8,512]{1,0:T(8,128)S(1)}, f32[8,512]{1,0:T(8,128)S(1)}, u32[]{:S(2)}, u32[]{:S(2)}) collective-permute-start(f32[8,512]{1,0:T(8,128)S(1)} %maximum_maximum_fusion.1), channel_id=1, source_target_pairs={{0,4},{1,5},{2,6},{3,7},{4,0},{5,1},{6,2},{7,3},{8,12},{9,13},{10,... | collective-permute-start | bytes 49160 | tf_op jit(solution)/shard_map/ppermute | solution.py:415
  26.5 8.2 %collective-permute-start.4 = (f32[256,1024]{1,0:T(8,128)S(1)}, f32[256,1024]{1,0:T(8,128)}, u32[]{:S(2)}, u32[]{:S(2)}) collective-permute-start(f32[256,1024]{1,0:T(8,128)S(1)} %get-tuple-element.70), channel_id=1, source_target_pairs={{0,1},{1,0},{2,3},{3,2},{4,5},{5,4},{6,7},{7,6},{8,9},{9,8},{10,11... | collective-permute-start | bytes 3145736 | tf_op jit(solution)/shard_map/ppermute | solution.py:415
  32.1 1.4 %collective-permute-start.3 = (f32[8,512]{1,0:T(8,128)S(1)}, f32[8,512]{1,0:T(8,128)S(1)}, u32[]{:S(2)}, u32[]{:S(2)}) collective-permute-start(f32[8,512]{1,0:T(8,128)S(1)} %maximum_maximum_fusion.2), channel_id=1, source_target_pairs={{0,1},{1,0},{2,3},{3,2},{4,5},{5,4},{6,7},{7,6},{8,9},{9,8},{10,11... | collective-permute-start | bytes 49160 | tf_op jit(solution)/shard_map/ppermute | solution.py:415
  32.7 1.9 %collective-permute-start.5 = (f32[256,512]{1,0:T(8,128)S(1)}, f32[256,512]{1,0:T(8,128)S(1)}, u32[]{:S(2)}, u32[]{:S(2)}) collective-permute-start(f32[256,512]{1,0:T(8,128)S(1)} %get-tuple-element.72), channel_id=1, source_target_pairs={{0,1},{1,0},{2,3},{3,2},{4,5},{5,4},{6,7},{7,6},{8,9},{9,8},{10,11... | collective-permute-start | bytes 1572872 | tf_op jit(solution)/shard_map/ppermute | solution.py:415
  36.5 15.1 %collective-permute-start.9 = (f32[128,768]{1,0:T(8,128)S(1)}, f32[128,768]{1,0:T(8,128)S(1)}, u32[]{:S(2)}, u32[]{:S(2)}) collective-permute-start(f32[128,768]{1,0:T(8,128)S(1)} %constant_dynamic-slice_fusion.6), channel_id=1, source_target_pairs={{0,16},{8,24},{16,0},{24,8},{1,17},{9,25},{17,1},{25,9},{2,18},{10... | collective-permute-start | bytes 1179656 | tf_op jit(solution)/shard_map/ppermute | solution.py:415
  38.4 3.7 %collective-permute-start.6 = (f32[8,512]{1,0:T(8,128)S(1)}, f32[8,512]{1,0:T(8,128)S(1)}, u32[]{:S(2)}, u32[]{:S(2)}) collective-permute-start(f32[8,512]{1,0:T(8,128)S(1)} %maximum_maximum_fusion.3), channel_id=1, source_target_pairs={{0,2},{1,3},{2,0},{3,1},{4,6},{5,7},{6,4},{7,5},{8,10},{9,11},{10,... | collective-permute-start | bytes 49160 | tf_op jit(solution)/shard_map/ppermute | solution.py:415
  40.0 11.6 %collective-permute-start.8 = (f32[128,768]{1,0:T(8,128)S(1)}, f32[128,768]{1,0:T(8,128)S(1)}, u32[]{:S(2)}, u32[]{:S(2)}) collective-permute-start(f32[128,768]{1,0:T(8,128)S(1)} %constant_dynamic-slice_fusion.7), channel_id=1, source_target_pairs={{0,8},{8,0},{16,24},{24,16},{1,9},{9,1},{17,25},{25,17},{2,10},{10... | collective-permute-start | bytes 1179656 | tf_op jit(solution)/shard_map/ppermute | solution.py:415
  42.2 4.7 %collective-permute-start.7 = (f32[8,512]{1,0:T(8,128)S(1)}, f32[8,512]{1,0:T(8,128)S(1)}, u32[]{:S(2)}, u32[]{:S(2)}) collective-permute-start(f32[8,512]{1,0:T(8,128)S(1)} %maximum_maximum_fusion.4), channel_id=1, source_target_pairs={{0,4},{1,5},{2,6},{3,7},{4,0},{5,1},{6,2},{7,3},{8,12},{9,13},{10,... | collective-permute-start | bytes 49160 | tf_op jit(solution)/shard_map/ppermute | solution.py:415
  51.7 5.7 %collective-permute-start.11 = (f32[64,768]{1,0:T(8,128)S(1)}, f32[64,768]{1,0:T(8,128)S(1)}, u32[]{:S(2)}, u32[]{:S(2)}) collective-permute-start(f32[64,768]{1,0:T(8,128)S(1)} %constant_dynamic-slice_fusion.4), channel_id=1, source_target_pairs={{0,8},{8,0},{16,24},{24,16},{1,9},{9,1},{17,25},{25,17},{2,10},{10... | collective-permute-start | bytes 589832 | tf_op jit(solution)/shard_map/ppermute | solution.py:415
  53.3 1.2 collective-permute-start.17
  54.5 9.2 %collective-permute-start.14 = (f32[256,512]{1,0:T(8,128)S(1)}, f32[256,512]{1,0:T(8,128)S(1)}, u32[]{:S(2)}, u32[]{:S(2)}) collective-permute-start(f32[256,512]{1,0:T(8,128)S(1)} %get-tuple-element.81), channel_id=1, source_target_pairs={{0,1},{1,0},{2,3},{3,2},{4,5},{5,4},{6,7},{7,6},{8,9},{9,8},{10,11... | collective-permute-start | bytes 1572872 | tf_op jit(solution)/shard_map/ppermute | solution.py:415
  54.7 7.2 %collective-permute-start.10 = (f32[64,768]{1,0:T(8,128)S(1)}, f32[64,768]{1,0:T(8,128)S(1)}, u32[]{:S(2)}, u32[]{:S(2)}) collective-permute-start(f32[64,768]{1,0:T(8,128)S(1)} %constant_dynamic-slice_fusion.5), channel_id=1, source_target_pairs={{0,16},{8,24},{16,0},{24,8},{1,17},{9,25},{17,1},{25,9},{2,18},{10... | collective-permute-start | bytes 589832 | tf_op jit(solution)/shard_map/ppermute | solution.py:415
  62.0 12.9 %collective-permute-start.12 = (f32[32,1536]{1,0:T(8,128)S(1)}, f32[32,1536]{1,0:T(8,128)S(1)}, u32[]{:S(2)}, u32[]{:S(2)}) collective-permute-start(f32[32,1536]{1,0:T(8,128)S(1)} %fusion), channel_id=1, source_target_pairs={{0,2},{1,3},{2,0},{3,1},{4,6},{5,7},{6,4},{7,5},{8,10},{9,11},{10,... | collective-permute-start | bytes 589832 | tf_op jit(solution)/shard_map/ppermute | solution.py:415
  63.8 5.0 %collective-permute-start.15 = (f32[128,256]{1,0:T(8,128)S(1)}, f32[128,256]{1,0:T(8,128)S(1)}, u32[]{:S(2)}, u32[]{:S(2)}) collective-permute-start(f32[128,256]{1,0:T(8,128)S(1)} %constant_dynamic-slice_fusion.3), channel_id=1, source_target_pairs={{0,8},{8,0},{16,24},{24,16},{1,9},{9,1},{17,25},{25,17},{2,10},{10... | collective-permute-start | bytes 393224 | tf_op jit(solution)/shard_map/ppermute | solution.py:415
  64.4 5.2 %collective-permute-start.18 = (f32[144,256]{1,0:T(8,128)S(1)}, f32[144,256]{1,0:T(8,128)S(1)}, u32[]{:S(2)}, u32[]{:S(2)}) collective-permute-start(f32[144,256]{1,0:T(8,128)S(1)} %pad_maximum_fusion.3), channel_id=1, source_target_pairs={{0,16},{8,24},{16,0},{24,8},{1,17},{9,25},{17,1},{25,9},{2,18},{10... | collective-permute-start | bytes 442376 | tf_op jit(solution)/shard_map/ppermute | solution.py:415
  68.9 4.3 %collective-permute-start.16 = (f32[64,256]{1,0:T(8,128)S(1)}, f32[64,256]{1,0:T(8,128)S(1)}, u32[]{:S(2)}, u32[]{:S(2)}) collective-permute-start(f32[64,256]{1,0:T(8,128)S(1)} %constant_dynamic-slice_fusion.2), channel_id=1, source_target_pairs={{0,16},{8,24},{16,0},{24,8},{1,17},{9,25},{17,1},{25,9},{2,18},{10... | collective-permute-start | bytes 196616 | tf_op jit(solution)/shard_map/ppermute | solution.py:415
  69.7 4.6 %collective-permute-start.19 = (f32[80,256]{1,0:T(8,128)S(1)}, f32[80,256]{1,0:T(8,128)S(1)}, u32[]{:S(2)}, u32[]{:S(2)}) collective-permute-start(f32[80,256]{1,0:T(8,128)S(1)} %pad_maximum_fusion.4), channel_id=1, source_target_pairs={{0,8},{8,0},{16,24},{24,16},{1,9},{9,1},{17,25},{25,17},{2,10},{10... | collective-permute-start | bytes 245768 | tf_op jit(solution)/shard_map/ppermute | solution.py:415
  74.4 4.5 %collective-permute-start.20 = (f32[40,512]{1,0:T(8,128)S(1)}, f32[40,512]{1,0:T(8,128)S(1)}, u32[]{:S(2)}, u32[]{:S(2)}) collective-permute-start(f32[40,512]{1,0:T(8,128)S(1)} %pad_maximum_fusion.5), channel_id=1, source_target_pairs={{0,2},{1,3},{2,0},{3,1},{4,6},{5,7},{6,4},{7,5},{8,10},{9,11},{10,... | collective-permute-start | bytes 245768 | tf_op jit(solution)/shard_map/ppermute | solution.py:415
  75.0 12.0 %collective-permute-start.13 = (f32[32,1536]{1,0:T(8,128)S(1)}, f32[32,1536]{1,0:T(8,128)S(1)}, u32[]{:S(2)}, u32[]{:S(2)}) collective-permute-start(f32[32,1536]{1,0:T(8,128)S(1)} %fusion.2), channel_id=1, source_target_pairs={{0,4},{1,5},{2,6},{3,7},{4,0},{5,1},{6,2},{7,3},{8,12},{9,13},{10,... | collective-permute-start | bytes 589832 | tf_op jit(solution)/shard_map/ppermute | solution.py:415
  79.0 8.1 %collective-permute-start.21 = (f32[40,512]{1,0:T(8,128)S(1)}, f32[40,512]{1,0:T(8,128)S(1)}, u32[]{:S(2)}, u32[]{:S(2)}) collective-permute-start(f32[40,512]{1,0:T(8,128)S(1)} %pad_maximum_fusion.6), channel_id=1, source_target_pairs={{0,4},{1,5},{2,6},{3,7},{4,0},{5,1},{6,2},{7,3},{8,12},{9,13},{10,... | collective-permute-start | bytes 245768 | tf_op jit(solution)/shard_map/ppermute | solution.py:415
  88.5 5.7 %collective-permute-start.22 = (f32[32,1536]{1,0:T(8,128)S(1)}, f32[32,1536]{1,0:T(8,128)S(1)}, u32[]{:S(2)}, u32[]{:S(2)}) collective-permute-start(f32[32,1536]{1,0:T(8,128)S(1)} %add.282), channel_id=1, source_target_pairs={{0,2},{1,3},{2,0},{3,1},{4,6},{5,7},{6,4},{7,5},{8,10},{9,11},{10,... | collective-permute-start | bytes 589832 | tf_op jit(solution)/shard_map/ppermute | solution.py:415
  94.3 6.1 %collective-permute-start.23 = (f32[64,768]{1,0:T(8,128)S(1)}, f32[64,768]{1,0:T(8,128)S(1)}, u32[]{:S(2)}, u32[]{:S(2)}) collective-permute-start(f32[64,768]{1,0:T(8,128)S(1)} %get-tuple-element.106), channel_id=1, source_target_pairs={{0,16},{8,24},{16,0},{24,8},{1,17},{9,25},{17,1},{25,9},{2,18},{10... | collective-permute-start | bytes 589832 | tf_op jit(solution)/shard_map/ppermute | solution.py:415
  95.7 8.4 %collective-permute-start.25 = (f32[64,768]{1,0:T(8,128)S(1)}, f32[64,768]{1,0:T(8,128)S(1)}, u32[]{:S(2)}, u32[]{:S(2)}) collective-permute-start(f32[64,768]{1,0:T(8,128)S(1)} %get-tuple-element.107), channel_id=1, source_target_pairs={{0,8},{8,0},{16,24},{24,16},{1,9},{9,1},{17,25},{25,17},{2,10},{10... | collective-permute-start | bytes 589832 | tf_op jit(solution)/shard_map/ppermute | solution.py:415
  96.7 7.5 %collective-permute-start.27 = (f32[32,512]{1,0:T(8,128)S(1)}, f32[32,512]{1,0:T(8,128)S(1)}, u32[]{:S(2)}, u32[]{:S(2)}) collective-permute-start(f32[32,512]{1,0:T(8,128)S(1)} %slice.413), channel_id=1, source_target_pairs={{0,2},{1,3},{2,0},{3,1},{4,6},{5,7},{6,4},{7,5},{8,10},{9,11},{10,... | collective-permute-start | bytes 196616 | tf_op jit(solution)/shard_map/ppermute | solution.py:415
  100.4 9.4 %collective-permute-start.24 = (f32[128,768]{1,0:T(8,128)S(1)}, f32[128,768]{1,0:T(8,128)S(1)}, u32[]{:S(2)}, u32[]{:S(2)}) collective-permute-start(f32[128,768]{1,0:T(8,128)S(1)} %maximum_select_fusion.3), channel_id=1, source_target_pairs={{0,8},{8,0},{16,24},{24,16},{1,9},{9,1},{17,25},{25,17},{2,10},{10... | collective-permute-start | bytes 1179656 | tf_op jit(solution)/shard_map/ppermute | solution.py:415
  104.1 7.8 %collective-permute-start.26 = (f32[128,768]{1,0:T(8,128)S(1)}, f32[128,768]{1,0:T(8,128)S(1)}, u32[]{:S(2)}, u32[]{:S(2)}) collective-permute-start(f32[128,768]{1,0:T(8,128)S(1)} %maximum_select_fusion.4), channel_id=1, source_target_pairs={{0,16},{8,24},{16,0},{24,8},{1,17},{9,25},{17,1},{25,9},{2,18},{10... | collective-permute-start | bytes 1179656 | tf_op jit(solution)/shard_map/ppermute | solution.py:415
  104.3 8.4 %collective-permute-start.28 = (f32[64,256]{1,0:T(8,128)S(1)}, f32[64,256]{1,0:T(8,128)S(1)}, u32[]{:S(2)}, u32[]{:S(2)}) collective-permute-start(f32[64,256]{1,0:T(8,128)S(1)} %get-tuple-element.108), channel_id=1, source_target_pairs={{0,16},{8,24},{16,0},{24,8},{1,17},{9,25},{17,1},{25,9},{2,18},{10... | collective-permute-start | bytes 196616 | tf_op jit(solution)/shard_map/ppermute | solution.py:415
  106.3 6.9 %collective-permute-start.30 = (f32[64,256]{1,0:T(8,128)S(1)}, f32[64,256]{1,0:T(8,128)S(1)}, u32[]{:S(2)}, u32[]{:S(2)}) collective-permute-start(f32[64,256]{1,0:T(8,128)S(1)} %get-tuple-element.109), channel_id=1, source_target_pairs={{0,8},{8,0},{16,24},{24,16},{1,9},{9,1},{17,25},{25,17},{2,10},{10... | collective-permute-start | bytes 196616 | tf_op jit(solution)/shard_map/ppermute | solution.py:415
  112.1 9.1 %collective-permute-start.32 = (f32[256,1024]{1,0:T(8,128)S(1)}, f32[256,1024]{1,0:T(8,128)S(1)}, u32[]{:S(2)}, u32[]{:S(2)}) collective-permute-start(f32[256,1024]{1,0:T(8,128)S(1)} %pad_maximum_fusion.1.refs_0_), channel_id=1, source_target_pairs={{0,1},{1,0},{2,3},{3,2},{4,5},{5,4},{6,7},{7,6},{8,9},{9,8},{10,11... | collective-permute-start | bytes 3145736 | tf_op jit(solution)/shard_map/ppermute | solution.py:415
  112.7 5.5 %collective-permute-start.29 = (f32[128,256]{1,0:T(8,128)S(1)}, f32[128,256]{1,0:T(8,128)S(1)}, u32[]{:S(2)}, u32[]{:S(2)}) collective-permute-start(f32[128,256]{1,0:T(8,128)S(1)} %maximum_select_fusion.8), channel_id=1, source_target_pairs={{0,8},{8,0},{16,24},{24,16},{1,9},{9,1},{17,25},{25,17},{2,10},{10... | collective-permute-start | bytes 393224 | tf_op jit(solution)/shard_map/ppermute | solution.py:415
  113.2 5.3 %collective-permute-start.31 = (f32[128,256]{1,0:T(8,128)S(1)}, f32[128,256]{1,0:T(8,128)S(1)}, u32[]{:S(2)}, u32[]{:S(2)}) collective-permute-start(f32[128,256]{1,0:T(8,128)S(1)} %maximum_select_fusion.9), channel_id=1, source_target_pairs={{0,16},{8,24},{16,0},{24,8},{1,17},{9,25},{17,1},{25,9},{2,18},{10... | collective-permute-start | bytes 393224 | tf_op jit(solution)/shard_map/ppermute | solution.py:415
  118.5 2.0 %collective-permute-start.34 = (f32[256,512]{1,0:T(8,128)S(1)}, f32[256,512]{1,0:T(8,128)S(1)}, u32[]{:S(2)}, u32[]{:S(2)}) collective-permute-start(f32[256,512]{1,0:T(8,128)S(1)} %pad_maximum_fusion.2.refs_2_), channel_id=1, source_target_pairs={{0,1},{1,0},{2,3},{3,2},{4,5},{5,4},{6,7},{7,6},{8,9},{9,8},{10,11... | collective-permute-start | bytes 1572872 | tf_op jit(solution)/shard_map/ppermute | solution.py:415
  118.7 2.6 %collective-permute-start.33 = (f32[256,512]{1,0:T(8,128)S(1)}, f32[256,512]{1,0:T(8,128)S(1)}, u32[]{:S(2)}, u32[]{:S(2)}) collective-permute-start(f32[256,512]{1,0:T(8,128)S(1)} %slice.417.refs_1_), channel_id=1, source_target_pairs={{0,1},{1,0},{2,3},{3,2},{4,5},{5,4},{6,7},{7,6},{8,9},{9,8},{10,11... | collective-permute-start | bytes 1572872 | tf_op jit(solution)/shard_map/ppermute | solution.py:415
where the time goes:
time: 124 us; the launch traced here: 123 us
  starting transfers between devices  43.7 us (35%)
  waiting for transfers between devices  41.6 us (34%)
  Pallas kernels  33.5 us (27%)
  other arithmetic  2.71 us (2%)
  between operations  1.55 us (1%)
    ppermute x35, starting transfers between devices, swap(): return lax.ppermute(value, axis, [(i, i ^ 1 << bit) for i in range(count)])  43.7 us
    ppermute x35, waiting for transfers between devices, swap(): return lax.ppermute(value, axis, [(i, i ^ 1 << bit) for i in range(count)])  41.6 us
    pallas_call x7, Pallas kernels, call(): pl.pallas_call(kernel, in_specs=[hbm] * len(far) + [vmem] * len(near), ou...  33.5 us
  transfers between devices with their start and end apart: 35, of which 25 were waited for; matrix products, arithmetic and copies ran while one was open for 1% of the time, Pallas kernels for 12%

commit v1 on v0

v1 whole, which is shorter than its diff:
```python
import functools

import jax
import jax.numpy as jnp
from jax import lax
from jax.experimental import pallas as pl
from jax.experimental.pallas import tpu as pltpu
from jax.sharding import PartitionSpec as P

EPS = 1e-05
CHUNKS = 8
LANE = 128
GELU_A = 0.044715
GELU_K = 0.7978845608028654
F32 = jnp.float32
BF16 = jnp.bfloat16


def dot_nt(left, right):
    return lax.dot_general(left, right, (((1,), (1,)), ((), ())), preferred_element_type=F32)


def dot_tn(left, right):
    return lax.dot_general(left, right, (((0,), (0,)), ((), ())), preferred_element_type=F32)


def dot_nn(left, right):
    return jnp.dot(left, right, preferred_element_type=F32)


def cmul(x, y):
    return x[0] * y[0] - x[1] * y[1], x[0] * y[1] + x[1] * y[0]


def cadd(x, y):
    return x[0] + y[0], x[1] + y[1]


def fma(a, x, y):
    return (y[0] - a[1] * x[1]) + a[0] * x[0], (y[1] + a[1] * x[0]) + a[0] * x[1]


def conj(x):
    return x[0], -x[1]


def cload(ref, first, count=1):
    n = ref.shape[-1] // 2
    return ref[first : first + count, :n], ref[first : first + count, n:]


def cstore(ref, first, value):
    n = ref.shape[-1] // 2
    rows = value[0].shape[0]
    ref[first : first + rows, :n], ref[first : first + rows, n:] = value


def kept(ref, row, value):
    keep = cload(ref, row)
    return value[0] * keep[0], value[1] * keep[1]


def scan_order(seg, back=False):
    row = lax.broadcasted_iota(jnp.int32, (seg, seg), 0)
    column = lax.broadcasted_iota(jnp.int32, (seg, seg), 1)
    if back:
        row, column = column, row
    span = seg // CHUNKS
    hit = (row % CHUNKS == column // span) & (row // CHUNKS == column % span)
    return jnp.where(hit, 1.0, 0.0).astype(BF16)


def fill_keeps(bucket, assign, keep_ref, lanes, seg, short):
    own = lax.axis_index("seq")
    for lane in range(lanes):
        pattern = assign[0, lane]
        for chunk in range(CHUNKS):
            token = own * seg + chunk * (seg // CHUNKS)
            here = bucket[pattern, lax.div(token, short)]
            span = jnp.where(here == 0, short, jnp.where(here == 1, 4 * short, 16 * short))
            keep = jnp.where(lax.rem(token, span) == 0, 0.0, 1.0).astype(F32)
            row = lane * CHUNKS + chunk
            keep_ref[row : row + 1, :] = jnp.full((1, keep_ref.shape[1]), keep)


def norm_stats(rows):
    mean = jnp.mean(rows, axis=-1, keepdims=True)
    centred = rows - mean
    var = jnp.mean(centred * centred, axis=-1, keepdims=True)
    scale = lax.rsqrt(var + EPS)
    return centred * scale, scale


def cost(micros):
    return pl.CostEstimate(flops=int(micros * 1.1e9), bytes_accessed=int(micros * 3e6), transcendentals=0)


def put_halves(value, keep, send):
    rows = value.shape[0] // 2
    first = lax.rem(lax.axis_index("seq"), 2) == 0
    top, bottom = value[:rows], value[rows:]
    keep[...] = jnp.where(first, top, bottom)
    send[...] = jnp.where(first, bottom, top)


class Copies:
    def __init__(self, sems):
        self.sems, self.all = sems, []

    def start(self, source, target):
        copy = pltpu.make_async_copy(source, target, self.sems.at[len(self.all)])
        copy.start()
        self.all.append(copy)
        return copy

    def lanes(self, lanes, *pairs):
        return [
            [self.start(lane_of(source, lane, lanes), lane_of(target, lane, lanes)) for source, target in pairs]
            for lane in range(lanes)
        ]


def lane_of(ref, lane, lanes):
    if len(ref.shape) == 3:
        return ref.at[lane]
    rows = ref.shape[0] // lanes
    return ref.at[pl.ds(lane * rows, rows)]


def wait(copies):
    for copy in copies:
        copy.wait()


def first_kernel(
    short, bucket_hbm, assign_hbm, x_hbm, gain_hbm, b_hbm, gamma_hbm, nu_hbm, th_hbm,
    xs_hbm, normed_hbm, loc_hbm, pair_ref, pow_ref, keep_ref,
    bucket, assign, x_ref, gain_ref, b_ref, gamma_ref, nu_ref, th_ref, xs_ref, normed_ref, loc_ref, sems,
):
    lanes, seg, width = x_ref.shape
    span = seg // CHUNKS
    copies = Copies(sems)
    x_here = copies.lanes(lanes, (x_hbm, x_ref))
    nu_here, th_here = copies.start(nu_hbm, nu_ref), copies.start(th_hbm, th_ref)
    gain_here, gamma_here = copies.start(gain_hbm, gain_ref), copies.start(gamma_hbm, gamma_ref)
    b_here = copies.start(b_hbm, b_ref)
    tables = copies.start(bucket_hbm, bucket), copies.start(assign_hbm, assign)
    leaving = []

    order = scan_order(seg)
    nu_here.wait(), th_here.wait()
    modulus = jnp.exp(-jnp.exp(nu_ref[...]))
    phase = jnp.exp(th_ref[...])
    cstore(pow_ref, 0, (modulus * jnp.cos(phase), modulus * jnp.sin(phase)))
    size = 1
    while size < span:
        cstore(pow_ref, size, cmul(cload(pow_ref, 0, size), cload(pow_ref, size - 1)))
        size *= 2

    gain_here.wait(), gamma_here.wait()
    lam = cload(pow_ref, 0)
    lam_span = cload(pow_ref, span - 1)
    ends = []
    factor = jnp.exp(gamma_ref[...])
    factor = jnp.concatenate([factor, factor], 1)
    for lane in range(lanes):
        rows = pl.ds(lane * seg, seg)
        wait(x_here[lane])
        x = dot_nn(order, x_ref[lane])
        xs_ref[rows, :] = x.astype(BF16)
        xhat, _ = norm_stats(x)
        low = (xhat * gain_ref[...]).astype(BF16)
        normed_ref[rows, :] = low
        if lane == 0:
            b_here.wait()
        loc_ref[rows, :] = dot_nn(low, b_ref[...]) * factor
        for source, target in ((xs_ref, xs_hbm), (normed_ref, normed_hbm)):
            leaving.append(copies.start(source.at[rows], target.at[rows]))
        h = cload(loc_ref, lane * seg, CHUNKS)
        for step in range(1, span):
            at = lane * seg + step * CHUNKS
            h = fma(lam, h, cload(loc_ref, at, CHUNKS))
            cstore(loc_ref, at, h)
        leaving.append(copies.start(loc_ref.at[rows], loc_hbm.at[rows]))
        ends.append(h)

    wait(tables)
    fill_keeps(bucket, assign, keep_ref, lanes, seg, short)
    for lane, h in enumerate(ends):
        state = h[0][0:1], h[1][0:1]
        decay = kept(keep_ref, lane * CHUNKS, lam_span)
        for chunk in range(1, CHUNKS):
            step = kept(keep_ref, lane * CHUNKS + chunk, lam_span)
            state = fma(step, state, (h[0][chunk : chunk + 1], h[1][chunk : chunk + 1]))
            decay = cmul(step, decay)
        cstore(pair_ref, lane, state)
        cstore(pair_ref, lanes + lane, decay)
    wait(leaving)


def order_kernel(ct_hbm, cts_hbm, ct_ref, cts_ref, sems):
    lanes, seg, _ = ct_ref.shape
    copies = Copies(sems)
    here = copies.lanes(lanes, (ct_hbm, ct_ref))
    order = scan_order(seg)
    leaving = []
    for lane in range(lanes):
        rows = pl.ds(lane * seg, seg)
        wait(here[lane])
        cts_ref[rows, :] = dot_nn(order, ct_ref[lane]).astype(BF16)
        leaving.append(copies.start(cts_ref.at[rows], cts_hbm.at[rows]))
    wait(leaving)


def block_kernel(
    w_hbm, c_hbm, d_hbm, xs_hbm, normed_hbm, loc_hbm, cts_hbm, enter_ref, pow_ref, keep_ref,
    out_hbm, h_hbm, mixed_hbm, adj_hbm, carry_hbm, c_go_hbm, back_ref, g_d_ref, w_go_ref, w_send_ref, c_send_ref,
    carry_ref, c_go_ref, w_ref, c_ref, d_ref, xs_ref, normed_ref, h_ref, cts_ref,
    out_ref, states_ref, gelu_ref, pre_ref, slope_ref, mixed_ref, low_ref, adj_ref, sems,
):
    lanes, width = enter_ref.shape[0], d_ref.shape[1]
    seg = h_ref.shape[0] // lanes
    span = seg // CHUNKS
    copies = Copies(sems)
    one, rest = pl.ds(0, seg), pl.ds(seg, (lanes - 1) * seg)
    arrays = (loc_hbm, h_ref), (normed_hbm, normed_ref), (xs_hbm, xs_ref), (cts_hbm, cts_ref)
    loc_here = copies.start(loc_hbm.at[one], h_ref.at[one])
    c_here, d_here = copies.start(c_hbm, c_ref), copies.start(d_hbm, d_ref)
    normed_here = copies.start(normed_hbm.at[one], normed_ref.at[one])
    w_here = copies.start(w_hbm, w_ref)
    late_here = [copies.start(a.at[one], b.at[one]) for a, b in arrays[2:]]
    rest_here = [copies.start(a.at[rest], b.at[rest]) for a, b in arrays]
    leaving = []
    lam_span = cload(pow_ref, span - 1)
    for lane in range(lanes):
        first = lane * seg
        rows = pl.ds(first, seg)
        if lane == 0:
            loc_here.wait()
        elif lane == 1:
            wait(rest_here)
        last = first + (span - 1) * CHUNKS
        state = kept(keep_ref, lane * CHUNKS, cload(enter_ref, lane))
        cstore(carry_ref, lane * CHUNKS, state)
        for chunk in range(1, CHUNKS):
            state = fma(lam_span, state, cload(h_ref, last + chunk - 1))
            state = kept(keep_ref, lane * CHUNKS + chunk, state)
            cstore(carry_ref, lane * CHUNKS + chunk, state)
        carry = cload(carry_ref, lane * CHUNKS, CHUNKS)
        for step in range(span):
            at = first + step * CHUNKS
            cstore(h_ref, at, fma(cload(pow_ref, step), carry, cload(h_ref, at, CHUNKS)))
        leaving.append(copies.start(h_ref.at[rows], h_hbm.at[rows]))

        states = h_ref[rows, :].astype(BF16)
        states_ref[rows, :] = states
        if lane == 0:
            wait([normed_here, c_here, d_here])
        mixed = dot_nn(states, c_ref[...]) + d_ref[...] * normed_ref[rows, :].astype(F32)
        square = mixed * mixed
        tanh = jnp.tanh(GELU_K * mixed * (1.0 + GELU_A * square))
        half_up = 0.5 * (1.0 + tanh)
        gelu = (mixed * half_up).astype(BF16)
        gelu_ref[rows, :] = gelu
        slope_ref[rows, :] = half_up + 0.5 * GELU_K * mixed * (1.0 - tanh * tanh) * (
            1.0 + 3.0 * GELU_A * square
        )
        if lane == 0:
            w_here.wait()
        pre = dot_nn(gelu, w_ref[...])
        value = pre[:, :width]
        sig = jax.nn.sigmoid(pre[:, width:])
        gated = value * sig
        if lane == 0:
            wait(late_here)
        out_ref[rows, :] = (xs_ref[rows, :].astype(F32) + gated).astype(BF16)
        leaving.append(copies.start(out_ref.at[rows], out_hbm.at[rows]))
        grad_value = cts_ref[rows, :].astype(F32) * sig
        pre_ref[rows, :width] = grad_value.astype(BF16)
        pre_ref[rows, width:] = (grad_value * (value - gated)).astype(BF16)

    lam, lam_span = conj(cload(pow_ref, 0)), conj(lam_span)
    total = None
    for lane in range(lanes):
        rows = pl.ds(lane * seg, seg)
        grad_mixed = dot_nt(pre_ref[rows, :], w_ref[...]) * slope_ref[rows, :]
        mixed_ref[rows, :] = grad_mixed
        leaving.append(copies.start(mixed_ref.at[rows], mixed_hbm.at[rows]))
        add = jnp.sum(grad_mixed * normed_ref[rows, :].astype(F32), axis=0, keepdims=True)
        total = add if total is None else total + add
        low = grad_mixed.astype(BF16)
        low_ref[rows, :] = low
        adj_ref[rows, :] = dot_nt(low, c_ref[...])
        adj = cload(adj_ref, (lane + 1) * seg - CHUNKS, CHUNKS)
        for step in reversed(range(span - 1)):
            at = lane * seg + step * CHUNKS
            adj = fma(lam, adj, cload(adj_ref, at, CHUNKS))
            cstore(adj_ref, at, adj)
        leaving.append(copies.start(adj_ref.at[rows], adj_hbm.at[rows]))
        state = None
        for chunk in reversed(range(CHUNKS)):
            here = adj[0][chunk : chunk + 1], adj[1][chunk : chunk + 1]
            state = here if state is None else fma(lam_span, state, here)
            state = kept(keep_ref, lane * CHUNKS + chunk, state)
        cstore(back_ref, lane, state)
    g_d_ref[...] = total
    leaving.append(copies.start(carry_ref, carry_hbm))
    put_halves(dot_tn(states_ref[...], low_ref[...]), c_go_ref, c_send_ref)
    leaving.append(copies.start(c_go_ref, c_go_hbm))
    put_halves(dot_tn(gelu_ref[...], pre_ref[...]), w_go_ref, w_send_ref)
    wait(leaving)


def states_kernel(
    c_go_hbm, carry_ref, b_ref, gamma_ref, d_ref, normed_ref, h_ref, adj_ref, leave_ref, pow_ref, keep_ref, g_d_ref,
    c_got_ref,
    low_hbm, go_ref, send_ref, c_ref, low_ref, after_ref, small_ref, sems,
):
    copies = Copies(sems)
    c_here = copies.start(c_go_hbm, c_ref)
    leaving = []
    lanes = leave_ref.shape[0]
    seg = normed_ref.shape[0] // lanes
    span = seg // CHUNKS
    back = conj(cload(pow_ref, span - 1))
    factor = jnp.exp(gamma_ref[...])
    sums = None
    for lane in range(lanes):
        first = lane * seg
        state = cload(leave_ref, lane)
        cstore(after_ref, CHUNKS - 1, state)
        for chunk in reversed(range(1, CHUNKS)):
            state = fma(back, state, cload(adj_ref, first + chunk))
            state = kept(keep_ref, lane * CHUNKS + chunk, state)
            cstore(after_ref, chunk - 1, state)
        after = cload(after_ref, 0, CHUNKS)
        before = cload(carry_ref, lane * CHUNKS, CHUNKS)
        for step in range(span):
            at = first + step * CHUNKS
            full = fma(conj(cload(pow_ref, span - 1 - step)), after, cload(adj_ref, at, CHUNKS))
            add = cmul(conj(before), full)
            sums = add if sums is None else cadd(sums, add)
            cstore(low_ref, at, ((full[0] * factor).astype(BF16), (full[1] * factor).astype(BF16)))
            before = cload(h_ref, at, CHUNKS)
        rows = pl.ds(first, seg)
        leaving.append(copies.start(low_ref.at[rows], low_hbm.at[rows]))
    grad_b = dot_tn(normed_ref[...], low_ref[...])
    n = gamma_ref.shape[1]
    prod = grad_b * b_ref[...].astype(F32)
    small_ref[...] = jnp.zeros_like(small_ref)
    small_ref[0:1, :n] = jnp.sum(sums[0], axis=0, keepdims=True)
    small_ref[0:1, n:] = jnp.sum(sums[1], axis=0, keepdims=True)
    small_ref[1:2, :] = jnp.sum(prod, axis=0, keepdims=True)
    small_ref[8:9, :] = jnp.sum(prod.T, axis=0, keepdims=True) + d_ref[...] * g_d_ref[...]
    small_ref[9:10, :] = g_d_ref[...]
    put_halves(grad_b, go_ref.at[pl.ds(0, n)], send_ref.at[pl.ds(0, n)])
    put_halves(small_ref[...], go_ref.at[pl.ds(n, 8)], send_ref.at[pl.ds(n, 8)])
    c_here.wait()
    c_ref[...] += c_got_ref[...]
    wait(leaving)


def pieces_kernel(c_ref, b_keep_ref, b_got_ref, own_ref, small_ref, *send_refs):
    count, n = len(send_refs) + 1, c_ref.shape[0]
    rows = n // count
    mine = lax.axis_index("dp")
    small = b_keep_ref[n:, :] + b_got_ref[n:, :]
    small_ref[...] = small
    for mask in range(count):
        start = pl.multiple_of((mine ^ mask) * rows, rows)
        at = pl.ds(start, rows)
        c = c_ref[at, :]
        b = b_keep_ref[at, :] + b_got_ref[at, :]
        if mask == 0:
            own_ref[0], own_ref[1] = c, b
        else:
            ref = send_refs[mask - 1]
            ref[:rows, :], ref[rows : 2 * rows, :], ref[2 * rows :, :] = c, b, small


def input_kernel(
    gain_hbm, b_hbm, d_hbm, xs_hbm, cts_hbm, low_hbm, mixed_hbm, out_hbm,
    in_hbm, block_hbm, gain_ref, b_ref, d_ref, xs_ref, cts_ref, low_ref, mixed_ref, out_ref,
    in_ref, block_ref, sems,
):
    lanes, seg, width = in_ref.shape
    copies = Copies(sems)
    params = [copies.start(a, b) for a, b in ((gain_hbm, gain_ref), (b_hbm, b_ref), (d_hbm, d_ref))]
    here = copies.lanes(
        lanes, (low_hbm, low_ref), (mixed_hbm, mixed_ref), (xs_hbm, xs_ref), (cts_hbm, cts_ref),
        (out_hbm, out_ref),
    )
    wait(params)
    leaving = []
    order_back = scan_order(seg, True)
    for lane in range(lanes):
        rows = pl.ds(lane * seg, seg)
        wait(here[lane])
        grad_normed = dot_nt(low_ref[rows, :], b_ref[...]) + mixed_ref[rows, :] * d_ref[...]
        xhat, scale = norm_stats(xs_ref[rows, :].astype(F32))
        dxhat = grad_normed * gain_ref[...]
        one = jnp.mean(dxhat, axis=-1, keepdims=True)
        two = jnp.mean(dxhat * xhat, axis=-1, keepdims=True)
        grad = (cts_ref[rows, :].astype(F32) + (dxhat - one - xhat * two) * scale).astype(BF16)
        in_ref[lane] = dot_nn(order_back, grad).astype(BF16)
        leaving.append(copies.start(in_ref.at[lane], in_hbm.at[lane]))
        block_ref[lane] = dot_nn(order_back, out_ref[rows, :]).astype(BF16)
        leaving.append(copies.start(block_ref.at[lane], block_hbm.at[lane]))
    wait(leaving)


def finish_kernel(
    nu_hbm, th_hbm, gain_hbm, small_ref, pow_ref, gain_out, gamma_out, nu_out, th_out, d_out,
    nu_ref, th_ref, gain_ref, sems,
):
    n = nu_ref.shape[1]
    copies = Copies(sems)
    for copy in [copies.start(a, b) for a, b in ((nu_hbm, nu_ref), (th_hbm, th_ref), (gain_hbm, gain_ref))]:
        copy.wait()
    lam = cload(pow_ref, 0)
    p, q = small_ref[0:1, :n], small_ref[0:1, n:]
    nu_out[...] = -jnp.exp(nu_ref[...]) * (p * lam[0] + q * lam[1])
    th_out[...] = -jnp.exp(th_ref[...]) * (p * lam[1] - q * lam[0])
    gamma_out[...] = small_ref[1:2, :n] + small_ref[1:2, n:]
    gain_out[...] = small_ref[8:9, :] / gain_ref[...]
    d_out[...] = small_ref[9:10, :]


def swap(value, axis, bit):
    count = lax.axis_size(axis)
    return lax.ppermute(value, axis, [(i, i ^ (1 << bit)) for i in range(count)])


def entering(pair, backward, beside=None):
    lanes, n = pair.shape[0] // 2, pair.shape[1] // 2

    def mul(x, y):
        return jnp.concatenate(
            [x[:, :n] * y[:, :n] - x[:, n:] * y[:, n:], x[:, :n] * y[:, n:] + x[:, n:] * y[:, :n]], 1
        )

    def join(early, late):
        return late[0] + mul(late[1], early[0]), mul(late[1], early[1])

    count, mine = lax.axis_size("seq"), lax.axis_index("seq")
    one = jnp.concatenate([jnp.ones_like(pair[:lanes, :n]), jnp.zeros_like(pair[:lanes, n:])], 1)
    before = jnp.zeros_like(one), one
    bit = 0
    while 1 << bit < count:
        size = 2 if bit == 0 else min(4, count >> bit)
        if beside is not None and bit == (1 if not backward else 0):
            pair, beside = tie(pair, beside)
        parts = [pair] + [
            lax.ppermute(pair, "seq", [(i, i ^ (mask << bit)) for i in range(count)])
            for mask in reversed(range(1, size))
        ][::-1]
        place = mine // (1 << bit) % size ^ (size - 1 if backward else 0)
        ordered = []
        for k in range(size):
            part = parts[0]
            for mask in range(1, size):
                part = jnp.where(place ^ k == mask, parts[mask], part)
            ordered.append((part[:lanes], part[lanes:]))
        sofar = None
        for k, item in enumerate(ordered):
            if k:
                joined = join(sofar, before)
                before = tuple(jnp.where(place == k, new, old) for new, old in zip(joined, before))
            sofar = item if sofar is None else join(sofar, item)
        pair = jnp.concatenate(sofar, 0)
        bit += size.bit_length() - 1
    return before[0] if beside is None else (before[0], beside)


def bits(axis, first=0):
    return [(axis, bit) for bit in range(first, lax.axis_size(axis).bit_length() - 1)]


def phases():
    return [bits("dp") + bits("seq", 1), bits("dp")[::-1] + bits("seq", 1)[::-1]]


def hop(value, phase):
    orders, count = phases(), lax.axis_size("seq")
    pairs = []
    for device in range(lax.axis_size("dp") * count):
        axis, bit = orders[device % 2][phase]
        pairs.append((device, device ^ ((1 << bit) * (count if axis == "dp" else 1))))
    return lax.ppermute(value, ("dp", "seq"), pairs)


def my_bit(phase):
    one, two = (lax.axis_index(axis) // (1 << bit) % 2 for axis, bit in (o[phase] for o in phases()))
    return jnp.where(lax.axis_index("seq") % 2 == 0, one, two)


def piece(value, which, count):
    rows = value.shape[1] // count
    return lax.dynamic_slice(value, (0, which * rows, 0), (value.shape[0], rows, value.shape[2]))


def pack(value, extra):
    if extra is None:
        return value
    return jnp.concatenate([value.reshape(-1, value.shape[2]), extra], 0)


def unpack(sent, value, extra):
    if extra is None:
        return sent, None
    rows = value.shape[0] * value.shape[1]
    return sent[:rows].reshape(value.shape), sent[rows:]


def tree_sum(values):
    while len(values) > 1:
        values = [a + b for a, b in zip(values[::2], values[1::2])]
    return values[0]


def scatter(value, phase, extra=None):
    mine = my_bit(phase)
    send, keep = piece(value, 1 - mine, 2), piece(value, mine, 2)
    got, more = unpack(hop(pack(send, extra), phase), send, extra)
    return keep + got, None if extra is None else extra + more


def double(value, phase, extra=None):
    got, more = unpack(hop(pack(value, extra), phase), value, extra)
    return value + got, None if extra is None else extra + more


def gather(value, phase):
    got = hop(value, phase)
    return join_rows([value, got], my_bit(phase))


def join_rows(parts, mine):
    count = len(parts)
    if count == 1:
        return parts[0]
    half = count // 2
    low = join_rows(parts[:half], mine % half)
    high = join_rows(parts[half:], mine % half)
    first = mine // half == 0
    return jnp.where(first, jnp.concatenate([low, high], 1), jnp.concatenate([high, low], 1))


def across(value, mask):
    return lax.ppermute(value, "dp", [(i, i ^ mask) for i in range(lax.axis_size("dp"))])


def sum_dp(own, sends, extra):
    parts, extras = [own], [extra]
    for mask, send in enumerate(sends):
        got, more = unpack(across(send, mask + 1), own, extra)
        parts.append(got)
        extras.append(more)
    return tree_sum(parts), tree_sum(extras)


def gather_dp(value):
    count, mine = lax.axis_size("dp"), lax.axis_index("dp")
    parts = [value]
    for mask in reversed(range(1, count)):
        parts.insert(1, across(value, mask))
    return join_rows(parts, mine)


def tie(*values):
    return lax.optimization_barrier(values)


def after(value, *others):
    for other in others:
        value = value + jnp.minimum(jnp.abs(other[(0,) * other.ndim]), 0.0)
    return value


def assemble_kernel(mine, other, *refs):
    whole, sems = refs[:-1], refs[-1]
    copies = Copies(sems)
    rows = mine.shape[0]
    first = pl.multiple_of(lax.rem(lax.axis_index("seq"), 2) * rows, rows)
    column = 0
    for out in whole:
        columns = pl.ds(column, out.shape[1])
        copies.start(mine.at[:, columns], out.at[pl.ds(first, rows)])
        copies.start(other.at[:, columns], out.at[pl.ds(pl.multiple_of(rows - first, rows), rows)])
        column += out.shape[1]
    wait(copies.all)


def on_device(
    block_in, cotangent, bucket_id, assignment, norm_gain, b_proj, gamma_log, nu_log, theta_log,
    c_proj, d_skip, glu_weight,
):
    _, lanes, seg, width = block_in.shape
    n = nu_log.shape[0]
    two = 2 * n
    tokens = lanes * seg
    span = seg // CHUNKS
    short = seg * lax.axis_size("seq") // bucket_id.shape[2]
    gain, gamma, nu, theta, skip = (
        v.reshape(1, -1) for v in (norm_gain, gamma_log, nu_log, theta_log, d_skip)
    )
    hbm, vmem = pl.BlockSpec(memory_space=pltpu.HBM), pl.BlockSpec(memory_space=pltpu.VMEM)

    def call(kernel, name, micros, outs, far, near, fetched=None, scratch=(), sems=0, far_outs=0, limit=4, pin=False, wait_for=()):
        fetched = far if fetched is None else fetched
        far = [pltpu.with_memory_space_constraint(v, pltpu.HBM) for v in far]
        if pin:
            near = [pltpu.with_memory_space_constraint(v, pltpu.VMEM) for v in near]
        shapes = [
            pltpu.HBM(shape, kind) if k < far_outs else jax.ShapeDtypeStruct(shape, kind)
            for k, (shape, kind) in enumerate(outs)
        ]
        room = [(pltpu.SMEM if v.dtype == jnp.int32 else pltpu.VMEM)(v.shape, v.dtype) for v in fetched]
        count, extra = len(far) + len(near), len(wait_for)

        def body(*refs):
            kernel(*refs[:count], *refs[count + extra :])

        return pl.pallas_call(
            body,
            in_specs=[hbm] * len(far) + [vmem] * len(near) + [pl.BlockSpec(memory_space=pl.ANY)] * extra,
            out_specs=[hbm] * far_outs + [vmem] * (len(outs) - far_outs),
            out_shape=shapes,
            scratch_shapes=room
            + [pltpu.VMEM(shape, kind) for shape, kind in scratch]
            + ([pltpu.SemaphoreType.DMA((sems,))] if sems else []),
            compiler_params=pltpu.CompilerParams(vmem_limit_bytes=limit * 1024 * 1024),
            cost_estimate=cost(micros),
            name=name,
        )(*far, *near, *wait_for)

    low_rows, full_rows = ((tokens, width), BF16), ((tokens, two), F32)
    lane_rows = ((lanes, seg, width), BF16)
    xs, normed, loc, pair, powers, keep = call(
        functools.partial(first_kernel, short), "forward_local", 4,
        [
            low_rows, low_rows, full_rows, ((2 * lanes, two), F32), ((span, two), F32),
            ((lanes * CHUNKS, two), F32),
        ],
        [bucket_id[0], assignment, block_in[0], gain, b_proj, gamma, nu, theta], [],
        scratch=[low_rows, low_rows, full_rows], sems=4 * lanes + 7, far_outs=3, limit=12,
    )
    enter, cotangent_later = entering(pair, False, cotangent[0])
    (cts,) = call(
        order_kernel, "cotangent_order", 2, [low_rows], [cotangent_later], [],
        scratch=[low_rows], sems=2 * lanes, far_outs=1, limit=8,
    )

    chunk_rows, half_rows = ((lanes * CHUNKS, two), F32), ((n, width), F32)
    out, h, grad_mixed, adj, carry, c_keep, back_total, grad_d, w_keep, w_send, c_send = call(
        block_kernel, "block", 10,
        [
            low_rows, full_rows, full_rows, full_rows, chunk_rows, half_rows, ((lanes, two), F32),
            ((1, width), F32), ((n, 2 * width), F32), ((n, 2 * width), F32), half_rows,
        ],
        [glu_weight, c_proj, skip, xs, normed, loc, cts], [enter, powers, keep], fetched=(),
        scratch=[
            chunk_rows, half_rows, ((width, 2 * width), BF16), ((two, width), BF16), ((1, width), F32),
            low_rows, low_rows, full_rows, low_rows,
            low_rows, low_rows, low_rows, ((tokens, 2 * width), BF16), full_rows, full_rows, low_rows,
            full_rows,
        ],
        sems=4 * lanes + 13, far_outs=6, limit=36,
    )

    decay = pair[lanes:]
    back_pair = jnp.concatenate(
        [back_total, jnp.concatenate([decay[:, :n], -decay[:, n:]], 1)], 0
    )
    near, last = len(bits("dp")), len(phases()[0]) - 1
    c_got = swap(c_send, "seq", 0)
    w = (w_keep + swap(w_send, "seq", 0))[None]
    leave, w = entering(back_pair, True, w)
    w, _ = scatter(w, 0)

    back_low, b_keep, b_send, c = call(
        states_kernel, "adjoint_states", 3,
        [low_rows, ((n + 8, two), F32), ((n + 8, two), F32), half_rows],
        [c_keep], [carry, b_proj, gamma, skip, normed, h, adj, leave, powers, keep, grad_d, c_got], fetched=(),
        scratch=[low_rows, ((CHUNKS, two), F32), ((16, two), F32)],
        sems=lanes + 1, far_outs=1, limit=8, wait_for=[w],
    )

    def back_input(back_low):
        return call(
            input_kernel, "back_input", 4, [lane_rows, lane_rows],
            [gain, b_proj, skip, xs, cts, back_low, grad_mixed, out], [], wait_for=[cb, finished[0], w],
            scratch=[lane_rows, lane_rows], sems=7 * lanes + 3, far_outs=2, limit=12,
        )

    for phase in range(1, near):
        w, _ = scatter(w, phase)
    groups = lax.axis_size("dp")
    cut = n // groups
    own, small, *sends = call(
        pieces_kernel, "pieces", 1,
        [((2, cut, width), F32), ((8, two), F32)] + [((2 * cut + 8, width), F32)] * (groups - 1),
        [], [c, b_keep, swap(b_send, "seq", 0)], wait_for=[w] if True else [],
    )
    cb, small = sum_dp(own, sends, small)

    def only(step):
        return lambda value, extra=None: (step(value), extra)

    steps = [functools.partial(scatter, phase=p) for p in range(near, last)]
    steps += [functools.partial(double, phase=last)]
    steps += [only(functools.partial(gather, phase=p)) for p in reversed(range(near, last))]
    ahead = steps + [only(functools.partial(gather, phase=p)) for p in reversed(range(near))]
    lead = 1
    for turn in range(lead):
        w, _ = ahead[turn](w)
    for turn, step in enumerate(steps):
        if turn + lead < len(ahead):
            w_next, _ = ahead[turn + lead](w)
        cb, small = step(cb, extra=small)
        w = w_next
    for turn in range(len(steps) + lead, len(ahead)):
        w, _ = ahead[turn](w)
    got = swap(small, "seq", 0)
    small = join_rows([small[None], got[None]], lax.axis_index("seq") % 2)[0]
    finished = call(
        finish_kernel, "finish", 1, [((1, v), F32) for v in (width, n, n, n, width)],
        [nu, theta, gain], [small, powers], sems=3,
    )
    grad_in, block_out = back_input(back_low)
    cb = gather_dp(cb)
    cb, grad_in, block_out = tie(cb, grad_in, block_out)
    w, cb = w[0], jnp.concatenate([cb[0], cb[1]], 1)

    grad_gain, grad_gamma, grad_nu, grad_theta, grad_d = finished

    def assemble(mine, widths, wait_for):
        return call(
            assemble_kernel, "assemble", 2, [((2 * mine.shape[0], v), F32) for v in widths],
            [], [mine, swap(mine, "seq", 0)], sems=2 * len(widths), far_outs=len(widths), pin=True, wait_for=wait_for,
        )

    (grad_w,) = assemble(w, [2 * width], [grad_in])
    grad_c, grad_b = assemble(cb, [width, two], [])
    return (
        block_out[None], grad_in[None], grad_gain[0], grad_b, grad_gamma[0], grad_nu[0], grad_theta[0],
        grad_c, grad_d[0], grad_w,
    )


def solution(mesh):
    rows = P("dp", None, "seq", None)
    in_specs = (rows, rows, P("dp", None, None), P("dp", None)) + (P(),) * 8
    out_specs = (rows, rows) + (P(),) * 8
    return jax.shard_map(
        on_device, mesh=mesh, in_specs=in_specs, out_specs=out_specs, check_vma=False
    )
```

time: 124 us -> 109 us (0.88)
  starting transfers between devices: 43.7 us -> 32.6 us
  Pallas kernels: 33.5 us -> 30 us
  waiting for transfers between devices: 41.6 us -> 38.1 us
  local copies, waits for them, and re-layouts: 0.42 us -> 2.26 us
    ppermute x35 -> x6, starting transfers between devices: 43.7 us -> 0.82 us  [swap(): return lax.ppermute(value, axis, [(i, i ^ 1 << bit) for i in range(count)])]
    ppermute x35 -> x6, waiting for transfers between devices: 41.6 us -> 3.28 us  [swap(): return lax.ppermute(value, axis, [(i, i ^ 1 << bit) for i in range(count)])]
    ppermute x0 -> x24, waiting for transfers between devices: none -> 34.8 us  [the longest x10 23 us: hop(): return lax.ppermute(value, ('dp', 'seq'), pairs)]
    ppermute x0 -> x24, starting transfers between devices: none -> 31.8 us  [the longest x10 14 us: hop(): return lax.ppermute(value, ('dp', 'seq'), pairs)]
    pallas_call x7 -> x9, Pallas kernels: 33.5 us -> 30 us  [call(): pl.pallas_call(body, in_specs=[hbm] * len(far) + [vmem] * len(near) + [pl...]
    broadcast_in_dim x0 -> x1, other arithmetic: none -> 1.51 us  [on_device(): w = (w_keep + swap(w_send, 'seq', 0))[None]]
    unnamed x2 -> x24, local copies, waits for them, and re-layouts: 0.01 us -> 1.35 us
  transfers between devices with their start and end apart: 35 -> 30, of which waited for: 25 -> 17; matrix products, arithmetic and copies ran while one was open for 1% -> 4% of each run, Pallas kernels for 12% -> 12%
where the time goes in v1:
time: 109 us
  waiting for transfers between devices  38.1 us (35%)
  starting transfers between devices  32.6 us (30%)
  Pallas kernels  30 us (28%)
  other arithmetic  3.73 us (3%)
  local copies, waits for them, and re-layouts  2.26 us (2%)
  between operations  1.73 us (2%)
    pallas_call x9, Pallas kernels, call(): pl.pallas_call(body, in_specs=[hbm] * len(far) + [vmem] * len(near) + [pl...  30 us
    ppermute x10, waiting for transfers between devices, hop(): return lax.ppermute(value, ('dp', 'seq'), pairs)  23 us
    ppermute x10, starting transfers between devices, hop(): return lax.ppermute(value, ('dp', 'seq'), pairs)  14 us
    ppermute x8, starting transfers between devices, entering(): lax.ppermute(pair, 'seq', [(i, i ^ mask << bit) for i in range(count)])  10.7 us
    ppermute x6, starting transfers between devices, across(): lax.ppermute(value, 'dp', [(i, i ^ mask) for i in range(lax.axis_size('dp...  7.11 us
    ppermute x8, waiting for transfers between devices, entering(): lax.ppermute(pair, 'seq', [(i, i ^ mask << bit) for i in range(count)])  6.37 us
    ppermute x6, waiting for transfers between devices, across(): lax.ppermute(value, 'dp', [(i, i ^ mask) for i in range(lax.axis_size('dp...  5.47 us
    ppermute x6, waiting for transfers between devices, swap(): return lax.ppermute(value, axis, [(i, i ^ 1 << bit) for i in range(count)])  3.28 us
  transfers between devices with their start and end apart: 30, of which 17 were waited for; matrix products, arithmetic and copies ran while one was open for 4% of the time, Pallas kernels for 12%

profile of v1, /device:TPU:0, one launch (start us, length us, event | category | flops | bytes accessed | tf_op | source)
XLA Modules:
  0.0 108.5 jit_solution(15137245011758549793)
XLA Ops:
  0.7 5.0 %forward_local.1 = (bf16[1024,512]{1,0:T(8,128)(2,1)}, bf16[1024,512]{1,0:T(8,128)(2,1)}, f32[1024,512]{1,0:T(8,128)}, f32[8,512]{1,0:T(8,128)S(1)}, f32[32,512]{1,0:T(8,128)S(1)}, /*index=5*/f32[32,512]{1,0:T(8,128)S(1)}) custom-call(s32[4,16]{1,0:T(4,128)} %bitcast.54, s32[1,4]{1,0:T(1,128)} %refs_1_.3, bf16[4,256,512]{2,1,0:T(8,128)(2,1)} %bitcast.52, ...), custom_call_target="tpu_custom_call" | custom-call | flops 4400000000 | bytes 12000000 | tf_op jit(solution)/shard_map/forward_local/pallas_call | solution.py:624
  5.6 0.5 collective-permute-start
  6.1 0.8 collective-permute-done
  7.0 3.0 %collective-permute-start.3 = (f32[8,512]{1,0:T(8,128)S(1)}, f32[8,512]{1,0:T(8,128)S(1)}, u32[]{:S(2)}, u32[]{:S(2)}) collective-permute-start(f32[8,512]{1,0:T(8,128)S(1)} %maximum_maximum_fusion), channel_id=1, source_target_pairs={{0,2},{1,3},{2,0},{3,1},{4,6},{5,7},{6,4},{7,5},{8,10},{9,11},{10,... | collective-permute-start | bytes 49160 | tf_op jit(solution)/shard_map/ppermute | solution.py:454
  10.0 2.6 %collective-permute-start.2 = (f32[8,512]{1,0:T(8,128)S(1)}, f32[8,512]{1,0:T(8,128)S(1)}, u32[]{:S(2)}, u32[]{:S(2)}) collective-permute-start(f32[8,512]{1,0:T(8,128)S(1)} %maximum_maximum_fusion), channel_id=1, source_target_pairs={{0,4},{1,5},{2,6},{3,7},{4,0},{5,1},{6,2},{7,3},{8,12},{9,13},{10,... | collective-permute-start | bytes 49160 | tf_op jit(solution)/shard_map/ppermute | solution.py:454
  12.6 2.7 %cotangent_order.1.refs_6_.refs_4_ = bf16[1024,512]{1,0:T(8,128)(2,1)} custom-call(bf16[4,256,512]{2,1,0:T(8,128)(2,1)} %bitcast.53), custom_call_target="tpu_custom_call" | custom-call | flops 2200000000 | bytes 6000000 | tf_op jit(solution)/shard_map/cotangent_order/pallas_call | solution.py:624
  15.4 2.8 %collective-permute-done.1 = f32[8,512]{1,0:T(8,128)S(1)} collective-permute-done((f32[8,512]{1,0:T(8,128)S(1)}, f32[8,512]{1,0:T(8,128)S(1)}, u32[]{:S(2)}, u32[]{:S(2)}) %collective-permute-start.1) | collective-permute-done | bytes 16416 | tf_op jit(solution)/shard_map/ppermute | solution.py:454
  18.3 10.4 %block.1 = (bf16[1024,512]{1,0:T(8,128)(2,1)}, f32[1024,512]{1,0:T(8,128)}, f32[1024,512]{1,0:T(8,128)}, f32[1024,512]{1,0:T(8,128)}, f32[32,512]{1,0:T(8,128)},...) custom-call(bf16[512,1024]{1,0:T(8,128)(2,1)} %refs_0_.1, ...), custom_call_target="tpu_custom_call" | custom-call | flops 11000000512 | bytes 30000000 | tf_op jit(solution)/shard_map/block/pallas_call | solution.py:624
  29.0 0.4 collective-permute-start.9
  29.4 2.3 %collective-permute-done.4 = f32[256,1024]{1,0:T(8,128)} collective-permute-done((f32[256,1024]{1,0:T(8,128)S(1)}, f32[256,1024]{1,0:T(8,128)}, u32[]{:S(2)}, u32[]{:S(2)}) %collective-permute-start.4) | collective-permute-done | bytes 1048608 | tf_op jit(solution)/shard_map/ppermute | solution.py:431
  31.6 1.5 %add_bitcast_fusion = f32[1,256,1024]{2,1,0:T(8,128)S(1)} fusion(f32[256,1024]{1,0:T(8,128)S(1)} %get-tuple-element.65, f32[256,1024]{1,0:T(8,128)} %collective-permute-done.4), kind=kLoop, calls=%fused_computation.4 | loop fusion | flops 262144 | bytes 3145728 | tf_op jit(solution)/shard_map/broadcast_in_dim | solution.py:677
  33.5 1.6 %collective-permute-start.10 = (f32[1,128,1024]{2,1,0:T(8,128)S(1)}, f32[1,128,1024]{2,1,0:T(8,128)S(1)}, u32[]{:S(2)}, u32[]{:S(2)}) collective-permute-start(f32[1,128,1024]{2,1,0:T(8,128)S(1)} %constant_dynamic-slice_fusion.3), channel_id=1, source_target_pairs={{0,8},{1,17},{2,10},{3,19},{4,12},{5,21},{6,14},{7,23},{8,0},{9,25... | collective-permute-start | bytes 1572872 | tf_op jit(solution)/shard_map/ppermute | solution.py:489
  35.2 1.6 %collective-permute-start.7 = (f32[8,512]{1,0:T(8,128)S(1)}, f32[8,512]{1,0:T(8,128)S(1)}, u32[]{:S(2)}, u32[]{:S(2)}) collective-permute-start(f32[8,512]{1,0:T(8,128)S(1)} %maximum_maximum_fusion.2), channel_id=1, source_target_pairs={{0,4},{1,5},{2,6},{3,7},{4,0},{5,1},{6,2},{7,3},{8,12},{9,13},{10,... | collective-permute-start | bytes 49160 | tf_op jit(solution)/shard_map/ppermute | solution.py:454
  36.8 2.8 %collective-permute-start.6 = (f32[8,512]{1,0:T(8,128)S(1)}, f32[8,512]{1,0:T(8,128)S(1)}, u32[]{:S(2)}, u32[]{:S(2)}) collective-permute-start(f32[8,512]{1,0:T(8,128)S(1)} %maximum_maximum_fusion.2), channel_id=1, source_target_pairs={{0,6},{1,7},{2,4},{3,5},{4,2},{5,3},{6,0},{7,1},{8,14},{9,15},{10,... | collective-permute-start | bytes 49160 | tf_op jit(solution)/shard_map/ppermute | solution.py:454
  39.6 0.3 collective-permute-done.7
  39.9 2.4 %collective-permute-done.6 = f32[8,512]{1,0:T(8,128)S(1)} collective-permute-done((f32[8,512]{1,0:T(8,128)S(1)}, f32[8,512]{1,0:T(8,128)S(1)}, u32[]{:S(2)}, u32[]{:S(2)}) %collective-permute-start.6) | collective-permute-done | bytes 16416 | tf_op jit(solution)/shard_map/ppermute | solution.py:454
  42.8 0.7 constant_dynamic-slice_fusion.2
  43.5 1.5 %collective-permute-start.12 = (f32[1,64,1024]{2,1,0:T(8,128)}, f32[1,64,1024]{2,1,0:T(8,128)}, u32[]{:S(2)}, u32[]{:S(2)}) collective-permute-start(f32[1,64,1024]{2,1,0:T(8,128)} %constant_dynamic-slice_fusion.2), channel_id=1, source_target_pairs={{0,16},{1,9},{2,18},{3,11},{4,20},{5,13},{6,22},{7,15},{8,24},{9,1... | collective-permute-start | bytes 786440 | tf_op jit(solution)/shard_map/ppermute | solution.py:489
  45.1 2.2 %adjoint_states.1 = (bf16[1024,512]{1,0:T(8,128)(2,1)}, f32[264,512]{1,0:T(8,128)S(1)}, f32[264,512]{1,0:T(8,128)S(1)}, f32[256,512]{1,0:T(8,128)S(1)}) custom-call(f32[256,512]{1,0:T(8,128)} %get-tuple-element.60.refs_0_, f32[32,512]{1,0:T(8,128)S(1)} %copy-done.10, bf16[512,512]{1,0:T(8,128)(2,1)S(1)} %copy-done, f32[1,256]{1,0:T(1,128)S(1)} %bitcast.37, ...), custom_call_target="tpu_custom_call" | custom-call | flops 3300000000 | bytes 9000000 | tf_op jit(solution)/shard_map/adjoint_states/pallas_call | solution.py:624
  47.4 2.8 %collective-permute-done.12 = f32[1,64,1024]{2,1,0:T(8,128)} collective-permute-done((f32[1,64,1024]{2,1,0:T(8,128)}, f32[1,64,1024]{2,1,0:T(8,128)}, u32[]{:S(2)}, u32[]{:S(2)}) %collective-permute-start.12) | collective-permute-done | bytes 262176 | tf_op jit(solution)/shard_map/ppermute | solution.py:489
  50.2 1.0 dynamic-slice_add_fusion.1.refs_3_
  51.4 1.6 %collective-permute-start.13 = (f32[136,512]{1,0:T(8,128)S(1)}, f32[136,512]{1,0:T(8,128)S(1)}, u32[]{:S(2)}, u32[]{:S(2)}) collective-permute-start(f32[136,512]{1,0:T(8,128)S(1)} %get-tuple-element.75), channel_id=1, source_target_pairs={{0,8},{8,0},{16,24},{24,16},{1,9},{9,1},{17,25},{25,17},{2,10},{10... | collective-permute-start | bytes 835592 | tf_op jit(solution)/shard_map/ppermute | solution.py:550
  53.0 1.5 %collective-permute-start.14 = (f32[136,512]{1,0:T(8,128)S(1)}, f32[136,512]{1,0:T(8,128)S(1)}, u32[]{:S(2)}, u32[]{:S(2)}) collective-permute-start(f32[136,512]{1,0:T(8,128)S(1)} %get-tuple-element.76), channel_id=1, source_target_pairs={{0,16},{8,24},{16,0},{24,8},{1,17},{9,25},{17,1},{25,9},{2,18},{10... | collective-permute-start | bytes 835592 | tf_op jit(solution)/shard_map/ppermute | solution.py:550
  54.5 0.5 collective-permute-start.15
  55.0 1.6 %collective-permute-done.23 = f32[1,32,1024]{2,1,0:T(8,128)S(1)} collective-permute-done((f32[1,32,1024]{2,1,0:T(8,128)S(1)}, f32[1,32,1024]{2,1,0:T(8,128)S(1)}, u32[]{:S(2)}, u32[]{:S(2)}) %collective-permute-start.23) | collective-permute-done | bytes 131104 | tf_op jit(solution)/shard_map/ppermute | solution.py:489
  56.6 1.6 %collective-permute-start.24 = (f32[1,32,1024]{2,1,0:T(8,128)S(1)}, f32[1,32,1024]{2,1,0:T(8,128)S(1)}, u32[]{:S(2)}, u32[]{:S(2)}) collective-permute-start(f32[1,32,1024]{2,1,0:T(8,128)S(1)} %dynamic-slice_add_fusion.2), channel_id=1, source_target_pairs={{0,4},{1,3},{2,6},{3,1},{4,0},{5,7},{6,2},{7,5},{8,12},{9,11},{10,... | collective-permute-start | bytes 393224 | tf_op jit(solution)/shard_map/ppermute | solution.py:489
  58.2 8.2 %collective-permute-done.24 = f32[1,32,1024]{2,1,0:T(8,128)S(1)} collective-permute-done((f32[1,32,1024]{2,1,0:T(8,128)S(1)}, f32[1,32,1024]{2,1,0:T(8,128)S(1)}, u32[]{:S(2)}, u32[]{:S(2)}) %collective-permute-start.24) | collective-permute-done | bytes 131104 | tf_op jit(solution)/shard_map/ppermute | solution.py:489
  66.7 2.1 %collective-permute-start.16 = (f32[72,512]{1,0:T(8,128)S(1)}, f32[72,512]{1,0:T(8,128)S(1)}, u32[]{:S(2)}, u32[]{:S(2)}) collective-permute-start(f32[72,512]{1,0:T(8,128)S(1)} %pad_maximum_fusion.1), channel_id=1, source_target_pairs={{0,2},{1,5},{2,0},{3,7},{4,6},{5,1},{6,4},{7,3},{8,10},{9,13},{10,... | collective-permute-start | bytes 442376 | tf_op jit(solution)/shard_map/ppermute | solution.py:489
  68.8 2.7 %collective-permute-done.25 = f32[1,32,1024]{2,1,0:T(8,128)S(1)} collective-permute-done((f32[1,32,1024]{2,1,0:T(8,128)S(1)}, f32[1,32,1024]{2,1,0:T(8,128)S(1)}, u32[]{:S(2)}, u32[]{:S(2)}) %collective-permute-start.25) | collective-permute-done | bytes 131104 | tf_op jit(solution)/shard_map/ppermute | solution.py:489
  71.5 1.4 %collective-permute-start.26 = (f32[1,64,1024]{2,1,0:T(8,128)S(1)}, f32[1,64,1024]{2,1,0:T(8,128)S(1)}, u32[]{:S(2)}, u32[]{:S(2)}) collective-permute-start(f32[1,64,1024]{2,1,0:T(8,128)S(1)} %maximum_select_fusion.9), channel_id=1, source_target_pairs={{0,16},{1,9},{2,18},{3,11},{4,20},{5,13},{6,22},{7,15},{8,24},{9,1... | collective-permute-start | bytes 786440 | tf_op jit(solution)/shard_map/ppermute | solution.py:489
  72.8 0.9 collective-permute-done.16
  73.7 2.5 %collective-permute-start.17 = (f32[72,512]{1,0:T(8,128)S(1)}, f32[72,512]{1,0:T(8,128)S(1)}, u32[]{:S(2)}, u32[]{:S(2)}) collective-permute-start(f32[72,512]{1,0:T(8,128)S(1)} %pad_maximum_fusion.2), channel_id=1, source_target_pairs={{0,4},{1,3},{2,6},{3,1},{4,0},{5,7},{6,2},{7,5},{8,12},{9,11},{10,... | collective-permute-start | bytes 442376 | tf_op jit(solution)/shard_map/ppermute | solution.py:489
  76.3 3.2 %collective-permute-done.26 = f32[1,64,1024]{2,1,0:T(8,128)S(1)} collective-permute-done((f32[1,64,1024]{2,1,0:T(8,128)S(1)}, f32[1,64,1024]{2,1,0:T(8,128)S(1)}, u32[]{:S(2)}, u32[]{:S(2)}) %collective-permute-start.26) | collective-permute-done | bytes 262176 | tf_op jit(solution)/shard_map/ppermute | solution.py:489
  79.5 2.9 %collective-permute-start.27 = (f32[1,128,1024]{2,1,0:T(8,128)S(1)}, f32[1,128,1024]{2,1,0:T(8,128)S(1)}, u32[]{:S(2)}, u32[]{:S(2)}) collective-permute-start(f32[1,128,1024]{2,1,0:T(8,128)S(1)} %maximum_select_fusion.6), channel_id=1, source_target_pairs={{0,8},{1,17},{2,10},{3,19},{4,12},{5,21},{6,14},{7,23},{8,0},{9,25... | collective-permute-start | bytes 1572872 | tf_op jit(solution)/shard_map/ppermute | solution.py:489
  82.6 0.4 collective-permute-start.18
  83.0 0.7 collective-permute-done.22
  83.6 1.3 %finish.1 = (f32[1,512]{1,0:T(1,128)}, f32[1,256]{1,0:T(1,128)}, f32[1,256]{1,0:T(1,128)}, f32[1,256]{1,0:T(1,128)}, f32[1,512]{1,0:T(1,128)}) custom-call(f32[1,256]{1,0:T(1,128)} %bitcast.59, f32[1,256]{1,0:T(1,128)} %bitcast.61, f32[1,512]{1,0:T(1,128)} %bitcast.56, f32[16,512]{1,0:T(8,128)S(1)} %maximum_select_fusion.10.refs_3_, ...), custom_call_target="tpu_custom_call" | custom-call | flops 1100000000 | bytes 3000000 | tf_op jit(solution)/shard_map/finish/pallas_call | solution.py:624
  85.0 3.5 %collective-permute-done.18 = f32[2,32,512]{2,1,0:T(8,128)S(1)} collective-permute-done((f32[2,32,512]{2,1,0:T(8,128)S(1)}, f32[2,32,512]{2,1,0:T(8,128)S(1)}, u32[]{:S(2)}, u32[]{:S(2)}) %collective-permute-start.18) | collective-permute-done | bytes 131104 | tf_op jit(solution)/shard_map/ppermute | solution.py:489
  88.5 1.1 %collective-permute-start.21 = (f32[2,64,512]{2,1,0:T(8,128)S(1)}, f32[2,64,512]{2,1,0:T(8,128)S(1)}, u32[]{:S(2)}, u32[]{:S(2)}) collective-permute-start(f32[2,64,512]{2,1,0:T(8,128)S(1)} %maximum_select_fusion.7.refs_8_), channel_id=1, source_target_pairs={{0,24},{8,16},{16,8},{24,0},{1,25},{9,17},{17,9},{25,1},{2,26},{10... | collective-permute-start | bytes 786440 | tf_op jit(solution)/shard_map/ppermute | solution.py:550
  89.6 0.9 collective-permute-start.20
  90.5 1.6 %collective-permute-start.19 = (f32[2,64,512]{2,1,0:T(8,128)S(1)}, f32[2,64,512]{2,1,0:T(8,128)S(1)}, u32[]{:S(2)}, u32[]{:S(2)}) collective-permute-start(f32[2,64,512]{2,1,0:T(8,128)S(1)} %maximum_select_fusion.7.refs_8_), channel_id=1, source_target_pairs={{0,8},{8,0},{16,24},{24,16},{1,9},{9,1},{17,25},{25,17},{2,10},{10... | collective-permute-start | bytes 786440 | tf_op jit(solution)/shard_map/ppermute | solution.py:550
  92.3 0.4 copy-done.4
  92.7 5.7 %back_input.1 = (bf16[4,256,512]{2,1,0:T(8,128)(2,1)}, bf16[4,256,512]{2,1,0:T(8,128)(2,1)}) custom-call(f32[1,512]{1,0:T(1,128)} %bitcast.57, bf16[512,512]{1,0:T(8,128)(2,1)} %refs_1_.5, f32[1,512]{1,0:T(1,128)} %bitcast.34, bf16[1024,512]{1,0:T(8,128)(2,1)} %get-tuple-element.52.refs_3_, bf16[1024,512]{1,0:T(8,128)(2,1)} %cotangent_order.1.refs_6_.refs_4_, ...), custom_call_target="tpu_custom_call" | custom-call | flops 4400000000 | bytes 12000000 | tf_op jit(solution)/shard_map/back_input/pallas_call | solution.py:624
  98.4 5.1 %collective-permute-done.19 = f32[2,64,512]{2,1,0:T(8,128)S(1)} collective-permute-done((f32[2,64,512]{2,1,0:T(8,128)S(1)}, f32[2,64,512]{2,1,0:T(8,128)S(1)}, u32[]{:S(2)}, u32[]{:S(2)}) %collective-permute-start.19) | collective-permute-done | bytes 262176 | tf_op jit(solution)/shard_map/ppermute | solution.py:550
  104.4 0.9 copy-done.3
  105.3 1.3 %assemble.3 = f32[512,1024]{1,0:T(8,128)} custom-call(f32[256,1024]{1,0:T(8,128)S(1)} %maximum_select_fusion.2.refs_0_, f32[256,1024]{1,0:T(8,128)S(1)} %collective-permute-done.29.refs_1_, bf16[4,256,512]{2,1,0:T(8,128)(2,1)S(1)} %copy-done.3), custom_call_target="tpu_custom_call" | custom-call | flops 2200000000 | bytes 6000000 | tf_op jit(solution)/shard_map/assemble/pallas_call | solution.py:624
  106.7 0.3 collective-permute-done.28.refs_1_
  107.0 1.3 %assemble.2 = (f32[512,512]{1,0:T(8,128)}, f32[512,512]{1,0:T(8,128)}) custom-call(f32[256,1024]{1,0:T(8,128)S(1)} %pad_maximum_fusion.refs_0_, f32[256,1024]{1,0:T(8,128)S(1)} %collective-permute-done.28.refs_1_), custom_call_target="tpu_custom_call" | custom-call | flops 2200000000 | bytes 6000000 | tf_op jit(solution)/shard_map/assemble/pallas_call | solution.py:624
  (115 shorter events, 3.0 us)
Async XLA Ops:
  0.6 12.0 %copy-start.11 = (f32[4,512]{1,0:T(4,128)S(1)}, f32[4,512]{1,0:T(4,128)}, u32[]{:S(2)}) copy-start(f32[4,512]{1,0:T(4,128)} %constant.224.clone.1) | copy-start | bytes 24580
  5.6 12.7 %copy-start.8 = (f32[32,512]{1,0:T(8,128)}, f32[32,512]{1,0:T(8,128)S(1)}, u32[]{:S(2)}) copy-start(f32[32,512]{1,0:T(8,128)S(1)} %get-tuple-element.59.refs_9_.refs_10_) | copy-start | bytes 196612
  5.6 1.3 %collective-permute-start = (f32[8,512]{1,0:T(8,128)S(1)}, f32[8,512]{1,0:T(8,128)S(1)}, u32[]{:S(2)}, u32[]{:S(2)}) collective-permute-start(f32[8,512]{1,0:T(8,128)S(1)} %get-tuple-element.55), channel_id=1, source_target_pairs={{0,1},{1,0},{2,3},{3,2},{4,5},{5,4},{6,7},{7,6},{8,9},{9,8},{10,11... | collective-permute-start | bytes 49160 | tf_op jit(solution)/shard_map/ppermute | solution.py:454
  7.0 8.3 %collective-permute-start.3 = (f32[8,512]{1,0:T(8,128)S(1)}, f32[8,512]{1,0:T(8,128)S(1)}, u32[]{:S(2)}, u32[]{:S(2)}) collective-permute-start(f32[8,512]{1,0:T(8,128)S(1)} %maximum_maximum_fusion), channel_id=1, source_target_pairs={{0,2},{1,3},{2,0},{3,1},{4,6},{5,7},{6,4},{7,5},{8,10},{9,11},{10,... | collective-permute-start | bytes 49160 | tf_op jit(solution)/shard_map/ppermute | solution.py:454
  10.0 5.3 %collective-permute-start.2 = (f32[8,512]{1,0:T(8,128)S(1)}, f32[8,512]{1,0:T(8,128)S(1)}, u32[]{:S(2)}, u32[]{:S(2)}) collective-permute-start(f32[8,512]{1,0:T(8,128)S(1)} %maximum_maximum_fusion), channel_id=1, source_target_pairs={{0,4},{1,5},{2,6},{3,7},{4,0},{5,1},{6,2},{7,3},{8,12},{9,13},{10,... | collective-permute-start | bytes 49160 | tf_op jit(solution)/shard_map/ppermute | solution.py:454
  12.6 5.5 %collective-permute-start.1 = (f32[8,512]{1,0:T(8,128)S(1)}, f32[8,512]{1,0:T(8,128)S(1)}, u32[]{:S(2)}, u32[]{:S(2)}) collective-permute-start(f32[8,512]{1,0:T(8,128)S(1)} %maximum_maximum_fusion), channel_id=1, source_target_pairs={{0,6},{1,7},{2,4},{3,5},{4,2},{5,3},{6,0},{7,1},{8,14},{9,15},{10,... | collective-permute-start | bytes 49160 | tf_op jit(solution)/shard_map/ppermute | solution.py:454
  28.8 2.9 %collective-permute-start.4 = (f32[256,1024]{1,0:T(8,128)S(1)}, f32[256,1024]{1,0:T(8,128)}, u32[]{:S(2)}, u32[]{:S(2)}) collective-permute-start(f32[256,1024]{1,0:T(8,128)S(1)} %get-tuple-element.66), channel_id=1, source_target_pairs={{0,1},{1,0},{2,3},{3,2},{4,5},{5,4},{6,7},{7,6},{8,9},{9,8},{10,11... | collective-permute-start | bytes 3145736 | tf_op jit(solution)/shard_map/ppermute | solution.py:431
  29.0 16.1 %collective-permute-start.9 = (f32[256,512]{1,0:T(8,128)S(1)}, f32[256,512]{1,0:T(8,128)S(1)}, u32[]{:S(2)}, u32[]{:S(2)}) collective-permute-start(f32[256,512]{1,0:T(8,128)S(1)} %get-tuple-element.69), channel_id=1, source_target_pairs={{0,1},{1,0},{2,3},{3,2},{4,5},{5,4},{6,7},{7,6},{8,9},{9,8},{10,11... | collective-permute-start | bytes 1572872 | tf_op jit(solution)/shard_map/ppermute | solution.py:431
  31.6 13.4 %copy-start.6 = (f32[1024,512]{1,0:T(8,128)S(1)}, f32[1024,512]{1,0:T(8,128)}, u32[]{:S(2)}) copy-start(f32[1024,512]{1,0:T(8,128)} %get-tuple-element.63.refs_7_) | copy-start | bytes 6291460
  33.1 11.9 %copy-start = (bf16[512,512]{1,0:T(8,128)(2,1)S(1)}, bf16[512,512]{1,0:T(8,128)(2,1)}, u32[]{:S(2)}) copy-start(bf16[512,512]{1,0:T(8,128)(2,1)} %refs_1_.5) | copy-start | bytes 1572868
  33.2 11.9 %copy-start.1 = (f32[512]{0:T(512)S(1)}, f32[512]{0:T(512)}, u32[]{:S(2)}) copy-start(f32[512]{0:T(512)} %param.22) | copy-start | bytes 6148
  33.2 11.9 %copy-start.2 = (f32[256]{0:T(256)S(1)}, f32[256]{0:T(256)}, u32[]{:S(2)}) copy-start(f32[256]{0:T(256)} %param.18) | copy-start | bytes 3076
  33.2 11.9 %copy-start.5 = (f32[1024,512]{1,0:T(8,128)S(1)}, f32[1024,512]{1,0:T(8,128)}, u32[]{:S(2)}) copy-start(f32[1024,512]{1,0:T(8,128)} %get-tuple-element.62.refs_6_) | copy-start | bytes 6291460
  33.2 11.9 %copy-start.7 = (bf16[1024,512]{1,0:T(8,128)(2,1)S(1)}, bf16[1024,512]{1,0:T(8,128)(2,1)}, u32[]{:S(2)}) copy-start(bf16[1024,512]{1,0:T(8,128)(2,1)} %get-tuple-element.53.refs_4_.refs_5_) | copy-start | bytes 3145732
  33.2 11.9 %copy-start.9 = (f32[32,512]{1,0:T(8,128)S(1)}, f32[32,512]{1,0:T(8,128)}, u32[]{:S(2)}) copy-start(f32[32,512]{1,0:T(8,128)} %copy-done.8) | copy-start | bytes 196612
  33.2 11.9 %copy-start.10 = (f32[32,512]{1,0:T(8,128)S(1)}, f32[32,512]{1,0:T(8,128)}, u32[]{:S(2)}) copy-start(f32[32,512]{1,0:T(8,128)} %get-tuple-element.61.refs_1_) | copy-start | bytes 196612
  33.2 1.8 %collective-permute-start.5 = (f32[8,512]{1,0:T(8,128)S(1)}, f32[8,512]{1,0:T(8,128)S(1)}, u32[]{:S(2)}, u32[]{:S(2)}) collective-permute-start(f32[8,512]{1,0:T(8,128)S(1)} %maximum_maximum_fusion.1), channel_id=1, source_target_pairs={{0,1},{1,0},{2,3},{3,2},{4,5},{5,4},{6,7},{7,6},{8,9},{9,8},{10,11... | collective-permute-start | bytes 49160 | tf_op jit(solution)/shard_map/ppermute | solution.py:454
  33.5 9.2 %collective-permute-start.10 = (f32[1,128,1024]{2,1,0:T(8,128)S(1)}, f32[1,128,1024]{2,1,0:T(8,128)S(1)}, u32[]{:S(2)}, u32[]{:S(2)}) collective-permute-start(f32[1,128,1024]{2,1,0:T(8,128)S(1)} %constant_dynamic-slice_fusion.3), channel_id=1, source_target_pairs={{0,8},{1,17},{2,10},{3,19},{4,12},{5,21},{6,14},{7,23},{8,0},{9,25... | collective-permute-start | bytes 1572872 | tf_op jit(solution)/shard_map/ppermute | solution.py:489
  35.1 4.5 %collective-permute-start.8 = (f32[8,512]{1,0:T(8,128)S(1)}, f32[8,512]{1,0:T(8,128)S(1)}, u32[]{:S(2)}, u32[]{:S(2)}) collective-permute-start(f32[8,512]{1,0:T(8,128)S(1)} %maximum_maximum_fusion.2), channel_id=1, source_target_pairs={{0,2},{1,3},{2,0},{3,1},{4,6},{5,7},{6,4},{7,5},{8,10},{9,11},{10,... | collective-permute-start | bytes 49160 | tf_op jit(solution)/shard_map/ppermute | solution.py:454
  35.2 4.7 %collective-permute-start.7 = (f32[8,512]{1,0:T(8,128)S(1)}, f32[8,512]{1,0:T(8,128)S(1)}, u32[]{:S(2)}, u32[]{:S(2)}) collective-permute-start(f32[8,512]{1,0:T(8,128)S(1)} %maximum_maximum_fusion.2), channel_id=1, source_target_pairs={{0,4},{1,5},{2,6},{3,7},{4,0},{5,1},{6,2},{7,3},{8,12},{9,13},{10,... | collective-permute-start | bytes 49160 | tf_op jit(solution)/shard_map/ppermute | solution.py:454
  36.8 5.5 %collective-permute-start.6 = (f32[8,512]{1,0:T(8,128)S(1)}, f32[8,512]{1,0:T(8,128)S(1)}, u32[]{:S(2)}, u32[]{:S(2)}) collective-permute-start(f32[8,512]{1,0:T(8,128)S(1)} %maximum_maximum_fusion.2), channel_id=1, source_target_pairs={{0,6},{1,7},{2,4},{3,5},{4,2},{5,3},{6,0},{7,1},{8,14},{9,15},{10,... | collective-permute-start | bytes 49160 | tf_op jit(solution)/shard_map/ppermute | solution.py:454
  43.5 6.7 %collective-permute-start.12 = (f32[1,64,1024]{2,1,0:T(8,128)}, f32[1,64,1024]{2,1,0:T(8,128)}, u32[]{:S(2)}, u32[]{:S(2)}) collective-permute-start(f32[1,64,1024]{2,1,0:T(8,128)} %constant_dynamic-slice_fusion.2), channel_id=1, source_target_pairs={{0,16},{1,9},{2,18},{3,11},{4,20},{5,13},{6,22},{7,15},{8,24},{9,1... | collective-permute-start | bytes 786440 | tf_op jit(solution)/shard_map/ppermute | solution.py:489
  47.3 4.0 %collective-permute-start.11 = (f32[264,512]{1,0:T(8,128)S(1)}, f32[264,512]{1,0:T(8,128)S(1)}, u32[]{:S(2)}, u32[]{:S(2)}) collective-permute-start(f32[264,512]{1,0:T(8,128)S(1)} %get-tuple-element.73), channel_id=1, source_target_pairs={{0,1},{1,0},{2,3},{3,2},{4,5},{5,4},{6,7},{7,6},{8,9},{9,8},{10,11... | collective-permute-start | bytes 1622024 | tf_op jit(solution)/shard_map/ppermute | solution.py:431
  51.2 5.4 %collective-permute-start.23 = (f32[1,32,1024]{2,1,0:T(8,128)S(1)}, f32[1,32,1024]{2,1,0:T(8,128)S(1)}, u32[]{:S(2)}, u32[]{:S(2)}) collective-permute-start(f32[1,32,1024]{2,1,0:T(8,128)S(1)} %constant_dynamic-slice_fusion), channel_id=1, source_target_pairs={{0,2},{1,5},{2,0},{3,7},{4,6},{5,1},{6,4},{7,3},{8,10},{9,13},{10,... | collective-permute-start | bytes 393224 | tf_op jit(solution)/shard_map/ppermute | solution.py:489
  51.4 15.1 %collective-permute-start.13 = (f32[136,512]{1,0:T(8,128)S(1)}, f32[136,512]{1,0:T(8,128)S(1)}, u32[]{:S(2)}, u32[]{:S(2)}) collective-permute-start(f32[136,512]{1,0:T(8,128)S(1)} %get-tuple-element.75), channel_id=1, source_target_pairs={{0,8},{8,0},{16,24},{24,16},{1,9},{9,1},{17,25},{25,17},{2,10},{10... | collective-permute-start | bytes 835592 | tf_op jit(solution)/shard_map/ppermute | solution.py:550
  53.0 13.5 %collective-permute-start.14 = (f32[136,512]{1,0:T(8,128)S(1)}, f32[136,512]{1,0:T(8,128)S(1)}, u32[]{:S(2)}, u32[]{:S(2)}) collective-permute-start(f32[136,512]{1,0:T(8,128)S(1)} %get-tuple-element.76), channel_id=1, source_target_pairs={{0,16},{8,24},{16,0},{24,8},{1,17},{9,25},{17,1},{25,9},{2,18},{10... | collective-permute-start | bytes 835592 | tf_op jit(solution)/shard_map/ppermute | solution.py:550
  54.5 12.0 %collective-permute-start.15 = (f32[136,512]{1,0:T(8,128)S(1)}, f32[136,512]{1,0:T(8,128)S(1)}, u32[]{:S(2)}, u32[]{:S(2)}) collective-permute-start(f32[136,512]{1,0:T(8,128)S(1)} %get-tuple-element.77), channel_id=1, source_target_pairs={{0,24},{8,16},{16,8},{24,0},{1,25},{9,17},{17,9},{25,1},{2,26},{10... | collective-permute-start | bytes 835592 | tf_op jit(solution)/shard_map/ppermute | solution.py:550
  56.6 9.8 %collective-permute-start.24 = (f32[1,32,1024]{2,1,0:T(8,128)S(1)}, f32[1,32,1024]{2,1,0:T(8,128)S(1)}, u32[]{:S(2)}, u32[]{:S(2)}) collective-permute-start(f32[1,32,1024]{2,1,0:T(8,128)S(1)} %dynamic-slice_add_fusion.2), channel_id=1, source_target_pairs={{0,4},{1,3},{2,6},{3,1},{4,0},{5,7},{6,2},{7,5},{8,12},{9,11},{10,... | collective-permute-start | bytes 393224 | tf_op jit(solution)/shard_map/ppermute | solution.py:489
  66.4 5.0 %collective-permute-start.25 = (f32[1,32,1024]{2,1,0:T(8,128)S(1)}, f32[1,32,1024]{2,1,0:T(8,128)S(1)}, u32[]{:S(2)}, u32[]{:S(2)}) collective-permute-start(f32[1,32,1024]{2,1,0:T(8,128)S(1)} %add.293), channel_id=1, source_target_pairs={{0,2},{1,5},{2,0},{3,7},{4,6},{5,1},{6,4},{7,3},{8,10},{9,13},{10,... | collective-permute-start | bytes 393224 | tf_op jit(solution)/shard_map/ppermute | solution.py:489
  66.7 7.0 %collective-permute-start.16 = (f32[72,512]{1,0:T(8,128)S(1)}, f32[72,512]{1,0:T(8,128)S(1)}, u32[]{:S(2)}, u32[]{:S(2)}) collective-permute-start(f32[72,512]{1,0:T(8,128)S(1)} %pad_maximum_fusion.1), channel_id=1, source_target_pairs={{0,2},{1,5},{2,0},{3,7},{4,6},{5,1},{6,4},{7,3},{8,10},{9,13},{10,... | collective-permute-start | bytes 442376 | tf_op jit(solution)/shard_map/ppermute | solution.py:489
  71.5 8.0 %collective-permute-start.26 = (f32[1,64,1024]{2,1,0:T(8,128)S(1)}, f32[1,64,1024]{2,1,0:T(8,128)S(1)}, u32[]{:S(2)}, u32[]{:S(2)}) collective-permute-start(f32[1,64,1024]{2,1,0:T(8,128)S(1)} %maximum_select_fusion.9), channel_id=1, source_target_pairs={{0,16},{1,9},{2,18},{3,11},{4,20},{5,13},{6,22},{7,15},{8,24},{9,1... | collective-permute-start | bytes 786440 | tf_op jit(solution)/shard_map/ppermute | solution.py:489
  73.7 8.6 %collective-permute-start.17 = (f32[72,512]{1,0:T(8,128)S(1)}, f32[72,512]{1,0:T(8,128)S(1)}, u32[]{:S(2)}, u32[]{:S(2)}) collective-permute-start(f32[72,512]{1,0:T(8,128)S(1)} %pad_maximum_fusion.2), channel_id=1, source_target_pairs={{0,4},{1,3},{2,6},{3,1},{4,0},{5,7},{6,2},{7,5},{8,12},{9,11},{10,... | collective-permute-start | bytes 442376 | tf_op jit(solution)/shard_map/ppermute | solution.py:489
  79.5 12.5 %collective-permute-start.27 = (f32[1,128,1024]{2,1,0:T(8,128)S(1)}, f32[1,128,1024]{2,1,0:T(8,128)S(1)}, u32[]{:S(2)}, u32[]{:S(2)}) collective-permute-start(f32[1,128,1024]{2,1,0:T(8,128)S(1)} %maximum_select_fusion.6), channel_id=1, source_target_pairs={{0,8},{1,17},{2,10},{3,19},{4,12},{5,21},{6,14},{7,23},{8,0},{9,25... | collective-permute-start | bytes 1572872 | tf_op jit(solution)/shard_map/ppermute | solution.py:489
  82.4 1.2 %collective-permute-start.22 = (f32[8,512]{1,0:T(8,128)S(1)}, f32[8,512]{1,0:T(8,128)S(1)}, u32[]{:S(2)}, u32[]{:S(2)}) collective-permute-start(f32[8,512]{1,0:T(8,128)S(1)} %slice_add_fusion.1), channel_id=1, source_target_pairs={{0,1},{1,0},{2,3},{3,2},{4,5},{5,4},{6,7},{7,6},{8,9},{9,8},{10,11... | collective-permute-start | bytes 49160 | tf_op jit(solution)/shard_map/ppermute | solution.py:431
  82.6 5.9 %collective-permute-start.18 = (f32[2,32,512]{2,1,0:T(8,128)S(1)}, f32[2,32,512]{2,1,0:T(8,128)S(1)}, u32[]{:S(2)}, u32[]{:S(2)}) collective-permute-start(f32[2,32,512]{2,1,0:T(8,128)S(1)} %add.290), channel_id=1, source_target_pairs={{0,2},{1,5},{2,0},{3,7},{4,6},{5,1},{6,4},{7,3},{8,10},{9,13},{10,... | collective-permute-start | bytes 393224 | tf_op jit(solution)/shard_map/ppermute | solution.py:489
  88.5 15.1 %collective-permute-start.21 = (f32[2,64,512]{2,1,0:T(8,128)S(1)}, f32[2,64,512]{2,1,0:T(8,128)S(1)}, u32[]{:S(2)}, u32[]{:S(2)}) collective-permute-start(f32[2,64,512]{2,1,0:T(8,128)S(1)} %maximum_select_fusion.7.refs_8_), channel_id=1, source_target_pairs={{0,24},{8,16},{16,8},{24,0},{1,25},{9,17},{17,9},{25,1},{2,26},{10... | collective-permute-start | bytes 786440 | tf_op jit(solution)/shard_map/ppermute | solution.py:550
  89.6 14.3 %collective-permute-start.20 = (f32[2,64,512]{2,1,0:T(8,128)S(1)}, f32[2,64,512]{2,1,0:T(8,128)S(1)}, u32[]{:S(2)}, u32[]{:S(2)}) collective-permute-start(f32[2,64,512]{2,1,0:T(8,128)S(1)} %maximum_select_fusion.7.refs_8_), channel_id=1, source_target_pairs={{0,16},{8,24},{16,0},{24,8},{1,17},{9,25},{17,1},{25,9},{2,18},{10... | collective-permute-start | bytes 786440 | tf_op jit(solution)/shard_map/ppermute | solution.py:550
  90.5 13.0 %collective-permute-start.19 = (f32[2,64,512]{2,1,0:T(8,128)S(1)}, f32[2,64,512]{2,1,0:T(8,128)S(1)}, u32[]{:S(2)}, u32[]{:S(2)}) collective-permute-start(f32[2,64,512]{2,1,0:T(8,128)S(1)} %maximum_select_fusion.7.refs_8_), channel_id=1, source_target_pairs={{0,8},{8,0},{16,24},{24,16},{1,9},{9,1},{17,25},{25,17},{2,10},{10... | collective-permute-start | bytes 786440 | tf_op jit(solution)/shard_map/ppermute | solution.py:550
  92.1 0.7 copy-start.4
  92.2 12.3 %collective-permute-start.29 = (f32[256,1024]{1,0:T(8,128)S(1)}, f32[256,1024]{1,0:T(8,128)S(1)}, u32[]{:S(2)}, u32[]{:S(2)}) collective-permute-start(f32[256,1024]{1,0:T(8,128)S(1)} %maximum_select_fusion.2.refs_0_), channel_id=1, source_target_pairs={{0,1},{1,0},{2,3},{3,2},{4,5},{5,4},{6,7},{7,6},{8,9},{9,8},{10,11... | collective-permute-start | bytes 3145736 | tf_op jit(solution)/shard_map/ppermute | solution.py:431
  104.1 1.2 %copy-start.3 = (bf16[4,256,512]{2,1,0:T(8,128)(2,1)S(1)}, bf16[4,256,512]{2,1,0:T(8,128)(2,1)}, u32[]{:S(2)}) copy-start(bf16[4,256,512]{2,1,0:T(8,128)(2,1)} %get-tuple-element.86.refs_2_) | copy-start | bytes 3145732
  104.3 2.7 %collective-permute-start.28 = (f32[256,1024]{1,0:T(8,128)S(1)}, f32[256,1024]{1,0:T(8,128)S(1)}, u32[]{:S(2)}, u32[]{:S(2)}) collective-permute-start(f32[256,1024]{1,0:T(8,128)S(1)} %pad_maximum_fusion.refs_0_), channel_id=1, source_target_pairs={{0,1},{1,0},{2,3},{3,2},{4,5},{5,4},{6,7},{7,6},{8,9},{9,8},{10,11... | collective-permute-start | bytes 3145736 | tf_op jit(solution)/shard_map/ppermute | solution.py:431

commit v2 on v1

--- a/solution.py
+++ b/solution.py
@@ -9,7 +9,6 @@
 
 EPS = 1e-05
 CHUNKS = 8
-LANE = 128
 GELU_A = 0.044715
 GELU_K = 0.7978845608028654
 F32 = jnp.float32
@@ -312,11 +311,13 @@
 
 
 def states_kernel(
-    c_go_hbm, carry_ref, b_ref, gamma_ref, d_ref, normed_ref, h_ref, adj_ref, leave_ref, pow_ref, keep_ref, g_d_ref,
+    c_go_hbm, h_hbm, adj_hbm, normed_hbm, carry_ref, b_ref, gamma_ref, d_ref, leave_ref, pow_ref, keep_ref, g_d_ref,
     c_got_ref,
-    low_hbm, go_ref, send_ref, c_ref, low_ref, after_ref, small_ref, sems,
+    low_hbm, go_ref, send_ref, c_ref, h_ref, adj_ref, normed_ref, low_ref, after_ref, small_ref, sems,
 ):
     copies = Copies(sems)
+    h_here = copies.lanes(leave_ref.shape[0], (adj_hbm, adj_ref), (h_hbm, h_ref))
+    normed_here = copies.start(normed_hbm, normed_ref)
     c_here = copies.start(c_go_hbm, c_ref)
     leaving = []
     lanes = leave_ref.shape[0]
@@ -328,6 +329,7 @@
     for lane in range(lanes):
         first = lane * seg
         state = cload(leave_ref, lane)
+        wait(h_here[lane])
         cstore(after_ref, CHUNKS - 1, state)
         for chunk in reversed(range(1, CHUNKS)):
             state = fma(back, state, cload(adj_ref, first + chunk))
@@ -344,6 +346,7 @@
             before = cload(h_ref, at, CHUNKS)
         rows = pl.ds(first, seg)
         leaving.append(copies.start(low_ref.at[rows], low_hbm.at[rows]))
+    normed_here.wait()
     grad_b = dot_tn(normed_ref[...], low_ref[...])
     n = gamma_ref.shape[1]
     prod = grad_b * b_ref[...].astype(F32)
@@ -360,22 +363,37 @@
     wait(leaving)
 
 
-def pieces_kernel(c_ref, b_keep_ref, b_got_ref, own_ref, small_ref, *send_refs):
-    count, n = len(send_refs) + 1, c_ref.shape[0]
-    rows = n // count
+def put_pieces(get, own_ref, send_refs):
+    rows = own_ref.shape[0]
     mine = lax.axis_index("dp")
-    small = b_keep_ref[n:, :] + b_got_ref[n:, :]
+    for mask, ref in enumerate((own_ref, *send_refs)):
+        ref[:rows, :] = get(pl.ds(pl.multiple_of((mine ^ mask) * rows, rows), rows))
+
+
+def c_pieces_kernel(c_ref, own_ref, *send_refs):
+    put_pieces(lambda at: c_ref[at, :], own_ref, send_refs)
+
+
+def b_pieces_kernel(keep_ref, got_ref, small_ref, own_ref, *send_refs):
+    n = own_ref.shape[0] * (len(send_refs) + 1)
+    small = keep_ref[n:, :] + got_ref[n:, :]
     small_ref[...] = small
-    for mask in range(count):
-        start = pl.multiple_of((mine ^ mask) * rows, rows)
-        at = pl.ds(start, rows)
-        c = c_ref[at, :]
-        b = b_keep_ref[at, :] + b_got_ref[at, :]
-        if mask == 0:
-            own_ref[0], own_ref[1] = c, b
-        else:
-            ref = send_refs[mask - 1]
-            ref[:rows, :], ref[rows : 2 * rows, :], ref[2 * rows :, :] = c, b, small
+    put_pieces(lambda at: keep_ref[at, :] + got_ref[at, :], own_ref, send_refs)
+    for ref in send_refs:
+        ref[own_ref.shape[0] :, :] = small
+
+
+def split_kernel(phase, keep_ref, got_ref, own_ref, send_ref):
+    rows = own_ref.shape[0]
+    mine = my_bit(phase)
+    if rows % 8:
+        total = keep_ref[...] + got_ref[...]
+        own_ref[...] = jnp.where(mine == 0, total[:rows], total[rows:])
+        send_ref[...] = jnp.where(mine == 0, total[rows:], total[:rows])
+        return
+    for ref, which in ((own_ref, mine), (send_ref, 1 - mine)):
+        at = pl.ds(pl.multiple_of(which * rows, rows), rows)
+        ref[...] = keep_ref[at, :] + got_ref[at, :]
 
 
 def input_kernel(
@@ -476,12 +494,16 @@
     return [(axis, bit) for bit in range(first, lax.axis_size(axis).bit_length() - 1)]
 
 
-def phases():
-    return [bits("dp") + bits("seq", 1), bits("dp")[::-1] + bits("seq", 1)[::-1]]
+def phases(first=False):
+    dp, far = bits("dp"), bits("seq", 1)
+    if first:
+        return [dp + far, dp[::-1] + far]
+    return [dp + far, dp[::-1] + far]
 
 
 def hop(value, phase):
-    orders, count = phases(), lax.axis_size("seq")
+    orders, count = phases(phase < 0), lax.axis_size("seq")
+    phase = phase if phase >= 0 else -1 - phase
     pairs = []
     for device in range(lax.axis_size("dp") * count):
         axis, bit = orders[device % 2][phase]
@@ -490,7 +512,8 @@
 
 
 def my_bit(phase):
-    one, two = (lax.axis_index(axis) // (1 << bit) % 2 for axis, bit in (o[phase] for o in phases()))
+    place = phase if phase >= 0 else -1 - phase
+    one, two = (lax.axis_index(axis) // (1 << bit) % 2 for axis, bit in (o[place] for o in phases(phase < 0)))
     return jnp.where(lax.axis_index("seq") % 2 == 0, one, two)
 
 
@@ -556,7 +579,7 @@
         got, more = unpack(across(send, mask + 1), own, extra)
         parts.append(got)
         extras.append(more)
-    return tree_sum(parts), tree_sum(extras)
+    return tree_sum(parts), None if extra is None else tree_sum(extras)
 
 
 def gather_dp(value):
@@ -565,6 +588,10 @@
     for mask in reversed(range(1, count)):
         parts.insert(1, across(value, mask))
     return join_rows(parts, mine)
+
+
+def only(step):
+    return lambda value, extra=None: (step(value), extra)
 
 
 def tie(*values):
@@ -674,16 +701,31 @@
     )
     near, last = len(bits("dp")), len(phases()[0]) - 1
     c_got = swap(c_send, "seq", 0)
-    w = (w_keep + swap(w_send, "seq", 0))[None]
-    leave, w = entering(back_pair, True, w)
-    w, _ = scatter(w, 0)
+
+    def split(keep, got, phase):
+        half = ((keep.shape[0] // 2, keep.shape[1]), F32)
+        return call(
+            functools.partial(split_kernel, phase), "split_sum", 0.5, [half, half], [], [keep, got], pin=True
+        )
+
+    own, send = split(w_keep, swap(w_send, "seq", 0), -1)
+    leave, own = entering(back_pair, True, own)
+    owns = [own]
+    for phase in range(1, last):
+        own, send = split(own, hop(send, -phase), -1 - phase)
+        owns.append(own)
+    w = (own + hop(send, -last))[None]
+    w_steps = [functools.partial(double, phase=-1 - last)]
+    w_steps += [only(functools.partial(gather, phase=-1 - p)) for p in reversed(range(last))]
+    for step in w_steps:
+        w, _ = step(w)
 
     back_low, b_keep, b_send, c = call(
         states_kernel, "adjoint_states", 3,
         [low_rows, ((n + 8, two), F32), ((n + 8, two), F32), half_rows],
-        [c_keep], [carry, b_proj, gamma, skip, normed, h, adj, leave, powers, keep, grad_d, c_got], fetched=(),
-        scratch=[low_rows, ((CHUNKS, two), F32), ((16, two), F32)],
-        sems=lanes + 1, far_outs=1, limit=8, wait_for=[w],
+        [c_keep, h, adj, normed], [carry, b_proj, gamma, skip, leave, powers, keep, grad_d, c_got], fetched=(),
+        scratch=[full_rows, full_rows, low_rows, low_rows, ((CHUNKS, two), F32), ((16, two), F32)],
+        sems=3 * lanes + 2, far_outs=1, limit=14, wait_for=[owns[1]],
     )
 
     def back_input(back_low):
@@ -693,34 +735,24 @@
             scratch=[lane_rows, lane_rows], sems=7 * lanes + 3, far_outs=2, limit=12,
         )
 
-    for phase in range(1, near):
-        w, _ = scatter(w, phase)
     groups = lax.axis_size("dp")
     cut = n // groups
-    own, small, *sends = call(
-        pieces_kernel, "pieces", 1,
-        [((2, cut, width), F32), ((8, two), F32)] + [((2 * cut + 8, width), F32)] * (groups - 1),
-        [], [c, b_keep, swap(b_send, "seq", 0)], wait_for=[w] if True else [],
-    )
-    cb, small = sum_dp(own, sends, small)
-
-    def only(step):
-        return lambda value, extra=None: (step(value), extra)
+    piece_rows = ((cut, width), F32)
+    c_own, *c_sends = call(c_pieces_kernel, "c_pieces", 0.5, [piece_rows] * groups, [], [c])
+    c, _ = sum_dp(c_own[None], [v[None] for v in c_sends], None)
+    small, b_own, *b_sends = call(
+        b_pieces_kernel, "b_pieces", 0.5,
+        [((8, two), F32), piece_rows] + [((cut + 8, width), F32)] * (groups - 1),
+        [], [b_keep, swap(b_send, "seq", 0)], wait_for=[owns[2]],
+    )
+    b, small = sum_dp(b_own[None], b_sends, small)
+    cb = jnp.concatenate([c, b], 0)
 
     steps = [functools.partial(scatter, phase=p) for p in range(near, last)]
     steps += [functools.partial(double, phase=last)]
     steps += [only(functools.partial(gather, phase=p)) for p in reversed(range(near, last))]
-    ahead = steps + [only(functools.partial(gather, phase=p)) for p in reversed(range(near))]
-    lead = 1
-    for turn in range(lead):
-        w, _ = ahead[turn](w)
-    for turn, step in enumerate(steps):
-        if turn + lead < len(ahead):
-            w_next, _ = ahead[turn + lead](w)
+    for step in steps:
         cb, small = step(cb, extra=small)
-        w = w_next
-    for turn in range(len(steps) + lead, len(ahead)):
-        w, _ = ahead[turn](w)
     got = swap(small, "seq", 0)
     small = join_rows([small[None], got[None]], lax.axis_index("seq") % 2)[0]
     finished = call(
@@ -728,6 +760,7 @@
         [nu, theta, gain], [small, powers], sems=3,
     )
     grad_in, block_out = back_input(back_low)
+    cb, w = tie(cb, w)
     cb = gather_dp(cb)
     cb, grad_in, block_out = tie(cb, grad_in, block_out)
     w, cb = w[0], jnp.concatenate([cb[0], cb[1]], 1)

time: 109 us -> 104 us (0.954)
  waiting for transfers between devices: 38.1 us -> 34.2 us
  other arithmetic: 3.73 us -> 1.12 us
  Pallas kernels: 30 us -> 31.8 us
  starting transfers between devices: 32.6 us -> 33.8 us
  local copies, waits for them, and re-layouts: 2.26 us -> 1.08 us
    ppermute x10, waiting for transfers between devices: 23 us -> 14.9 us  [hop(): return lax.ppermute(value, ('dp', 'seq'), pairs)]
    ppermute x6 -> x9, waiting for transfers between devices: 5.47 us -> 9.57 us  [across(): lax.ppermute(value, 'dp', [(i, i ^ mask) for i in range(lax.axis_size('dp...]
    ppermute x6 -> x9, starting transfers between devices: 7.11 us -> 10.1 us  [across(): lax.ppermute(value, 'dp', [(i, i ^ mask) for i in range(lax.axis_size('dp...]
    pallas_call x9 -> x13, Pallas kernels: 30 us -> 31.8 us  [call(): pl.pallas_call(body, in_specs=[hbm] * len(far) + [vmem] * len(near) + [pl...]
    ppermute x10, starting transfers between devices: 14 us -> 12.4 us  [hop(): return lax.ppermute(value, ('dp', 'seq'), pairs)]
    broadcast_in_dim x1, other arithmetic: 1.51 us -> 0.02 us  [on_device(): w = (own + hop(send, -last))[None]]
  transfers between devices with their start and end apart: 30 -> 33, of which waited for: 17 -> 22; matrix products, arithmetic and copies ran while one was open for 4% -> 1% of each run, Pallas kernels for 12% -> 15%
where the time goes in v2:
time: 104 us
  waiting for transfers between devices  34.2 us (33%)
  starting transfers between devices  33.8 us (32%)
  Pallas kernels  31.8 us (31%)
  between operations  1.51 us (1%)
  other arithmetic  1.12 us (1%)
  local copies, waits for them, and re-layouts  1.08 us (1%)
    pallas_call x13, Pallas kernels, call(): pl.pallas_call(body, in_specs=[hbm] * len(far) + [vmem] * len(near) + [pl...  31.8 us
    ppermute x10, waiting for transfers between devices, hop(): return lax.ppermute(value, ('dp', 'seq'), pairs)  14.9 us
    ppermute x10, starting transfers between devices, hop(): return lax.ppermute(value, ('dp', 'seq'), pairs)  12.4 us
    ppermute x8, starting transfers between devices, entering(): lax.ppermute(pair, 'seq', [(i, i ^ mask << bit) for i in range(count)])  10.7 us
    ppermute x9, starting transfers between devices, across(): lax.ppermute(value, 'dp', [(i, i ^ mask) for i in range(lax.axis_size('dp...  10.1 us
    ppermute x9, waiting for transfers between devices, across(): lax.ppermute(value, 'dp', [(i, i ^ mask) for i in range(lax.axis_size('dp...  9.57 us
    ppermute x8, waiting for transfers between devices, entering(): lax.ppermute(pair, 'seq', [(i, i ^ mask << bit) for i in range(count)])  6.38 us
    ppermute x6, waiting for transfers between devices, swap(): return lax.ppermute(value, axis, [(i, i ^ 1 << bit) for i in range(count)])  3.33 us
  transfers between devices with their start and end apart: 33, of which 22 were waited for; matrix products, arithmetic and copies ran while one was open for 1% of the time, Pallas kernels for 15%

profile of v2, /device:TPU:0, one launch (start us, length us, event | category | flops | bytes accessed | tf_op | source)
XLA Modules:
  0.0 103.5 jit_solution(8129470719733332118)
XLA Ops:
  0.7 5.0 %forward_local.1 = (bf16[1024,512]{1,0:T(8,128)(2,1)}, bf16[1024,512]{1,0:T(8,128)(2,1)}, f32[1024,512]{1,0:T(8,128)}, f32[8,512]{1,0:T(8,128)S(1)}, f32[32,512]{1,0:T(8,128)S(1)}, /*index=5*/f32[32,512]{1,0:T(8,128)S(1)}) custom-call(s32[4,16]{1,0:T(4,128)} %bitcast.64, s32[1,4]{1,0:T(1,128)} %refs_1_.3, bf16[4,256,512]{2,1,0:T(8,128)(2,1)} %bitcast.62, ...), custom_call_target="tpu_custom_call" | custom-call | flops 4400000000 | bytes 12000000 | tf_op jit(solution)/shard_map/forward_local/pallas_call | solution.py:651
  5.6 0.5 collective-permute-start
  6.1 0.8 collective-permute-done
  7.0 3.0 %collective-permute-start.3 = (f32[8,512]{1,0:T(8,128)S(1)}, f32[8,512]{1,0:T(8,128)S(1)}, u32[]{:S(2)}, u32[]{:S(2)}) collective-permute-start(f32[8,512]{1,0:T(8,128)S(1)} %maximum_maximum_fusion), channel_id=1, source_target_pairs={{0,2},{1,3},{2,0},{3,1},{4,6},{5,7},{6,4},{7,5},{8,10},{9,11},{10,... | collective-permute-start | bytes 49160 | tf_op jit(solution)/shard_map/ppermute | solution.py:472
  10.0 2.6 %collective-permute-start.2 = (f32[8,512]{1,0:T(8,128)S(1)}, f32[8,512]{1,0:T(8,128)S(1)}, u32[]{:S(2)}, u32[]{:S(2)}) collective-permute-start(f32[8,512]{1,0:T(8,128)S(1)} %maximum_maximum_fusion), channel_id=1, source_target_pairs={{0,4},{1,5},{2,6},{3,7},{4,0},{5,1},{6,2},{7,3},{8,12},{9,13},{10,... | collective-permute-start | bytes 49160 | tf_op jit(solution)/shard_map/ppermute | solution.py:472
  12.6 2.7 %cotangent_order.1.refs_6_.refs_4_ = bf16[1024,512]{1,0:T(8,128)(2,1)} custom-call(bf16[4,256,512]{2,1,0:T(8,128)(2,1)} %bitcast.63), custom_call_target="tpu_custom_call" | custom-call | flops 2200000000 | bytes 6000000 | tf_op jit(solution)/shard_map/cotangent_order/pallas_call | solution.py:651
  15.4 2.8 %collective-permute-done.1 = f32[8,512]{1,0:T(8,128)S(1)} collective-permute-done((f32[8,512]{1,0:T(8,128)S(1)}, f32[8,512]{1,0:T(8,128)S(1)}, u32[]{:S(2)}, u32[]{:S(2)}) %collective-permute-start.1) | collective-permute-done | bytes 16416 | tf_op jit(solution)/shard_map/ppermute | solution.py:472
  18.3 10.4 %block.1 = (bf16[1024,512]{1,0:T(8,128)(2,1)}, f32[1024,512]{1,0:T(8,128)}, f32[1024,512]{1,0:T(8,128)}, f32[1024,512]{1,0:T(8,128)}, f32[32,512]{1,0:T(8,128)},...) custom-call(bf16[512,1024]{1,0:T(8,128)(2,1)} %refs_0_.1, ...), custom_call_target="tpu_custom_call" | custom-call | flops 11000000512 | bytes 30000000 | tf_op jit(solution)/shard_map/block/pallas_call | solution.py:651
  28.8 2.6 %collective-permute-done.4.refs_1_ = f32[256,1024]{1,0:T(8,128)S(1)} collective-permute-done((f32[256,1024]{1,0:T(8,128)S(1)}, f32[256,1024]{1,0:T(8,128)S(1)}, u32[]{:S(2)}, u32[]{:S(2)}) %collective-permute-start.4) | collective-permute-done | bytes 1048608 | tf_op jit(solution)/shard_map/ppermute | solution.py:449
  32.2 1.5 %collective-permute-start.10 = (f32[128,1024]{1,0:T(8,128)S(1)}, f32[128,1024]{1,0:T(8,128)S(1)}, u32[]{:S(2)}, u32[]{:S(2)}) collective-permute-start(f32[128,1024]{1,0:T(8,128)S(1)} %get-tuple-element.84), channel_id=1, source_target_pairs={{0,8},{1,17},{2,10},{3,19},{4,12},{5,21},{6,14},{7,23},{8,0},{9,25... | collective-permute-start | bytes 1572872 | tf_op jit(solution)/shard_map/ppermute | solution.py:511
  33.8 1.6 %collective-permute-start.7 = (f32[8,512]{1,0:T(8,128)S(1)}, f32[8,512]{1,0:T(8,128)S(1)}, u32[]{:S(2)}, u32[]{:S(2)}) collective-permute-start(f32[8,512]{1,0:T(8,128)S(1)} %maximum_maximum_fusion.2), channel_id=1, source_target_pairs={{0,4},{1,5},{2,6},{3,7},{4,0},{5,1},{6,2},{7,3},{8,12},{9,13},{10,... | collective-permute-start | bytes 49160 | tf_op jit(solution)/shard_map/ppermute | solution.py:472
  35.4 2.8 %collective-permute-start.6 = (f32[8,512]{1,0:T(8,128)S(1)}, f32[8,512]{1,0:T(8,128)S(1)}, u32[]{:S(2)}, u32[]{:S(2)}) collective-permute-start(f32[8,512]{1,0:T(8,128)S(1)} %maximum_maximum_fusion.2), channel_id=1, source_target_pairs={{0,6},{1,7},{2,4},{3,5},{4,2},{5,3},{6,0},{7,1},{8,14},{9,15},{10,... | collective-permute-start | bytes 49160 | tf_op jit(solution)/shard_map/ppermute | solution.py:472
  38.2 0.5 collective-permute-done.7
  38.7 2.2 %collective-permute-done.6 = f32[8,512]{1,0:T(8,128)S(1)} collective-permute-done((f32[8,512]{1,0:T(8,128)S(1)}, f32[8,512]{1,0:T(8,128)S(1)}, u32[]{:S(2)}, u32[]{:S(2)}) %collective-permute-start.6) | collective-permute-done | bytes 16416 | tf_op jit(solution)/shard_map/ppermute | solution.py:472
  41.4 1.6 %collective-permute-start.15 = (f32[64,1024]{1,0:T(8,128)S(1)}, f32[64,1024]{1,0:T(8,128)S(1)}, u32[]{:S(2)}, u32[]{:S(2)}) collective-permute-start(f32[64,1024]{1,0:T(8,128)S(1)} %get-tuple-element.93), channel_id=1, source_target_pairs={{0,16},{1,9},{2,18},{3,11},{4,20},{5,13},{6,22},{7,15},{8,24},{9,1... | collective-permute-start | bytes 786440 | tf_op jit(solution)/shard_map/ppermute | solution.py:511
  43.1 3.8 %adjoint_states.1 = (bf16[1024,512]{1,0:T(8,128)(2,1)}, f32[264,512]{1,0:T(8,128)S(1)}, f32[264,512]{1,0:T(8,128)S(1)}, f32[256,512]{1,0:T(8,128)S(1)}) custom-call(f32[256,512]{1,0:T(8,128)} %get-tuple-element.72.refs_0_, f32[1024,512]{1,0:T(8,128)} %get-tuple-element.73.refs_1_, f32[1024,512]{1,0:T(8,128)} %get-tuple-element.74.refs_2_, ...), custom_call_target="tpu_custom_call" | custom-call | flops 3300000000 | bytes 9000000 | tf_op jit(solution)/shard_map/adjoint_states/pallas_call | solution.py:651
  46.9 0.9 collective-permute-done.15.refs_1_
  48.1 1.6 %collective-permute-start.11 = (f32[1,64,512]{2,1,0:T(8,128)S(1)}, f32[1,64,512]{2,1,0:T(8,128)S(1)}, u32[]{:S(2)}, u32[]{:S(2)}) collective-permute-start(f32[1,64,512]{2,1,0:T(8,128)S(1)} %bitcast.45), channel_id=1, source_target_pairs={{0,8},{8,0},{16,24},{24,16},{1,9},{9,1},{17,25},{25,17},{2,10},{10... | collective-permute-start | bytes 393224 | tf_op jit(solution)/shard_map/ppermute | solution.py:573
  49.7 1.5 %collective-permute-start.12 = (f32[1,64,512]{2,1,0:T(8,128)S(1)}, f32[1,64,512]{2,1,0:T(8,128)S(1)}, u32[]{:S(2)}, u32[]{:S(2)}) collective-permute-start(f32[1,64,512]{2,1,0:T(8,128)S(1)} %bitcast.44), channel_id=1, source_target_pairs={{0,16},{8,24},{16,0},{24,8},{1,17},{9,25},{17,1},{25,9},{2,18},{10... | collective-permute-start | bytes 393224 | tf_op jit(solution)/shard_map/ppermute | solution.py:573
  51.2 0.5 collective-permute-start.13
  51.7 1.3 %collective-permute-done.22 = f32[32,1024]{1,0:T(8,128)S(1)} collective-permute-done((f32[32,1024]{1,0:T(8,128)S(1)}, f32[32,1024]{1,0:T(8,128)S(1)}, u32[]{:S(2)}, u32[]{:S(2)}) %collective-permute-start.22) | collective-permute-done | bytes 131104 | tf_op jit(solution)/shard_map/ppermute | solution.py:511
  53.0 1.9 %collective-permute-start.23 = (f32[1,32,1024]{2,1,0:T(8,128)S(1)}, f32[1,32,1024]{2,1,0:T(8,128)S(1)}, u32[]{:S(2)}, u32[]{:S(2)}) collective-permute-start(f32[1,32,1024]{2,1,0:T(8,128)S(1)} %add_bitcast_fusion), channel_id=1, source_target_pairs={{0,4},{1,5},{2,6},{3,7},{4,0},{5,1},{6,2},{7,3},{8,12},{9,13},{10,... | collective-permute-start | bytes 393224 | tf_op jit(solution)/shard_map/ppermute | solution.py:511
  54.9 0.7 collective-permute-start.16
  55.6 1.5 %collective-permute-start.17 = (f32[72,512]{1,0:T(8,128)S(1)}, f32[72,512]{1,0:T(8,128)S(1)}, u32[]{:S(2)}, u32[]{:S(2)}) collective-permute-start(f32[72,512]{1,0:T(8,128)S(1)} %get-tuple-element.97), channel_id=1, source_target_pairs={{0,16},{8,24},{16,0},{24,8},{1,17},{9,25},{17,1},{25,9},{2,18},{10... | collective-permute-start | bytes 442376 | tf_op jit(solution)/shard_map/ppermute | solution.py:573
  57.2 1.1 %collective-permute-done.12 = f32[1,64,512]{2,1,0:T(8,128)S(1)} collective-permute-done((f32[1,64,512]{2,1,0:T(8,128)S(1)}, f32[1,64,512]{2,1,0:T(8,128)S(1)}, u32[]{:S(2)}, u32[]{:S(2)}) %collective-permute-start.12) | collective-permute-done | bytes 131104 | tf_op jit(solution)/shard_map/ppermute | solution.py:573
  58.5 2.0 %collective-permute-done.23 = f32[1,32,1024]{2,1,0:T(8,128)S(1)} collective-permute-done((f32[1,32,1024]{2,1,0:T(8,128)S(1)}, f32[1,32,1024]{2,1,0:T(8,128)S(1)}, u32[]{:S(2)}, u32[]{:S(2)}) %collective-permute-start.23) | collective-permute-done | bytes 131104 | tf_op jit(solution)/shard_map/ppermute | solution.py:511
  60.9 1.2 %collective-permute-done.17 = f32[72,512]{1,0:T(8,128)S(1)} collective-permute-done((f32[72,512]{1,0:T(8,128)S(1)}, f32[72,512]{1,0:T(8,128)S(1)}, u32[]{:S(2)}, u32[]{:S(2)}) %collective-permute-start.17) | collective-permute-done | bytes 147488 | tf_op jit(solution)/shard_map/ppermute | solution.py:573
  62.1 2.2 %collective-permute-done.18 = f32[72,512]{1,0:T(8,128)S(1)} collective-permute-done((f32[72,512]{1,0:T(8,128)S(1)}, f32[72,512]{1,0:T(8,128)S(1)}, u32[]{:S(2)}, u32[]{:S(2)}) %collective-permute-start.18) | collective-permute-done | bytes 147488 | tf_op jit(solution)/shard_map/ppermute | solution.py:573
  64.4 0.9 collective-permute-start.19
  65.3 1.2 %collective-permute-done.24 = f32[1,32,1024]{2,1,0:T(8,128)S(1)} collective-permute-done((f32[1,32,1024]{2,1,0:T(8,128)S(1)}, f32[1,32,1024]{2,1,0:T(8,128)S(1)}, u32[]{:S(2)}, u32[]{:S(2)}) %collective-permute-start.24) | collective-permute-done | bytes 131104 | tf_op jit(solution)/shard_map/ppermute | solution.py:511
  66.5 1.9 %collective-permute-start.25 = (f32[1,64,1024]{2,1,0:T(8,128)S(1)}, f32[1,64,1024]{2,1,0:T(8,128)S(1)}, u32[]{:S(2)}, u32[]{:S(2)}) collective-permute-start(f32[1,64,1024]{2,1,0:T(8,128)S(1)} %maximum_select_fusion.8), channel_id=1, source_target_pairs={{0,16},{1,9},{2,18},{3,11},{4,20},{5,13},{6,22},{7,15},{8,24},{9,1... | collective-permute-start | bytes 786440 | tf_op jit(solution)/shard_map/ppermute | solution.py:511
  68.5 1.2 %collective-permute-done.19 = f32[72,512]{1,0:T(8,128)S(1)} collective-permute-done((f32[72,512]{1,0:T(8,128)S(1)}, f32[72,512]{1,0:T(8,128)S(1)}, u32[]{:S(2)}, u32[]{:S(2)}) %collective-permute-start.19) | collective-permute-done | bytes 147488 | tf_op jit(solution)/shard_map/ppermute | solution.py:511
  69.7 2.8 %collective-permute-start.20 = (f32[72,512]{1,0:T(8,128)S(1)}, f32[72,512]{1,0:T(8,128)S(1)}, u32[]{:S(2)}, u32[]{:S(2)}) collective-permute-start(f32[72,512]{1,0:T(8,128)S(1)} %pad_maximum_fusion.2), channel_id=1, source_target_pairs={{0,4},{1,5},{2,6},{3,7},{4,0},{5,1},{6,2},{7,3},{8,12},{9,13},{10,... | collective-permute-start | bytes 442376 | tf_op jit(solution)/shard_map/ppermute | solution.py:511
  72.5 2.4 %collective-permute-done.25 = f32[1,64,1024]{2,1,0:T(8,128)S(1)} collective-permute-done((f32[1,64,1024]{2,1,0:T(8,128)S(1)}, f32[1,64,1024]{2,1,0:T(8,128)S(1)}, u32[]{:S(2)}, u32[]{:S(2)}) %collective-permute-start.25) | collective-permute-done | bytes 262176 | tf_op jit(solution)/shard_map/ppermute | solution.py:511
  75.0 0.9 collective-permute-start.26
  75.9 1.5 %collective-permute-done.20 = f32[72,512]{1,0:T(8,128)S(1)} collective-permute-done((f32[72,512]{1,0:T(8,128)S(1)}, f32[72,512]{1,0:T(8,128)S(1)}, u32[]{:S(2)}, u32[]{:S(2)}) %collective-permute-start.20) | collective-permute-done | bytes 147488 | tf_op jit(solution)/shard_map/ppermute | solution.py:511
  77.5 0.8 collective-permute-start.21
  78.6 1.3 %finish.1 = (f32[1,512]{1,0:T(1,128)}, f32[1,256]{1,0:T(1,128)}, f32[1,256]{1,0:T(1,128)}, f32[1,256]{1,0:T(1,128)}, f32[1,512]{1,0:T(1,128)}) custom-call(f32[1,256]{1,0:T(1,128)} %bitcast.69, f32[1,256]{1,0:T(1,128)} %bitcast.71, f32[1,512]{1,0:T(1,128)} %bitcast.66, f32[16,512]{1,0:T(8,128)S(1)} %maximum_select_fusion.9.refs_3_, ...), custom_call_target="tpu_custom_call" | custom-call | flops 1100000000 | bytes 3000000 | tf_op jit(solution)/shard_map/finish/pallas_call | solution.py:651
  80.0 3.5 %collective-permute-done.21 = f32[2,32,512]{2,1,0:T(8,128)S(1)} collective-permute-done((f32[2,32,512]{2,1,0:T(8,128)S(1)}, f32[2,32,512]{2,1,0:T(8,128)S(1)}, u32[]{:S(2)}, u32[]{:S(2)}) %collective-permute-start.21) | collective-permute-done | bytes 131104 | tf_op jit(solution)/shard_map/ppermute | solution.py:511
  83.5 0.8 collective-permute-done.26
  84.4 2.5 %collective-permute-start.28 = (f32[2,64,512]{2,1,0:T(8,128)S(1)}, f32[2,64,512]{2,1,0:T(8,128)S(1)}, u32[]{:S(2)}, u32[]{:S(2)}) collective-permute-start(f32[2,64,512]{2,1,0:T(8,128)S(1)} %maximum_select_fusion.6.refs_8_), channel_id=1, source_target_pairs={{0,16},{8,24},{16,0},{24,8},{1,17},{9,25},{17,1},{25,9},{2,18},{10... | collective-permute-start | bytes 786440 | tf_op jit(solution)/shard_map/ppermute | solution.py:573
  86.9 0.5 collective-permute-start.29
  87.4 1.0 %collective-permute-start.27 = (f32[2,64,512]{2,1,0:T(8,128)S(1)}, f32[2,64,512]{2,1,0:T(8,128)S(1)}, u32[]{:S(2)}, u32[]{:S(2)}) collective-permute-start(f32[2,64,512]{2,1,0:T(8,128)S(1)} %maximum_select_fusion.6.refs_8_), channel_id=1, source_target_pairs={{0,8},{8,0},{16,24},{24,16},{1,9},{9,1},{17,25},{25,17},{2,10},{10... | collective-permute-start | bytes 786440 | tf_op jit(solution)/shard_map/ppermute | solution.py:573
  88.5 5.7 %back_input.1 = (bf16[4,256,512]{2,1,0:T(8,128)(2,1)}, bf16[4,256,512]{2,1,0:T(8,128)(2,1)}) custom-call(f32[1,512]{1,0:T(1,128)} %bitcast.67, bf16[512,512]{1,0:T(8,128)(2,1)} %refs_1_.5, f32[1,512]{1,0:T(1,128)} %bitcast.47, bf16[1024,512]{1,0:T(8,128)(2,1)} %get-tuple-element.64.refs_3_, bf16[1024,512]{1,0:T(8,128)(2,1)} %cotangent_order.1.refs_6_.refs_4_, ...), custom_call_target="tpu_custom_call" | custom-call | flops 4400000000 | bytes 12000000 | tf_op jit(solution)/shard_map/back_input/pallas_call | solution.py:651
  94.1 4.7 %collective-permute-done.27 = f32[2,64,512]{2,1,0:T(8,128)S(1)} collective-permute-done((f32[2,64,512]{2,1,0:T(8,128)S(1)}, f32[2,64,512]{2,1,0:T(8,128)S(1)}, u32[]{:S(2)}, u32[]{:S(2)}) %collective-permute-start.27) | collective-permute-done | bytes 262176 | tf_op jit(solution)/shard_map/ppermute | solution.py:573
  99.4 1.0 copy-done.3
  100.3 1.3 %assemble.3 = f32[512,1024]{1,0:T(8,128)} custom-call(f32[256,1024]{1,0:T(8,128)S(1)} %bitcast.42, f32[256,1024]{1,0:T(8,128)S(1)} %collective-permute-done.32.refs_1_, bf16[4,256,512]{2,1,0:T(8,128)(2,1)S(1)} %copy-done.3), custom_call_target="tpu_custom_call" | custom-call | flops 2200000000 | bytes 6000000 | tf_op jit(solution)/shard_map/assemble/pallas_call | solution.py:651
  102.0 1.3 %assemble.2 = (f32[512,512]{1,0:T(8,128)}, f32[512,512]{1,0:T(8,128)}) custom-call(f32[256,1024]{1,0:T(8,128)S(1)} %pad_maximum_fusion.refs_0_, f32[256,1024]{1,0:T(8,128)S(1)} %collective-permute-done.31.refs_1_), custom_call_target="tpu_custom_call" | custom-call | flops 2200000000 | bytes 6000000 | tf_op jit(solution)/shard_map/assemble/pallas_call | solution.py:651
  (107 shorter events, 3.9 us)
Async XLA Ops:
  0.6 12.0 %copy-start.6 = (f32[4,512]{1,0:T(4,128)S(1)}, f32[4,512]{1,0:T(4,128)}, u32[]{:S(2)}) copy-start(f32[4,512]{1,0:T(4,128)} %constant.184.clone.1) | copy-start | bytes 24580
  5.6 1.3 %collective-permute-start = (f32[8,512]{1,0:T(8,128)S(1)}, f32[8,512]{1,0:T(8,128)S(1)}, u32[]{:S(2)}, u32[]{:S(2)}) collective-permute-start(f32[8,512]{1,0:T(8,128)S(1)} %get-tuple-element.67), channel_id=1, source_target_pairs={{0,1},{1,0},{2,3},{3,2},{4,5},{5,4},{6,7},{7,6},{8,9},{9,8},{10,11... | collective-permute-start | bytes 49160 | tf_op jit(solution)/shard_map/ppermute | solution.py:472
  7.0 8.3 %collective-permute-start.3 = (f32[8,512]{1,0:T(8,128)S(1)}, f32[8,512]{1,0:T(8,128)S(1)}, u32[]{:S(2)}, u32[]{:S(2)}) collective-permute-start(f32[8,512]{1,0:T(8,128)S(1)} %maximum_maximum_fusion), channel_id=1, source_target_pairs={{0,2},{1,3},{2,0},{3,1},{4,6},{5,7},{6,4},{7,5},{8,10},{9,11},{10,... | collective-permute-start | bytes 49160 | tf_op jit(solution)/shard_map/ppermute | solution.py:472
  10.0 5.3 %collective-permute-start.2 = (f32[8,512]{1,0:T(8,128)S(1)}, f32[8,512]{1,0:T(8,128)S(1)}, u32[]{:S(2)}, u32[]{:S(2)}) collective-permute-start(f32[8,512]{1,0:T(8,128)S(1)} %maximum_maximum_fusion), channel_id=1, source_target_pairs={{0,4},{1,5},{2,6},{3,7},{4,0},{5,1},{6,2},{7,3},{8,12},{9,13},{10,... | collective-permute-start | bytes 49160 | tf_op jit(solution)/shard_map/ppermute | solution.py:472
  12.6 5.5 %collective-permute-start.1 = (f32[8,512]{1,0:T(8,128)S(1)}, f32[8,512]{1,0:T(8,128)S(1)}, u32[]{:S(2)}, u32[]{:S(2)}) collective-permute-start(f32[8,512]{1,0:T(8,128)S(1)} %maximum_maximum_fusion), channel_id=1, source_target_pairs={{0,6},{1,7},{2,4},{3,5},{4,2},{5,3},{6,0},{7,1},{8,14},{9,15},{10,... | collective-permute-start | bytes 49160 | tf_op jit(solution)/shard_map/ppermute | solution.py:472
  28.7 2.7 %collective-permute-start.4 = (f32[256,1024]{1,0:T(8,128)S(1)}, f32[256,1024]{1,0:T(8,128)S(1)}, u32[]{:S(2)}, u32[]{:S(2)}) collective-permute-start(f32[256,1024]{1,0:T(8,128)S(1)} %get-tuple-element.78), channel_id=1, source_target_pairs={{0,1},{1,0},{2,3},{3,2},{4,5},{5,4},{6,7},{7,6},{8,9},{9,8},{10,11... | collective-permute-start | bytes 3145736 | tf_op jit(solution)/shard_map/ppermute | solution.py:449
  31.4 11.6 %copy-start = (bf16[512,512]{1,0:T(8,128)(2,1)S(1)}, bf16[512,512]{1,0:T(8,128)(2,1)}, u32[]{:S(2)}) copy-start(bf16[512,512]{1,0:T(8,128)(2,1)} %refs_1_.5) | copy-start | bytes 1572868
  31.4 11.6 %copy-start.1 = (f32[512]{0:T(512)S(1)}, f32[512]{0:T(512)}, u32[]{:S(2)}) copy-start(f32[512]{0:T(512)} %param.22) | copy-start | bytes 6148
  31.4 11.6 %copy-start.2 = (f32[256]{0:T(256)S(1)}, f32[256]{0:T(256)}, u32[]{:S(2)}) copy-start(f32[256]{0:T(256)} %param.18) | copy-start | bytes 3076
  31.4 11.6 %copy-start.5 = (f32[32,512]{1,0:T(8,128)S(1)}, f32[32,512]{1,0:T(8,128)}, u32[]{:S(2)}) copy-start(f32[32,512]{1,0:T(8,128)} %get-tuple-element.75.refs_4_) | copy-start | bytes 196612
  31.6 2.1 %collective-permute-start.5 = (f32[8,512]{1,0:T(8,128)S(1)}, f32[8,512]{1,0:T(8,128)S(1)}, u32[]{:S(2)}, u32[]{:S(2)}) collective-permute-start(f32[8,512]{1,0:T(8,128)S(1)} %maximum_maximum_fusion.1), channel_id=1, source_target_pairs={{0,1},{1,0},{2,3},{3,2},{4,5},{5,4},{6,7},{7,6},{8,9},{9,8},{10,11... | collective-permute-start | bytes 49160 | tf_op jit(solution)/shard_map/ppermute | solution.py:472
  31.8 11.2 %collective-permute-start.9 = (f32[256,512]{1,0:T(8,128)S(1)}, f32[256,512]{1,0:T(8,128)S(1)}, u32[]{:S(2)}, u32[]{:S(2)}) collective-permute-start(f32[256,512]{1,0:T(8,128)S(1)} %get-tuple-element.82), channel_id=1, source_target_pairs={{0,1},{1,0},{2,3},{3,2},{4,5},{5,4},{6,7},{7,6},{8,9},{9,8},{10,11... | collective-permute-start | bytes 1572872 | tf_op jit(solution)/shard_map/ppermute | solution.py:449
  32.2 9.2 %collective-permute-start.10 = (f32[128,1024]{1,0:T(8,128)S(1)}, f32[128,1024]{1,0:T(8,128)S(1)}, u32[]{:S(2)}, u32[]{:S(2)}) collective-permute-start(f32[128,1024]{1,0:T(8,128)S(1)} %get-tuple-element.84), channel_id=1, source_target_pairs={{0,8},{1,17},{2,10},{3,19},{4,12},{5,21},{6,14},{7,23},{8,0},{9,25... | collective-permute-start | bytes 1572872 | tf_op jit(solution)/shard_map/ppermute | solution.py:511
  33.7 4.5 %collective-permute-start.8 = (f32[8,512]{1,0:T(8,128)S(1)}, f32[8,512]{1,0:T(8,128)S(1)}, u32[]{:S(2)}, u32[]{:S(2)}) collective-permute-start(f32[8,512]{1,0:T(8,128)S(1)} %maximum_maximum_fusion.2), channel_id=1, source_target_pairs={{0,2},{1,3},{2,0},{3,1},{4,6},{5,7},{6,4},{7,5},{8,10},{9,11},{10,... | collective-permute-start | bytes 49160 | tf_op jit(solution)/shard_map/ppermute | solution.py:472
  33.8 4.9 %collective-permute-start.7 = (f32[8,512]{1,0:T(8,128)S(1)}, f32[8,512]{1,0:T(8,128)S(1)}, u32[]{:S(2)}, u32[]{:S(2)}) collective-permute-start(f32[8,512]{1,0:T(8,128)S(1)} %maximum_maximum_fusion.2), channel_id=1, source_target_pairs={{0,4},{1,5},{2,6},{3,7},{4,0},{5,1},{6,2},{7,3},{8,12},{9,13},{10,... | collective-permute-start | bytes 49160 | tf_op jit(solution)/shard_map/ppermute | solution.py:472
  35.4 5.5 %collective-permute-start.6 = (f32[8,512]{1,0:T(8,128)S(1)}, f32[8,512]{1,0:T(8,128)S(1)}, u32[]{:S(2)}, u32[]{:S(2)}) collective-permute-start(f32[8,512]{1,0:T(8,128)S(1)} %maximum_maximum_fusion.2), channel_id=1, source_target_pairs={{0,6},{1,7},{2,4},{3,5},{4,2},{5,3},{6,0},{7,1},{8,14},{9,15},{10,... | collective-permute-start | bytes 49160 | tf_op jit(solution)/shard_map/ppermute | solution.py:472
  41.4 6.4 %collective-permute-start.15 = (f32[64,1024]{1,0:T(8,128)S(1)}, f32[64,1024]{1,0:T(8,128)S(1)}, u32[]{:S(2)}, u32[]{:S(2)}) collective-permute-start(f32[64,1024]{1,0:T(8,128)S(1)} %get-tuple-element.93), channel_id=1, source_target_pairs={{0,16},{1,9},{2,18},{3,11},{4,20},{5,13},{6,22},{7,15},{8,24},{9,1... | collective-permute-start | bytes 786440 | tf_op jit(solution)/shard_map/ppermute | solution.py:511
  46.8 8.0 %collective-permute-start.14 = (f32[264,512]{1,0:T(8,128)S(1)}, f32[264,512]{1,0:T(8,128)S(1)}, u32[]{:S(2)}, u32[]{:S(2)}) collective-permute-start(f32[264,512]{1,0:T(8,128)S(1)} %get-tuple-element.92), channel_id=1, source_target_pairs={{0,1},{1,0},{2,3},{3,2},{4,5},{5,4},{6,7},{7,6},{8,9},{9,8},{10,11... | collective-permute-start | bytes 1622024 | tf_op jit(solution)/shard_map/ppermute | solution.py:449
  47.9 5.0 %collective-permute-start.22 = (f32[32,1024]{1,0:T(8,128)S(1)}, f32[32,1024]{1,0:T(8,128)S(1)}, u32[]{:S(2)}, u32[]{:S(2)}) collective-permute-start(f32[32,1024]{1,0:T(8,128)S(1)} %get-tuple-element.100), channel_id=1, source_target_pairs={{0,2},{1,3},{2,0},{3,1},{4,6},{5,7},{6,4},{7,5},{8,10},{9,11},{10,... | collective-permute-start | bytes 393224 | tf_op jit(solution)/shard_map/ppermute | solution.py:511
  48.1 7.5 %collective-permute-start.11 = (f32[1,64,512]{2,1,0:T(8,128)S(1)}, f32[1,64,512]{2,1,0:T(8,128)S(1)}, u32[]{:S(2)}, u32[]{:S(2)}) collective-permute-start(f32[1,64,512]{2,1,0:T(8,128)S(1)} %bitcast.45), channel_id=1, source_target_pairs={{0,8},{8,0},{16,24},{24,16},{1,9},{9,1},{17,25},{25,17},{2,10},{10... | collective-permute-start | bytes 393224 | tf_op jit(solution)/shard_map/ppermute | solution.py:573
  49.7 8.6 %collective-permute-start.12 = (f32[1,64,512]{2,1,0:T(8,128)S(1)}, f32[1,64,512]{2,1,0:T(8,128)S(1)}, u32[]{:S(2)}, u32[]{:S(2)}) collective-permute-start(f32[1,64,512]{2,1,0:T(8,128)S(1)} %bitcast.44), channel_id=1, source_target_pairs={{0,16},{8,24},{16,0},{24,8},{1,17},{9,25},{17,1},{25,9},{2,18},{10... | collective-permute-start | bytes 393224 | tf_op jit(solution)/shard_map/ppermute | solution.py:573
  51.2 7.3 %collective-permute-start.13 = (f32[1,64,512]{2,1,0:T(8,128)S(1)}, f32[1,64,512]{2,1,0:T(8,128)S(1)}, u32[]{:S(2)}, u32[]{:S(2)}) collective-permute-start(f32[1,64,512]{2,1,0:T(8,128)S(1)} %bitcast.43), channel_id=1, source_target_pairs={{0,24},{8,16},{16,8},{24,0},{1,25},{9,17},{17,9},{25,1},{2,26},{10... | collective-permute-start | bytes 393224 | tf_op jit(solution)/shard_map/ppermute | solution.py:573
  53.0 7.6 %collective-permute-start.23 = (f32[1,32,1024]{2,1,0:T(8,128)S(1)}, f32[1,32,1024]{2,1,0:T(8,128)S(1)}, u32[]{:S(2)}, u32[]{:S(2)}) collective-permute-start(f32[1,32,1024]{2,1,0:T(8,128)S(1)} %add_bitcast_fusion), channel_id=1, source_target_pairs={{0,4},{1,5},{2,6},{3,7},{4,0},{5,1},{6,2},{7,3},{8,12},{9,13},{10,... | collective-permute-start | bytes 393224 | tf_op jit(solution)/shard_map/ppermute | solution.py:511
  54.9 6.0 %collective-permute-start.16 = (f32[72,512]{1,0:T(8,128)S(1)}, f32[72,512]{1,0:T(8,128)S(1)}, u32[]{:S(2)}, u32[]{:S(2)}) collective-permute-start(f32[72,512]{1,0:T(8,128)S(1)} %get-tuple-element.96), channel_id=1, source_target_pairs={{0,8},{8,0},{16,24},{24,16},{1,9},{9,1},{17,25},{25,17},{2,10},{10... | collective-permute-start | bytes 442376 | tf_op jit(solution)/shard_map/ppermute | solution.py:573
  55.6 6.5 %collective-permute-start.17 = (f32[72,512]{1,0:T(8,128)S(1)}, f32[72,512]{1,0:T(8,128)S(1)}, u32[]{:S(2)}, u32[]{:S(2)}) collective-permute-start(f32[72,512]{1,0:T(8,128)S(1)} %get-tuple-element.97), channel_id=1, source_target_pairs={{0,16},{8,24},{16,0},{24,8},{1,17},{9,25},{17,1},{25,9},{2,18},{10... | collective-permute-start | bytes 442376 | tf_op jit(solution)/shard_map/ppermute | solution.py:573
  58.3 6.0 %collective-permute-start.18 = (f32[72,512]{1,0:T(8,128)S(1)}, f32[72,512]{1,0:T(8,128)S(1)}, u32[]{:S(2)}, u32[]{:S(2)}) collective-permute-start(f32[72,512]{1,0:T(8,128)S(1)} %get-tuple-element.98), channel_id=1, source_target_pairs={{0,24},{8,16},{16,8},{24,0},{1,25},{9,17},{17,9},{25,1},{2,26},{10... | collective-permute-start | bytes 442376 | tf_op jit(solution)/shard_map/ppermute | solution.py:573
  60.6 5.9 %collective-permute-start.24 = (f32[1,32,1024]{2,1,0:T(8,128)S(1)}, f32[1,32,1024]{2,1,0:T(8,128)S(1)}, u32[]{:S(2)}, u32[]{:S(2)}) collective-permute-start(f32[1,32,1024]{2,1,0:T(8,128)S(1)} %add.263), channel_id=1, source_target_pairs={{0,2},{1,3},{2,0},{3,1},{4,6},{5,7},{6,4},{7,5},{8,10},{9,11},{10,... | collective-permute-start | bytes 393224 | tf_op jit(solution)/shard_map/ppermute | solution.py:511
  64.4 5.2 %collective-permute-start.19 = (f32[72,512]{1,0:T(8,128)S(1)}, f32[72,512]{1,0:T(8,128)S(1)}, u32[]{:S(2)}, u32[]{:S(2)}) collective-permute-start(f32[72,512]{1,0:T(8,128)S(1)} %pad_maximum_fusion.1), channel_id=1, source_target_pairs={{0,2},{1,3},{2,0},{3,1},{4,6},{5,7},{6,4},{7,5},{8,10},{9,11},{10,... | collective-permute-start | bytes 442376 | tf_op jit(solution)/shard_map/ppermute | solution.py:511
  66.5 8.4 %collective-permute-start.25 = (f32[1,64,1024]{2,1,0:T(8,128)S(1)}, f32[1,64,1024]{2,1,0:T(8,128)S(1)}, u32[]{:S(2)}, u32[]{:S(2)}) collective-permute-start(f32[1,64,1024]{2,1,0:T(8,128)S(1)} %maximum_select_fusion.8), channel_id=1, source_target_pairs={{0,16},{1,9},{2,18},{3,11},{4,20},{5,13},{6,22},{7,15},{8,24},{9,1... | collective-permute-start | bytes 786440 | tf_op jit(solution)/shard_map/ppermute | solution.py:511
  69.7 7.7 %collective-permute-start.20 = (f32[72,512]{1,0:T(8,128)S(1)}, f32[72,512]{1,0:T(8,128)S(1)}, u32[]{:S(2)}, u32[]{:S(2)}) collective-permute-start(f32[72,512]{1,0:T(8,128)S(1)} %pad_maximum_fusion.2), channel_id=1, source_target_pairs={{0,4},{1,5},{2,6},{3,7},{4,0},{5,1},{6,2},{7,3},{8,12},{9,13},{10,... | collective-permute-start | bytes 442376 | tf_op jit(solution)/shard_map/ppermute | solution.py:511
  75.0 9.2 %collective-permute-start.26 = (f32[1,128,1024]{2,1,0:T(8,128)S(1)}, f32[1,128,1024]{2,1,0:T(8,128)S(1)}, u32[]{:S(2)}, u32[]{:S(2)}) collective-permute-start(f32[1,128,1024]{2,1,0:T(8,128)S(1)} %maximum_select_fusion.3), channel_id=1, source_target_pairs={{0,8},{1,17},{2,10},{3,19},{4,12},{5,21},{6,14},{7,23},{8,0},{9,25... | collective-permute-start | bytes 1572872 | tf_op jit(solution)/shard_map/ppermute | solution.py:511
  77.4 1.2 %collective-permute-start.30 = (f32[8,512]{1,0:T(8,128)S(1)}, f32[8,512]{1,0:T(8,128)S(1)}, u32[]{:S(2)}, u32[]{:S(2)}) collective-permute-start(f32[8,512]{1,0:T(8,128)S(1)} %slice_add_fusion.2), channel_id=1, source_target_pairs={{0,1},{1,0},{2,3},{3,2},{4,5},{5,4},{6,7},{7,6},{8,9},{9,8},{10,11... | collective-permute-start | bytes 49160 | tf_op jit(solution)/shard_map/ppermute | solution.py:449
  77.5 6.0 %collective-permute-start.21 = (f32[2,32,512]{2,1,0:T(8,128)S(1)}, f32[2,32,512]{2,1,0:T(8,128)S(1)}, u32[]{:S(2)}, u32[]{:S(2)}) collective-permute-start(f32[2,32,512]{2,1,0:T(8,128)S(1)} %fusion.9), channel_id=1, source_target_pairs={{0,2},{1,3},{2,0},{3,1},{4,6},{5,7},{6,4},{7,5},{8,10},{9,11},{10,... | collective-permute-start | bytes 393224 | tf_op jit(solution)/shard_map/ppermute | solution.py:511
  79.9 8.5 %copy-start.4 = (f32[1,512]{1,0:T(1,128)S(1)}, f32[1,512]{1,0:T(1,128)}, u32[]{:S(2)}) copy-start(f32[1,512]{1,0:T(1,128)} %get-tuple-element.105.refs_9_) | copy-start | bytes 6148
  84.4 14.6 %collective-permute-start.28 = (f32[2,64,512]{2,1,0:T(8,128)S(1)}, f32[2,64,512]{2,1,0:T(8,128)S(1)}, u32[]{:S(2)}, u32[]{:S(2)}) collective-permute-start(f32[2,64,512]{2,1,0:T(8,128)S(1)} %maximum_select_fusion.6.refs_8_), channel_id=1, source_target_pairs={{0,16},{8,24},{16,0},{24,8},{1,17},{9,25},{17,1},{25,9},{2,18},{10... | collective-permute-start | bytes 786440 | tf_op jit(solution)/shard_map/ppermute | solution.py:573
  86.9 12.0 %collective-permute-start.29 = (f32[2,64,512]{2,1,0:T(8,128)S(1)}, f32[2,64,512]{2,1,0:T(8,128)S(1)}, u32[]{:S(2)}, u32[]{:S(2)}) collective-permute-start(f32[2,64,512]{2,1,0:T(8,128)S(1)} %maximum_select_fusion.6.refs_8_), channel_id=1, source_target_pairs={{0,24},{8,16},{16,8},{24,0},{1,25},{9,17},{17,9},{25,1},{2,26},{10... | collective-permute-start | bytes 786440 | tf_op jit(solution)/shard_map/ppermute | solution.py:573
  87.4 11.5 %collective-permute-start.27 = (f32[2,64,512]{2,1,0:T(8,128)S(1)}, f32[2,64,512]{2,1,0:T(8,128)S(1)}, u32[]{:S(2)}, u32[]{:S(2)}) collective-permute-start(f32[2,64,512]{2,1,0:T(8,128)S(1)} %maximum_select_fusion.6.refs_8_), channel_id=1, source_target_pairs={{0,8},{8,0},{16,24},{24,16},{1,9},{9,1},{17,25},{25,17},{2,10},{10... | collective-permute-start | bytes 786440 | tf_op jit(solution)/shard_map/ppermute | solution.py:573
  88.5 10.9 %collective-permute-start.32 = (f32[256,1024]{1,0:T(8,128)S(1)}, f32[256,1024]{1,0:T(8,128)S(1)}, u32[]{:S(2)}, u32[]{:S(2)}) collective-permute-start(f32[256,1024]{1,0:T(8,128)S(1)} %bitcast.41), channel_id=1, source_target_pairs={{0,1},{1,0},{2,3},{3,2},{4,5},{5,4},{6,7},{7,6},{8,9},{9,8},{10,11... | collective-permute-start | bytes 3145736 | tf_op jit(solution)/shard_map/ppermute | solution.py:449
  99.1 1.2 %copy-start.3 = (bf16[4,256,512]{2,1,0:T(8,128)(2,1)S(1)}, bf16[4,256,512]{2,1,0:T(8,128)(2,1)}, u32[]{:S(2)}) copy-start(bf16[4,256,512]{2,1,0:T(8,128)(2,1)} %get-tuple-element.109.refs_2_) | copy-start | bytes 3145732
  99.3 2.7 %collective-permute-start.31 = (f32[256,1024]{1,0:T(8,128)S(1)}, f32[256,1024]{1,0:T(8,128)S(1)}, u32[]{:S(2)}, u32[]{:S(2)}) collective-permute-start(f32[256,1024]{1,0:T(8,128)S(1)} %pad_maximum_fusion.refs_0_), channel_id=1, source_target_pairs={{0,1},{1,0},{2,3},{3,2},{4,5},{5,4},{6,7},{7,6},{8,9},{9,8},{10,11... | collective-permute-start | bytes 3145736 | tf_op jit(solution)/shard_map/ppermute | solution.py:449

commit v3 on v2

--- a/solution.py
+++ b/solution.py
@@ -100,6 +100,12 @@
     top, bottom = value[:rows], value[rows:]
     keep[...] = jnp.where(first, top, bottom)
     send[...] = jnp.where(first, bottom, top)
+
+
+def half_tn(left, right, other):
+    columns = left.shape[1] // 2
+    first = lax.rem(lax.axis_index("seq"), 2) == other
+    return dot_tn(jnp.where(first, left[:, :columns], left[:, columns:]), right)
 
 
 class Copies:
@@ -213,9 +219,9 @@
 
 def block_kernel(
     w_hbm, c_hbm, d_hbm, xs_hbm, normed_hbm, loc_hbm, cts_hbm, enter_ref, pow_ref, keep_ref,
-    out_hbm, h_hbm, mixed_hbm, adj_hbm, carry_hbm, c_go_hbm, back_ref, g_d_ref, w_go_ref, w_send_ref, c_send_ref,
-    carry_ref, c_go_ref, w_ref, c_ref, d_ref, xs_ref, normed_ref, h_ref, cts_ref,
-    out_ref, states_ref, gelu_ref, pre_ref, slope_ref, mixed_ref, low_ref, adj_ref, sems,
+    out_hbm, h_hbm, mixed_hbm, adj_hbm, carry_hbm, back_ref, g_d_ref, w_send_ref,
+    states_ref, gelu_ref, pre_ref, low_ref, carry_ref, w_ref, c_ref, d_ref, xs_ref, normed_ref, h_ref, cts_ref,
+    out_ref, slope_ref, mixed_ref, adj_ref, sems,
 ):
     lanes, width = enter_ref.shape[0], d_ref.shape[1]
     seg = h_ref.shape[0] // lanes
@@ -304,10 +310,16 @@
         cstore(back_ref, lane, state)
     g_d_ref[...] = total
     leaving.append(copies.start(carry_ref, carry_hbm))
+    w_send_ref[...] = half_tn(gelu_ref[...], pre_ref[...], 1)
+    wait(leaving)
+
+
+def own_kernel(gelu_ref, pre_ref, states_ref, low_ref, c_go_hbm, w_go_ref, c_send_ref, c_go_ref, sems):
     put_halves(dot_tn(states_ref[...], low_ref[...]), c_go_ref, c_send_ref)
-    leaving.append(copies.start(c_go_ref, c_go_hbm))
-    put_halves(dot_tn(gelu_ref[...], pre_ref[...]), w_go_ref, w_send_ref)
-    wait(leaving)
+    copy = pltpu.make_async_copy(c_go_ref, c_go_hbm, sems.at[0])
+    copy.start()
+    w_go_ref[...] = half_tn(gelu_ref[...], pre_ref[...], 0)
+    copy.wait()
 
 
 def states_kernel(
@@ -679,20 +691,22 @@
     )
 
     chunk_rows, half_rows = ((lanes * CHUNKS, two), F32), ((n, width), F32)
-    out, h, grad_mixed, adj, carry, c_keep, back_total, grad_d, w_keep, w_send, c_send = call(
+    out, h, grad_mixed, adj, carry, back_total, grad_d, w_send, states, gelu, pre, low = call(
         block_kernel, "block", 10,
         [
-            low_rows, full_rows, full_rows, full_rows, chunk_rows, half_rows, ((lanes, two), F32),
-            ((1, width), F32), ((n, 2 * width), F32), ((n, 2 * width), F32), half_rows,
+            low_rows, full_rows, full_rows, full_rows, chunk_rows, ((lanes, two), F32), ((1, width), F32),
+            ((n, 2 * width), F32), low_rows, low_rows, ((tokens, 2 * width), BF16), low_rows,
         ],
         [glu_weight, c_proj, skip, xs, normed, loc, cts], [enter, powers, keep], fetched=(),
         scratch=[
-            chunk_rows, half_rows, ((width, 2 * width), BF16), ((two, width), BF16), ((1, width), F32),
-            low_rows, low_rows, full_rows, low_rows,
-            low_rows, low_rows, low_rows, ((tokens, 2 * width), BF16), full_rows, full_rows, low_rows,
-            full_rows,
+            chunk_rows, ((width, 2 * width), BF16), ((two, width), BF16), ((1, width), F32),
+            low_rows, low_rows, full_rows, low_rows, low_rows, full_rows, full_rows, full_rows,
         ],
-        sems=4 * lanes + 13, far_outs=6, limit=36,
+        sems=4 * lanes + 12, far_outs=5, limit=30,
+    )
+    c_keep, w_keep, c_send = call(
+        own_kernel, "own_grads", 2, [half_rows, ((n, 2 * width), F32), half_rows],
+        [], [gelu, pre, states, low], scratch=[half_rows], sems=1, far_outs=1, limit=8,
     )
 
     decay = pair[lanes:]

time: 104 us -> 103 us (level)
  waiting for transfers between devices: 34.2 us -> 32.3 us
  Pallas kernels: 31.8 us -> 32.9 us
    ppermute x6, waiting for transfers between devices: 3.33 us -> 1.47 us  [swap(): return lax.ppermute(value, axis, [(i, i ^ 1 << bit) for i in range(count)])]
    pallas_call x13 -> x14, Pallas kernels: 31.8 us -> 32.9 us  [call(): pl.pallas_call(body, in_specs=[hbm] * len(far) + [vmem] * len(near) + [pl...]
  transfers between devices with their start and end apart: 33 -> 33, of which waited for: 22 -> 22; matrix products, arithmetic and copies ran while one was open for 1% -> 1% of each run, Pallas kernels for 15% -> 16%
where the time goes in v3:
time: 103 us
  starting transfers between devices  33.7 us (33%)
  Pallas kernels  32.9 us (32%)
  waiting for transfers between devices  32.3 us (31%)
  between operations  1.52 us (1%)
  other arithmetic  1.12 us (1%)
  local copies, waits for them, and re-layouts  1.08 us (1%)
    pallas_call x14, Pallas kernels, call(): pl.pallas_call(body, in_specs=[hbm] * len(far) + [vmem] * len(near) + [pl...  32.9 us
    ppermute x10, waiting for transfers between devices, hop(): return lax.ppermute(value, ('dp', 'seq'), pairs)  14.9 us
    ppermute x10, starting transfers between devices, hop(): return lax.ppermute(value, ('dp', 'seq'), pairs)  12.3 us
    ppermute x8, starting transfers between devices, entering(): lax.ppermute(pair, 'seq', [(i, i ^ mask << bit) for i in range(count)])  10.7 us
    ppermute x9, starting transfers between devices, across(): lax.ppermute(value, 'dp', [(i, i ^ mask) for i in range(lax.axis_size('dp...  10.1 us
    ppermute x9, waiting for transfers between devices, across(): lax.ppermute(value, 'dp', [(i, i ^ mask) for i in range(lax.axis_size('dp...  9.59 us
    ppermute x8, waiting for transfers between devices, entering(): lax.ppermute(pair, 'seq', [(i, i ^ mask << bit) for i in range(count)])  6.39 us
  transfers between devices with their start and end apart: 33, of which 22 were waited for; matrix products, arithmetic and copies ran while one was open for 1% of the time, Pallas kernels for 16%

profile of v3, /device:TPU:0, one launch (start us, length us, event | category | flops | bytes accessed | tf_op | source)
XLA Modules:
  0.0 102.7 jit_solution(11301857565636701771)
XLA Ops:
  0.7 5.0 %forward_local.1 = (bf16[1024,512]{1,0:T(8,128)(2,1)}, bf16[1024,512]{1,0:T(8,128)(2,1)}, f32[1024,512]{1,0:T(8,128)}, f32[8,512]{1,0:T(8,128)S(1)}, f32[32,512]{1,0:T(8,128)S(1)}, /*index=5*/f32[32,512]{1,0:T(8,128)S(1)}) custom-call(s32[4,16]{1,0:T(4,128)} %bitcast.64, s32[1,4]{1,0:T(1,128)} %refs_1_.3, bf16[4,256,512]{2,1,0:T(8,128)(2,1)} %bitcast.62, ...), custom_call_target="tpu_custom_call" | custom-call | flops 4400000000 | bytes 12000000 | tf_op jit(solution)/shard_map/forward_local/pallas_call | solution.py:663
  5.6 0.5 collective-permute-start
  6.1 0.8 collective-permute-done
  7.0 3.0 %collective-permute-start.3 = (f32[8,512]{1,0:T(8,128)S(1)}, f32[8,512]{1,0:T(8,128)S(1)}, u32[]{:S(2)}, u32[]{:S(2)}) collective-permute-start(f32[8,512]{1,0:T(8,128)S(1)} %maximum_maximum_fusion), channel_id=1, source_target_pairs={{0,2},{1,3},{2,0},{3,1},{4,6},{5,7},{6,4},{7,5},{8,10},{9,11},{10,... | collective-permute-start | bytes 49160 | tf_op jit(solution)/shard_map/ppermute | solution.py:484
  10.0 2.6 %collective-permute-start.2 = (f32[8,512]{1,0:T(8,128)S(1)}, f32[8,512]{1,0:T(8,128)S(1)}, u32[]{:S(2)}, u32[]{:S(2)}) collective-permute-start(f32[8,512]{1,0:T(8,128)S(1)} %maximum_maximum_fusion), channel_id=1, source_target_pairs={{0,4},{1,5},{2,6},{3,7},{4,0},{5,1},{6,2},{7,3},{8,12},{9,13},{10,... | collective-permute-start | bytes 49160 | tf_op jit(solution)/shard_map/ppermute | solution.py:484
  12.6 2.7 %cotangent_order.1.refs_6_.refs_4_ = bf16[1024,512]{1,0:T(8,128)(2,1)} custom-call(bf16[4,256,512]{2,1,0:T(8,128)(2,1)} %bitcast.63), custom_call_target="tpu_custom_call" | custom-call | flops 2200000000 | bytes 6000000 | tf_op jit(solution)/shard_map/cotangent_order/pallas_call | solution.py:663
  15.4 2.8 %collective-permute-done.1 = f32[8,512]{1,0:T(8,128)S(1)} collective-permute-done((f32[8,512]{1,0:T(8,128)S(1)}, f32[8,512]{1,0:T(8,128)S(1)}, u32[]{:S(2)}, u32[]{:S(2)}) %collective-permute-start.1) | collective-permute-done | bytes 16416 | tf_op jit(solution)/shard_map/ppermute | solution.py:484
  18.3 9.6 %block.1 = (bf16[1024,512]{1,0:T(8,128)(2,1)}, f32[1024,512]{1,0:T(8,128)}, f32[1024,512]{1,0:T(8,128)}, f32[1024,512]{1,0:T(8,128)}, f32[32,512]{1,0:T(8,128)},...) custom-call(bf16[512,1024]{1,0:T(8,128)(2,1)} %refs_0_.1, ...), custom_call_target="tpu_custom_call" | custom-call | flops 11000000512 | bytes 30000000 | tf_op jit(solution)/shard_map/block/pallas_call | solution.py:663
  28.0 1.9 %own_grads.1 = (f32[256,512]{1,0:T(8,128)}, f32[256,1024]{1,0:T(8,128)S(1)}, f32[256,512]{1,0:T(8,128)S(1)}) custom-call(bf16[1024,512]{1,0:T(8,128)(2,1)S(1)} %get-tuple-element.76.refs_0_, bf16[1024,1024]{1,0:T(8,128)(2,1)S(1)} %get-tuple-element.77.refs_1_, bf16[1024,512]{1,0:T(8,128)(2,1)S(1)} %get-tuple-element.78.refs_2_, ...), custom_call_target="tpu_custom_call" | custom-call | flops 2200000000 | bytes 6000000 | tf_op jit(solution)/shard_map/own_grads/pallas_call | solution.py:663
  29.9 0.7 collective-permute-done.4.refs_1_
  31.3 1.5 %collective-permute-start.10 = (f32[128,1024]{1,0:T(8,128)S(1)}, f32[128,1024]{1,0:T(8,128)S(1)}, u32[]{:S(2)}, u32[]{:S(2)}) collective-permute-start(f32[128,1024]{1,0:T(8,128)S(1)} %get-tuple-element.92), channel_id=1, source_target_pairs={{0,8},{1,17},{2,10},{3,19},{4,12},{5,21},{6,14},{7,23},{8,0},{9,25... | collective-permute-start | bytes 1572872 | tf_op jit(solution)/shard_map/ppermute | solution.py:523
  33.0 1.6 %collective-permute-start.7 = (f32[8,512]{1,0:T(8,128)S(1)}, f32[8,512]{1,0:T(8,128)S(1)}, u32[]{:S(2)}, u32[]{:S(2)}) collective-permute-start(f32[8,512]{1,0:T(8,128)S(1)} %maximum_maximum_fusion.2), channel_id=1, source_target_pairs={{0,4},{1,5},{2,6},{3,7},{4,0},{5,1},{6,2},{7,3},{8,12},{9,13},{10,... | collective-permute-start | bytes 49160 | tf_op jit(solution)/shard_map/ppermute | solution.py:484
  34.6 2.8 %collective-permute-start.6 = (f32[8,512]{1,0:T(8,128)S(1)}, f32[8,512]{1,0:T(8,128)S(1)}, u32[]{:S(2)}, u32[]{:S(2)}) collective-permute-start(f32[8,512]{1,0:T(8,128)S(1)} %maximum_maximum_fusion.2), channel_id=1, source_target_pairs={{0,6},{1,7},{2,4},{3,5},{4,2},{5,3},{6,0},{7,1},{8,14},{9,15},{10,... | collective-permute-start | bytes 49160 | tf_op jit(solution)/shard_map/ppermute | solution.py:484
  37.4 0.5 collective-permute-done.7
  37.9 2.3 %collective-permute-done.6 = f32[8,512]{1,0:T(8,128)S(1)} collective-permute-done((f32[8,512]{1,0:T(8,128)S(1)}, f32[8,512]{1,0:T(8,128)S(1)}, u32[]{:S(2)}, u32[]{:S(2)}) %collective-permute-start.6) | collective-permute-done | bytes 16416 | tf_op jit(solution)/shard_map/ppermute | solution.py:484
  40.6 1.6 %collective-permute-start.15 = (f32[64,1024]{1,0:T(8,128)S(1)}, f32[64,1024]{1,0:T(8,128)S(1)}, u32[]{:S(2)}, u32[]{:S(2)}) collective-permute-start(f32[64,1024]{1,0:T(8,128)S(1)} %get-tuple-element.101), channel_id=1, source_target_pairs={{0,16},{1,9},{2,18},{3,11},{4,20},{5,13},{6,22},{7,15},{8,24},{9,1... | collective-permute-start | bytes 786440 | tf_op jit(solution)/shard_map/ppermute | solution.py:523
  42.2 3.8 %adjoint_states.1 = (bf16[1024,512]{1,0:T(8,128)(2,1)}, f32[264,512]{1,0:T(8,128)S(1)}, f32[264,512]{1,0:T(8,128)S(1)}, f32[256,512]{1,0:T(8,128)S(1)}) custom-call(f32[256,512]{1,0:T(8,128)} %get-tuple-element.80.refs_0_, f32[1024,512]{1,0:T(8,128)} %get-tuple-element.81.refs_1_, f32[1024,512]{1,0:T(8,128)} %get-tuple-element.82.refs_2_, ...), custom_call_target="tpu_custom_call" | custom-call | flops 3300000000 | bytes 9000000 | tf_op jit(solution)/shard_map/adjoint_states/pallas_call | solution.py:663
  46.1 0.9 collective-permute-done.15.refs_1_
  47.3 1.6 %collective-permute-start.11 = (f32[1,64,512]{2,1,0:T(8,128)S(1)}, f32[1,64,512]{2,1,0:T(8,128)S(1)}, u32[]{:S(2)}, u32[]{:S(2)}) collective-permute-start(f32[1,64,512]{2,1,0:T(8,128)S(1)} %bitcast.45), channel_id=1, source_target_pairs={{0,8},{8,0},{16,24},{24,16},{1,9},{9,1},{17,25},{25,17},{2,10},{10... | collective-permute-start | bytes 393224 | tf_op jit(solution)/shard_map/ppermute | solution.py:585
  48.9 1.5 %collective-permute-start.12 = (f32[1,64,512]{2,1,0:T(8,128)S(1)}, f32[1,64,512]{2,1,0:T(8,128)S(1)}, u32[]{:S(2)}, u32[]{:S(2)}) collective-permute-start(f32[1,64,512]{2,1,0:T(8,128)S(1)} %bitcast.44), channel_id=1, source_target_pairs={{0,16},{8,24},{16,0},{24,8},{1,17},{9,25},{17,1},{25,9},{2,18},{10... | collective-permute-start | bytes 393224 | tf_op jit(solution)/shard_map/ppermute | solution.py:585
  50.8 1.3 %collective-permute-done.22 = f32[32,1024]{1,0:T(8,128)S(1)} collective-permute-done((f32[32,1024]{1,0:T(8,128)S(1)}, f32[32,1024]{1,0:T(8,128)S(1)}, u32[]{:S(2)}, u32[]{:S(2)}) %collective-permute-start.22) | collective-permute-done | bytes 131104 | tf_op jit(solution)/shard_map/ppermute | solution.py:523
  52.1 1.9 %collective-permute-start.23 = (f32[1,32,1024]{2,1,0:T(8,128)S(1)}, f32[1,32,1024]{2,1,0:T(8,128)S(1)}, u32[]{:S(2)}, u32[]{:S(2)}) collective-permute-start(f32[1,32,1024]{2,1,0:T(8,128)S(1)} %add_bitcast_fusion), channel_id=1, source_target_pairs={{0,4},{1,5},{2,6},{3,7},{4,0},{5,1},{6,2},{7,3},{8,12},{9,13},{10,... | collective-permute-start | bytes 393224 | tf_op jit(solution)/shard_map/ppermute | solution.py:523
  54.1 0.7 collective-permute-start.16
  54.8 1.5 %collective-permute-start.17 = (f32[72,512]{1,0:T(8,128)S(1)}, f32[72,512]{1,0:T(8,128)S(1)}, u32[]{:S(2)}, u32[]{:S(2)}) collective-permute-start(f32[72,512]{1,0:T(8,128)S(1)} %get-tuple-element.105), channel_id=1, source_target_pairs={{0,16},{8,24},{16,0},{24,8},{1,17},{9,25},{17,1},{25,9},{2,18},{10... | collective-permute-start | bytes 442376 | tf_op jit(solution)/shard_map/ppermute | solution.py:585
  56.3 1.1 %collective-permute-done.12 = f32[1,64,512]{2,1,0:T(8,128)S(1)} collective-permute-done((f32[1,64,512]{2,1,0:T(8,128)S(1)}, f32[1,64,512]{2,1,0:T(8,128)S(1)}, u32[]{:S(2)}, u32[]{:S(2)}) %collective-permute-start.12) | collective-permute-done | bytes 131104 | tf_op jit(solution)/shard_map/ppermute | solution.py:585
  57.7 2.0 %collective-permute-done.23 = f32[1,32,1024]{2,1,0:T(8,128)S(1)} collective-permute-done((f32[1,32,1024]{2,1,0:T(8,128)S(1)}, f32[1,32,1024]{2,1,0:T(8,128)S(1)}, u32[]{:S(2)}, u32[]{:S(2)}) %collective-permute-start.23) | collective-permute-done | bytes 131104 | tf_op jit(solution)/shard_map/ppermute | solution.py:523
  60.0 1.2 %collective-permute-done.17 = f32[72,512]{1,0:T(8,128)S(1)} collective-permute-done((f32[72,512]{1,0:T(8,128)S(1)}, f32[72,512]{1,0:T(8,128)S(1)}, u32[]{:S(2)}, u32[]{:S(2)}) %collective-permute-start.17) | collective-permute-done | bytes 147488 | tf_op jit(solution)/shard_map/ppermute | solution.py:585
  61.3 2.2 %collective-permute-done.18 = f32[72,512]{1,0:T(8,128)S(1)} collective-permute-done((f32[72,512]{1,0:T(8,128)S(1)}, f32[72,512]{1,0:T(8,128)S(1)}, u32[]{:S(2)}, u32[]{:S(2)}) %collective-permute-start.18) | collective-permute-done | bytes 147488 | tf_op jit(solution)/shard_map/ppermute | solution.py:585
  63.6 0.9 collective-permute-start.19
  64.5 1.2 %collective-permute-done.24 = f32[1,32,1024]{2,1,0:T(8,128)S(1)} collective-permute-done((f32[1,32,1024]{2,1,0:T(8,128)S(1)}, f32[1,32,1024]{2,1,0:T(8,128)S(1)}, u32[]{:S(2)}, u32[]{:S(2)}) %collective-permute-start.24) | collective-permute-done | bytes 131104 | tf_op jit(solution)/shard_map/ppermute | solution.py:523
  65.7 1.9 %collective-permute-start.25 = (f32[1,64,1024]{2,1,0:T(8,128)S(1)}, f32[1,64,1024]{2,1,0:T(8,128)S(1)}, u32[]{:S(2)}, u32[]{:S(2)}) collective-permute-start(f32[1,64,1024]{2,1,0:T(8,128)S(1)} %maximum_select_fusion.8), channel_id=1, source_target_pairs={{0,16},{1,9},{2,18},{3,11},{4,20},{5,13},{6,22},{7,15},{8,24},{9,1... | collective-permute-start | bytes 786440 | tf_op jit(solution)/shard_map/ppermute | solution.py:523
  67.6 1.2 %collective-permute-done.19 = f32[72,512]{1,0:T(8,128)S(1)} collective-permute-done((f32[72,512]{1,0:T(8,128)S(1)}, f32[72,512]{1,0:T(8,128)S(1)}, u32[]{:S(2)}, u32[]{:S(2)}) %collective-permute-start.19) | collective-permute-done | bytes 147488 | tf_op jit(solution)/shard_map/ppermute | solution.py:523
  68.9 2.8 %collective-permute-start.20 = (f32[72,512]{1,0:T(8,128)S(1)}, f32[72,512]{1,0:T(8,128)S(1)}, u32[]{:S(2)}, u32[]{:S(2)}) collective-permute-start(f32[72,512]{1,0:T(8,128)S(1)} %pad_maximum_fusion.2), channel_id=1, source_target_pairs={{0,4},{1,5},{2,6},{3,7},{4,0},{5,1},{6,2},{7,3},{8,12},{9,13},{10,... | collective-permute-start | bytes 442376 | tf_op jit(solution)/shard_map/ppermute | solution.py:523
  71.7 2.4 %collective-permute-done.25 = f32[1,64,1024]{2,1,0:T(8,128)S(1)} collective-permute-done((f32[1,64,1024]{2,1,0:T(8,128)S(1)}, f32[1,64,1024]{2,1,0:T(8,128)S(1)}, u32[]{:S(2)}, u32[]{:S(2)}) %collective-permute-start.25) | collective-permute-done | bytes 262176 | tf_op jit(solution)/shard_map/ppermute | solution.py:523
  74.1 0.9 collective-permute-start.26
  75.1 1.5 %collective-permute-done.20 = f32[72,512]{1,0:T(8,128)S(1)} collective-permute-done((f32[72,512]{1,0:T(8,128)S(1)}, f32[72,512]{1,0:T(8,128)S(1)}, u32[]{:S(2)}, u32[]{:S(2)}) %collective-permute-start.20) | collective-permute-done | bytes 147488 | tf_op jit(solution)/shard_map/ppermute | solution.py:523
  76.6 0.7 collective-permute-start.21
  77.8 1.3 %finish.1 = (f32[1,512]{1,0:T(1,128)}, f32[1,256]{1,0:T(1,128)}, f32[1,256]{1,0:T(1,128)}, f32[1,256]{1,0:T(1,128)}, f32[1,512]{1,0:T(1,128)}) custom-call(f32[1,256]{1,0:T(1,128)} %bitcast.69, f32[1,256]{1,0:T(1,128)} %bitcast.71, f32[1,512]{1,0:T(1,128)} %bitcast.66, f32[16,512]{1,0:T(8,128)S(1)} %maximum_select_fusion.9.refs_3_, ...), custom_call_target="tpu_custom_call" | custom-call | flops 1100000000 | bytes 3000000 | tf_op jit(solution)/shard_map/finish/pallas_call | solution.py:663
  79.1 3.5 %collective-permute-done.21 = f32[2,32,512]{2,1,0:T(8,128)S(1)} collective-permute-done((f32[2,32,512]{2,1,0:T(8,128)S(1)}, f32[2,32,512]{2,1,0:T(8,128)S(1)}, u32[]{:S(2)}, u32[]{:S(2)}) %collective-permute-start.21) | collective-permute-done | bytes 131104 | tf_op jit(solution)/shard_map/ppermute | solution.py:523
  82.6 0.7 collective-permute-done.26
  83.5 2.5 %collective-permute-start.28 = (f32[2,64,512]{2,1,0:T(8,128)S(1)}, f32[2,64,512]{2,1,0:T(8,128)S(1)}, u32[]{:S(2)}, u32[]{:S(2)}) collective-permute-start(f32[2,64,512]{2,1,0:T(8,128)S(1)} %maximum_select_fusion.6.refs_8_), channel_id=1, source_target_pairs={{0,16},{8,24},{16,0},{24,8},{1,17},{9,25},{17,1},{25,9},{2,18},{10... | collective-permute-start | bytes 786440 | tf_op jit(solution)/shard_map/ppermute | solution.py:585
  86.1 0.5 collective-permute-start.29
  86.6 1.0 %collective-permute-start.27 = (f32[2,64,512]{2,1,0:T(8,128)S(1)}, f32[2,64,512]{2,1,0:T(8,128)S(1)}, u32[]{:S(2)}, u32[]{:S(2)}) collective-permute-start(f32[2,64,512]{2,1,0:T(8,128)S(1)} %maximum_select_fusion.6.refs_8_), channel_id=1, source_target_pairs={{0,8},{8,0},{16,24},{24,16},{1,9},{9,1},{17,25},{25,17},{2,10},{10... | collective-permute-start | bytes 786440 | tf_op jit(solution)/shard_map/ppermute | solution.py:585
  87.6 5.7 %back_input.1 = (bf16[4,256,512]{2,1,0:T(8,128)(2,1)}, bf16[4,256,512]{2,1,0:T(8,128)(2,1)}) custom-call(f32[1,512]{1,0:T(1,128)} %bitcast.67, bf16[512,512]{1,0:T(8,128)(2,1)} %refs_1_.5, f32[1,512]{1,0:T(1,128)} %bitcast.47, bf16[1024,512]{1,0:T(8,128)(2,1)} %get-tuple-element.68.refs_3_, bf16[1024,512]{1,0:T(8,128)(2,1)} %cotangent_order.1.refs_6_.refs_4_, ...), custom_call_target="tpu_custom_call" | custom-call | flops 4400000000 | bytes 12000000 | tf_op jit(solution)/shard_map/back_input/pallas_call | solution.py:663
  93.3 4.8 %collective-permute-done.27 = f32[2,64,512]{2,1,0:T(8,128)S(1)} collective-permute-done((f32[2,64,512]{2,1,0:T(8,128)S(1)}, f32[2,64,512]{2,1,0:T(8,128)S(1)}, u32[]{:S(2)}, u32[]{:S(2)}) %collective-permute-start.27) | collective-permute-done | bytes 262176 | tf_op jit(solution)/shard_map/ppermute | solution.py:585
  98.5 1.0 copy-done.3
  99.5 1.3 %assemble.3 = f32[512,1024]{1,0:T(8,128)} custom-call(f32[256,1024]{1,0:T(8,128)S(1)} %bitcast.42, f32[256,1024]{1,0:T(8,128)S(1)} %collective-permute-done.32.refs_1_, bf16[4,256,512]{2,1,0:T(8,128)(2,1)S(1)} %copy-done.3), custom_call_target="tpu_custom_call" | custom-call | flops 2200000000 | bytes 6000000 | tf_op jit(solution)/shard_map/assemble/pallas_call | solution.py:663
  101.2 1.3 %assemble.2 = (f32[512,512]{1,0:T(8,128)}, f32[512,512]{1,0:T(8,128)}) custom-call(f32[256,1024]{1,0:T(8,128)S(1)} %pad_maximum_fusion.refs_0_, f32[256,1024]{1,0:T(8,128)S(1)} %collective-permute-done.31.refs_1_), custom_call_target="tpu_custom_call" | custom-call | flops 2200000000 | bytes 6000000 | tf_op jit(solution)/shard_map/assemble/pallas_call | solution.py:663
  (108 shorter events, 4.4 us)
Async XLA Ops:
  0.6 12.0 %copy-start.6 = (f32[4,512]{1,0:T(4,128)S(1)}, f32[4,512]{1,0:T(4,128)}, u32[]{:S(2)}) copy-start(f32[4,512]{1,0:T(4,128)} %constant.184.clone.1) | copy-start | bytes 24580
  5.6 1.3 %collective-permute-start = (f32[8,512]{1,0:T(8,128)S(1)}, f32[8,512]{1,0:T(8,128)S(1)}, u32[]{:S(2)}, u32[]{:S(2)}) collective-permute-start(f32[8,512]{1,0:T(8,128)S(1)} %get-tuple-element.71), channel_id=1, source_target_pairs={{0,1},{1,0},{2,3},{3,2},{4,5},{5,4},{6,7},{7,6},{8,9},{9,8},{10,11... | collective-permute-start | bytes 49160 | tf_op jit(solution)/shard_map/ppermute | solution.py:484
  7.0 8.3 %collective-permute-start.3 = (f32[8,512]{1,0:T(8,128)S(1)}, f32[8,512]{1,0:T(8,128)S(1)}, u32[]{:S(2)}, u32[]{:S(2)}) collective-permute-start(f32[8,512]{1,0:T(8,128)S(1)} %maximum_maximum_fusion), channel_id=1, source_target_pairs={{0,2},{1,3},{2,0},{3,1},{4,6},{5,7},{6,4},{7,5},{8,10},{9,11},{10,... | collective-permute-start | bytes 49160 | tf_op jit(solution)/shard_map/ppermute | solution.py:484
  10.0 5.3 %collective-permute-start.2 = (f32[8,512]{1,0:T(8,128)S(1)}, f32[8,512]{1,0:T(8,128)S(1)}, u32[]{:S(2)}, u32[]{:S(2)}) collective-permute-start(f32[8,512]{1,0:T(8,128)S(1)} %maximum_maximum_fusion), channel_id=1, source_target_pairs={{0,4},{1,5},{2,6},{3,7},{4,0},{5,1},{6,2},{7,3},{8,12},{9,13},{10,... | collective-permute-start | bytes 49160 | tf_op jit(solution)/shard_map/ppermute | solution.py:484
  12.6 5.5 %collective-permute-start.1 = (f32[8,512]{1,0:T(8,128)S(1)}, f32[8,512]{1,0:T(8,128)S(1)}, u32[]{:S(2)}, u32[]{:S(2)}) collective-permute-start(f32[8,512]{1,0:T(8,128)S(1)} %maximum_maximum_fusion), channel_id=1, source_target_pairs={{0,6},{1,7},{2,4},{3,5},{4,2},{5,3},{6,0},{7,1},{8,14},{9,15},{10,... | collective-permute-start | bytes 49160 | tf_op jit(solution)/shard_map/ppermute | solution.py:484
  27.9 2.7 %collective-permute-start.4 = (f32[256,1024]{1,0:T(8,128)S(1)}, f32[256,1024]{1,0:T(8,128)S(1)}, u32[]{:S(2)}, u32[]{:S(2)}) collective-permute-start(f32[256,1024]{1,0:T(8,128)S(1)} %get-tuple-element.86), channel_id=1, source_target_pairs={{0,1},{1,0},{2,3},{3,2},{4,5},{5,4},{6,7},{7,6},{8,9},{9,8},{10,11... | collective-permute-start | bytes 3145736 | tf_op jit(solution)/shard_map/ppermute | solution.py:461
  30.6 11.6 %copy-start = (bf16[512,512]{1,0:T(8,128)(2,1)S(1)}, bf16[512,512]{1,0:T(8,128)(2,1)}, u32[]{:S(2)}) copy-start(bf16[512,512]{1,0:T(8,128)(2,1)} %refs_1_.5) | copy-start | bytes 1572868
  30.6 11.6 %copy-start.1 = (f32[512]{0:T(512)S(1)}, f32[512]{0:T(512)}, u32[]{:S(2)}) copy-start(f32[512]{0:T(512)} %param.22) | copy-start | bytes 6148
  30.6 11.6 %copy-start.2 = (f32[256]{0:T(256)S(1)}, f32[256]{0:T(256)}, u32[]{:S(2)}) copy-start(f32[256]{0:T(256)} %param.18) | copy-start | bytes 3076
  30.6 11.6 %copy-start.5 = (f32[32,512]{1,0:T(8,128)S(1)}, f32[32,512]{1,0:T(8,128)}, u32[]{:S(2)}) copy-start(f32[32,512]{1,0:T(8,128)} %get-tuple-element.83.refs_4_) | copy-start | bytes 196612
  30.8 2.1 %collective-permute-start.5 = (f32[8,512]{1,0:T(8,128)S(1)}, f32[8,512]{1,0:T(8,128)S(1)}, u32[]{:S(2)}, u32[]{:S(2)}) collective-permute-start(f32[8,512]{1,0:T(8,128)S(1)} %maximum_maximum_fusion.1), channel_id=1, source_target_pairs={{0,1},{1,0},{2,3},{3,2},{4,5},{5,4},{6,7},{7,6},{8,9},{9,8},{10,11... | collective-permute-start | bytes 49160 | tf_op jit(solution)/shard_map/ppermute | solution.py:484
  31.0 11.2 %collective-permute-start.9 = (f32[256,512]{1,0:T(8,128)S(1)}, f32[256,512]{1,0:T(8,128)S(1)}, u32[]{:S(2)}, u32[]{:S(2)}) collective-permute-start(f32[256,512]{1,0:T(8,128)S(1)} %get-tuple-element.90), channel_id=1, source_target_pairs={{0,1},{1,0},{2,3},{3,2},{4,5},{5,4},{6,7},{7,6},{8,9},{9,8},{10,11... | collective-permute-start | bytes 1572872 | tf_op jit(solution)/shard_map/ppermute | solution.py:461
  31.3 9.2 %collective-permute-start.10 = (f32[128,1024]{1,0:T(8,128)S(1)}, f32[128,1024]{1,0:T(8,128)S(1)}, u32[]{:S(2)}, u32[]{:S(2)}) collective-permute-start(f32[128,1024]{1,0:T(8,128)S(1)} %get-tuple-element.92), channel_id=1, source_target_pairs={{0,8},{1,17},{2,10},{3,19},{4,12},{5,21},{6,14},{7,23},{8,0},{9,25... | collective-permute-start | bytes 1572872 | tf_op jit(solution)/shard_map/ppermute | solution.py:523
  32.9 4.5 %collective-permute-start.8 = (f32[8,512]{1,0:T(8,128)S(1)}, f32[8,512]{1,0:T(8,128)S(1)}, u32[]{:S(2)}, u32[]{:S(2)}) collective-permute-start(f32[8,512]{1,0:T(8,128)S(1)} %maximum_maximum_fusion.2), channel_id=1, source_target_pairs={{0,2},{1,3},{2,0},{3,1},{4,6},{5,7},{6,4},{7,5},{8,10},{9,11},{10,... | collective-permute-start | bytes 49160 | tf_op jit(solution)/shard_map/ppermute | solution.py:484
  33.0 4.9 %collective-permute-start.7 = (f32[8,512]{1,0:T(8,128)S(1)}, f32[8,512]{1,0:T(8,128)S(1)}, u32[]{:S(2)}, u32[]{:S(2)}) collective-permute-start(f32[8,512]{1,0:T(8,128)S(1)} %maximum_maximum_fusion.2), channel_id=1, source_target_pairs={{0,4},{1,5},{2,6},{3,7},{4,0},{5,1},{6,2},{7,3},{8,12},{9,13},{10,... | collective-permute-start | bytes 49160 | tf_op jit(solution)/shard_map/ppermute | solution.py:484
  34.6 5.5 %collective-permute-start.6 = (f32[8,512]{1,0:T(8,128)S(1)}, f32[8,512]{1,0:T(8,128)S(1)}, u32[]{:S(2)}, u32[]{:S(2)}) collective-permute-start(f32[8,512]{1,0:T(8,128)S(1)} %maximum_maximum_fusion.2), channel_id=1, source_target_pairs={{0,6},{1,7},{2,4},{3,5},{4,2},{5,3},{6,0},{7,1},{8,14},{9,15},{10,... | collective-permute-start | bytes 49160 | tf_op jit(solution)/shard_map/ppermute | solution.py:484
  40.6 6.4 %collective-permute-start.15 = (f32[64,1024]{1,0:T(8,128)S(1)}, f32[64,1024]{1,0:T(8,128)S(1)}, u32[]{:S(2)}, u32[]{:S(2)}) collective-permute-start(f32[64,1024]{1,0:T(8,128)S(1)} %get-tuple-element.101), channel_id=1, source_target_pairs={{0,16},{1,9},{2,18},{3,11},{4,20},{5,13},{6,22},{7,15},{8,24},{9,1... | collective-permute-start | bytes 786440 | tf_op jit(solution)/shard_map/ppermute | solution.py:523
  46.0 8.0 %collective-permute-start.14 = (f32[264,512]{1,0:T(8,128)S(1)}, f32[264,512]{1,0:T(8,128)S(1)}, u32[]{:S(2)}, u32[]{:S(2)}) collective-permute-start(f32[264,512]{1,0:T(8,128)S(1)} %get-tuple-element.100), channel_id=1, source_target_pairs={{0,1},{1,0},{2,3},{3,2},{4,5},{5,4},{6,7},{7,6},{8,9},{9,8},{10,11... | collective-permute-start | bytes 1622024 | tf_op jit(solution)/shard_map/ppermute | solution.py:461
  47.1 5.0 %collective-permute-start.22 = (f32[32,1024]{1,0:T(8,128)S(1)}, f32[32,1024]{1,0:T(8,128)S(1)}, u32[]{:S(2)}, u32[]{:S(2)}) collective-permute-start(f32[32,1024]{1,0:T(8,128)S(1)} %get-tuple-element.108), channel_id=1, source_target_pairs={{0,2},{1,3},{2,0},{3,1},{4,6},{5,7},{6,4},{7,5},{8,10},{9,11},{10,... | collective-permute-start | bytes 393224 | tf_op jit(solution)/shard_map/ppermute | solution.py:523
  47.3 7.5 %collective-permute-start.11 = (f32[1,64,512]{2,1,0:T(8,128)S(1)}, f32[1,64,512]{2,1,0:T(8,128)S(1)}, u32[]{:S(2)}, u32[]{:S(2)}) collective-permute-start(f32[1,64,512]{2,1,0:T(8,128)S(1)} %bitcast.45), channel_id=1, source_target_pairs={{0,8},{8,0},{16,24},{24,16},{1,9},{9,1},{17,25},{25,17},{2,10},{10... | collective-permute-start | bytes 393224 | tf_op jit(solution)/shard_map/ppermute | solution.py:585
  48.9 8.6 %collective-permute-start.12 = (f32[1,64,512]{2,1,0:T(8,128)S(1)}, f32[1,64,512]{2,1,0:T(8,128)S(1)}, u32[]{:S(2)}, u32[]{:S(2)}) collective-permute-start(f32[1,64,512]{2,1,0:T(8,128)S(1)} %bitcast.44), channel_id=1, source_target_pairs={{0,16},{8,24},{16,0},{24,8},{1,17},{9,25},{17,1},{25,9},{2,18},{10... | collective-permute-start | bytes 393224 | tf_op jit(solution)/shard_map/ppermute | solution.py:585
  50.4 7.3 %collective-permute-start.13 = (f32[1,64,512]{2,1,0:T(8,128)S(1)}, f32[1,64,512]{2,1,0:T(8,128)S(1)}, u32[]{:S(2)}, u32[]{:S(2)}) collective-permute-start(f32[1,64,512]{2,1,0:T(8,128)S(1)} %bitcast.43), channel_id=1, source_target_pairs={{0,24},{8,16},{16,8},{24,0},{1,25},{9,17},{17,9},{25,1},{2,26},{10... | collective-permute-start | bytes 393224 | tf_op jit(solution)/shard_map/ppermute | solution.py:585
  52.1 7.6 %collective-permute-start.23 = (f32[1,32,1024]{2,1,0:T(8,128)S(1)}, f32[1,32,1024]{2,1,0:T(8,128)S(1)}, u32[]{:S(2)}, u32[]{:S(2)}) collective-permute-start(f32[1,32,1024]{2,1,0:T(8,128)S(1)} %add_bitcast_fusion), channel_id=1, source_target_pairs={{0,4},{1,5},{2,6},{3,7},{4,0},{5,1},{6,2},{7,3},{8,12},{9,13},{10,... | collective-permute-start | bytes 393224 | tf_op jit(solution)/shard_map/ppermute | solution.py:523
  54.1 6.0 %collective-permute-start.16 = (f32[72,512]{1,0:T(8,128)S(1)}, f32[72,512]{1,0:T(8,128)S(1)}, u32[]{:S(2)}, u32[]{:S(2)}) collective-permute-start(f32[72,512]{1,0:T(8,128)S(1)} %get-tuple-element.104), channel_id=1, source_target_pairs={{0,8},{8,0},{16,24},{24,16},{1,9},{9,1},{17,25},{25,17},{2,10},{10... | collective-permute-start | bytes 442376 | tf_op jit(solution)/shard_map/ppermute | solution.py:585
  54.8 6.5 %collective-permute-start.17 = (f32[72,512]{1,0:T(8,128)S(1)}, f32[72,512]{1,0:T(8,128)S(1)}, u32[]{:S(2)}, u32[]{:S(2)}) collective-permute-start(f32[72,512]{1,0:T(8,128)S(1)} %get-tuple-element.105), channel_id=1, source_target_pairs={{0,16},{8,24},{16,0},{24,8},{1,17},{9,25},{17,1},{25,9},{2,18},{10... | collective-permute-start | bytes 442376 | tf_op jit(solution)/shard_map/ppermute | solution.py:585
  57.5 6.0 %collective-permute-start.18 = (f32[72,512]{1,0:T(8,128)S(1)}, f32[72,512]{1,0:T(8,128)S(1)}, u32[]{:S(2)}, u32[]{:S(2)}) collective-permute-start(f32[72,512]{1,0:T(8,128)S(1)} %get-tuple-element.106), channel_id=1, source_target_pairs={{0,24},{8,16},{16,8},{24,0},{1,25},{9,17},{17,9},{25,1},{2,26},{10... | collective-permute-start | bytes 442376 | tf_op jit(solution)/shard_map/ppermute | solution.py:585
  59.7 5.9 %collective-permute-start.24 = (f32[1,32,1024]{2,1,0:T(8,128)S(1)}, f32[1,32,1024]{2,1,0:T(8,128)S(1)}, u32[]{:S(2)}, u32[]{:S(2)}) collective-permute-start(f32[1,32,1024]{2,1,0:T(8,128)S(1)} %add.263), channel_id=1, source_target_pairs={{0,2},{1,3},{2,0},{3,1},{4,6},{5,7},{6,4},{7,5},{8,10},{9,11},{10,... | collective-permute-start | bytes 393224 | tf_op jit(solution)/shard_map/ppermute | solution.py:523
  63.6 5.2 %collective-permute-start.19 = (f32[72,512]{1,0:T(8,128)S(1)}, f32[72,512]{1,0:T(8,128)S(1)}, u32[]{:S(2)}, u32[]{:S(2)}) collective-permute-start(f32[72,512]{1,0:T(8,128)S(1)} %pad_maximum_fusion.1), channel_id=1, source_target_pairs={{0,2},{1,3},{2,0},{3,1},{4,6},{5,7},{6,4},{7,5},{8,10},{9,11},{10,... | collective-permute-start | bytes 442376 | tf_op jit(solution)/shard_map/ppermute | solution.py:523
  65.7 8.4 %collective-permute-start.25 = (f32[1,64,1024]{2,1,0:T(8,128)S(1)}, f32[1,64,1024]{2,1,0:T(8,128)S(1)}, u32[]{:S(2)}, u32[]{:S(2)}) collective-permute-start(f32[1,64,1024]{2,1,0:T(8,128)S(1)} %maximum_select_fusion.8), channel_id=1, source_target_pairs={{0,16},{1,9},{2,18},{3,11},{4,20},{5,13},{6,22},{7,15},{8,24},{9,1... | collective-permute-start | bytes 786440 | tf_op jit(solution)/shard_map/ppermute | solution.py:523
  68.9 7.7 %collective-permute-start.20 = (f32[72,512]{1,0:T(8,128)S(1)}, f32[72,512]{1,0:T(8,128)S(1)}, u32[]{:S(2)}, u32[]{:S(2)}) collective-permute-start(f32[72,512]{1,0:T(8,128)S(1)} %pad_maximum_fusion.2), channel_id=1, source_target_pairs={{0,4},{1,5},{2,6},{3,7},{4,0},{5,1},{6,2},{7,3},{8,12},{9,13},{10,... | collective-permute-start | bytes 442376 | tf_op jit(solution)/shard_map/ppermute | solution.py:523
  74.1 9.2 %collective-permute-start.26 = (f32[1,128,1024]{2,1,0:T(8,128)S(1)}, f32[1,128,1024]{2,1,0:T(8,128)S(1)}, u32[]{:S(2)}, u32[]{:S(2)}) collective-permute-start(f32[1,128,1024]{2,1,0:T(8,128)S(1)} %maximum_select_fusion.3), channel_id=1, source_target_pairs={{0,8},{1,17},{2,10},{3,19},{4,12},{5,21},{6,14},{7,23},{8,0},{9,25... | collective-permute-start | bytes 1572872 | tf_op jit(solution)/shard_map/ppermute | solution.py:523
  76.6 1.2 %collective-permute-start.30 = (f32[8,512]{1,0:T(8,128)S(1)}, f32[8,512]{1,0:T(8,128)S(1)}, u32[]{:S(2)}, u32[]{:S(2)}) collective-permute-start(f32[8,512]{1,0:T(8,128)S(1)} %slice_add_fusion.2), channel_id=1, source_target_pairs={{0,1},{1,0},{2,3},{3,2},{4,5},{5,4},{6,7},{7,6},{8,9},{9,8},{10,11... | collective-permute-start | bytes 49160 | tf_op jit(solution)/shard_map/ppermute | solution.py:461
  76.6 6.0 %collective-permute-start.21 = (f32[2,32,512]{2,1,0:T(8,128)S(1)}, f32[2,32,512]{2,1,0:T(8,128)S(1)}, u32[]{:S(2)}, u32[]{:S(2)}) collective-permute-start(f32[2,32,512]{2,1,0:T(8,128)S(1)} %fusion.9), channel_id=1, source_target_pairs={{0,2},{1,3},{2,0},{3,1},{4,6},{5,7},{6,4},{7,5},{8,10},{9,11},{10,... | collective-permute-start | bytes 393224 | tf_op jit(solution)/shard_map/ppermute | solution.py:523
  79.1 8.5 %copy-start.4 = (f32[1,512]{1,0:T(1,128)S(1)}, f32[1,512]{1,0:T(1,128)}, u32[]{:S(2)}) copy-start(f32[1,512]{1,0:T(1,128)} %get-tuple-element.113.refs_9_) | copy-start | bytes 6148
  83.5 14.6 %collective-permute-start.28 = (f32[2,64,512]{2,1,0:T(8,128)S(1)}, f32[2,64,512]{2,1,0:T(8,128)S(1)}, u32[]{:S(2)}, u32[]{:S(2)}) collective-permute-start(f32[2,64,512]{2,1,0:T(8,128)S(1)} %maximum_select_fusion.6.refs_8_), channel_id=1, source_target_pairs={{0,16},{8,24},{16,0},{24,8},{1,17},{9,25},{17,1},{25,9},{2,18},{10... | collective-permute-start | bytes 786440 | tf_op jit(solution)/shard_map/ppermute | solution.py:585
  86.1 12.0 %collective-permute-start.29 = (f32[2,64,512]{2,1,0:T(8,128)S(1)}, f32[2,64,512]{2,1,0:T(8,128)S(1)}, u32[]{:S(2)}, u32[]{:S(2)}) collective-permute-start(f32[2,64,512]{2,1,0:T(8,128)S(1)} %maximum_select_fusion.6.refs_8_), channel_id=1, source_target_pairs={{0,24},{8,16},{16,8},{24,0},{1,25},{9,17},{17,9},{25,1},{2,26},{10... | collective-permute-start | bytes 786440 | tf_op jit(solution)/shard_map/ppermute | solution.py:585
  86.6 11.5 %collective-permute-start.27 = (f32[2,64,512]{2,1,0:T(8,128)S(1)}, f32[2,64,512]{2,1,0:T(8,128)S(1)}, u32[]{:S(2)}, u32[]{:S(2)}) collective-permute-start(f32[2,64,512]{2,1,0:T(8,128)S(1)} %maximum_select_fusion.6.refs_8_), channel_id=1, source_target_pairs={{0,8},{8,0},{16,24},{24,16},{1,9},{9,1},{17,25},{25,17},{2,10},{10... | collective-permute-start | bytes 786440 | tf_op jit(solution)/shard_map/ppermute | solution.py:585
  87.6 10.9 %collective-permute-start.32 = (f32[256,1024]{1,0:T(8,128)S(1)}, f32[256,1024]{1,0:T(8,128)S(1)}, u32[]{:S(2)}, u32[]{:S(2)}) collective-permute-start(f32[256,1024]{1,0:T(8,128)S(1)} %bitcast.41), channel_id=1, source_target_pairs={{0,1},{1,0},{2,3},{3,2},{4,5},{5,4},{6,7},{7,6},{8,9},{9,8},{10,11... | collective-permute-start | bytes 3145736 | tf_op jit(solution)/shard_map/ppermute | solution.py:461
  98.3 1.2 %copy-start.3 = (bf16[4,256,512]{2,1,0:T(8,128)(2,1)S(1)}, bf16[4,256,512]{2,1,0:T(8,128)(2,1)}, u32[]{:S(2)}) copy-start(bf16[4,256,512]{2,1,0:T(8,128)(2,1)} %get-tuple-element.117.refs_2_) | copy-start | bytes 3145732
  98.5 2.7 %collective-permute-start.31 = (f32[256,1024]{1,0:T(8,128)S(1)}, f32[256,1024]{1,0:T(8,128)S(1)}, u32[]{:S(2)}, u32[]{:S(2)}) collective-permute-start(f32[256,1024]{1,0:T(8,128)S(1)} %pad_maximum_fusion.refs_0_), channel_id=1, source_target_pairs={{0,1},{1,0},{2,3},{3,2},{4,5},{5,4},{6,7},{7,6},{8,9},{9,8},{10,11... | collective-permute-start | bytes 3145736 | tf_op jit(solution)/shard_map/ppermute | solution.py:461

commit v4 on v3

--- a/solution.py
+++ b/solution.py
@@ -366,7 +366,8 @@
     small_ref[0:1, :n] = jnp.sum(sums[0], axis=0, keepdims=True)
     small_ref[0:1, n:] = jnp.sum(sums[1], axis=0, keepdims=True)
     small_ref[1:2, :] = jnp.sum(prod, axis=0, keepdims=True)
-    small_ref[8:9, :] = jnp.sum(prod.T, axis=0, keepdims=True) + d_ref[...] * g_d_ref[...]
+    narrow = sum(prod[:, k : k + 128] for k in range(0, 2 * n, 128))
+    small_ref[8:9, :] = jnp.sum(narrow.T, axis=0, keepdims=True) + d_ref[...] * g_d_ref[...]
     small_ref[9:10, :] = g_d_ref[...]
     put_halves(grad_b, go_ref.at[pl.ds(0, n)], send_ref.at[pl.ds(0, n)])
     put_halves(small_ref[...], go_ref.at[pl.ds(n, 8)], send_ref.at[pl.ds(n, 8)])

time: 103 us -> 104 us (level)
  starting transfers between devices: 33.7 us -> 37.3 us
  waiting for transfers between devices: 32.3 us -> 29.5 us
    ppermute x10, starting transfers between devices: 12.3 us -> 15.2 us  [hop(): return lax.ppermute(value, ('dp', 'seq'), pairs)]
    ppermute x9, waiting for transfers between devices: 9.59 us -> 7.13 us  [across(): lax.ppermute(value, 'dp', [(i, i ^ mask) for i in range(lax.axis_size('dp...]
  transfers between devices with their start and end apart: 33 -> 33, of which waited for: 22 -> 18; matrix products, arithmetic and copies ran while one was open for 1% -> 1% of each run, Pallas kernels for 16% -> 16%
where the time goes in v4:
time: 104 us; the launch traced here: 103 us
  starting transfers between devices  37.3 us (36%)
  Pallas kernels  32.8 us (32%)
  waiting for transfers between devices  29.5 us (28%)
  between operations  1.53 us (1%)
  other arithmetic  1.12 us (1%)
  local copies, waits for them, and re-layouts  1.08 us (1%)
    pallas_call x14, Pallas kernels, call(): pl.pallas_call(body, in_specs=[hbm] * len(far) + [vmem] * len(near) + [pl...  32.8 us
    ppermute x10, starting transfers between devices, hop(): return lax.ppermute(value, ('dp', 'seq'), pairs)  15.2 us
    ppermute x10, waiting for transfers between devices, hop(): return lax.ppermute(value, ('dp', 'seq'), pairs)  14.9 us
    ppermute x9, starting transfers between devices, across(): lax.ppermute(value, 'dp', [(i, i ^ mask) for i in range(lax.axis_size('dp...  10.8 us
    ppermute x8, starting transfers between devices, entering(): lax.ppermute(pair, 'seq', [(i, i ^ mask << bit) for i in range(count)])  10.7 us
    ppermute x9, waiting for transfers between devices, across(): lax.ppermute(value, 'dp', [(i, i ^ mask) for i in range(lax.axis_size('dp...  7.13 us
    ppermute x8, waiting for transfers between devices, entering(): lax.ppermute(pair, 'seq', [(i, i ^ mask << bit) for i in range(count)])  6.39 us
  transfers between devices with their start and end apart: 33, of which 18 were waited for; matrix products, arithmetic and copies ran while one was open for 1% of the time, Pallas kernels for 16%

profile of v4, /device:TPU:0, one launch (start us, length us, event | category | flops | bytes accessed | tf_op | source)
XLA Modules:
  0.0 103.3 jit_solution(2132417641281259512)
XLA Ops:
  0.7 5.0 %forward_local.1 = (bf16[1024,512]{1,0:T(8,128)(2,1)}, bf16[1024,512]{1,0:T(8,128)(2,1)}, f32[1024,512]{1,0:T(8,128)}, f32[8,512]{1,0:T(8,128)S(1)}, f32[32,512]{1,0:T(8,128)S(1)}, /*index=5*/f32[32,512]{1,0:T(8,128)S(1)}) custom-call(s32[4,16]{1,0:T(4,128)} %bitcast.64, s32[1,4]{1,0:T(1,128)} %refs_1_.3, bf16[4,256,512]{2,1,0:T(8,128)(2,1)} %bitcast.62, ...), custom_call_target="tpu_custom_call" | custom-call | flops 4400000000 | bytes 12000000 | tf_op jit(solution)/shard_map/forward_local/pallas_call | solution.py:664
  5.6 0.5 collective-permute-start
  6.1 0.8 collective-permute-done
  7.0 3.0 %collective-permute-start.3 = (f32[8,512]{1,0:T(8,128)S(1)}, f32[8,512]{1,0:T(8,128)S(1)}, u32[]{:S(2)}, u32[]{:S(2)}) collective-permute-start(f32[8,512]{1,0:T(8,128)S(1)} %maximum_maximum_fusion), channel_id=1, source_target_pairs={{0,2},{1,3},{2,0},{3,1},{4,6},{5,7},{6,4},{7,5},{8,10},{9,11},{10,... | collective-permute-start | bytes 49160 | tf_op jit(solution)/shard_map/ppermute | solution.py:485
  10.0 2.6 %collective-permute-start.2 = (f32[8,512]{1,0:T(8,128)S(1)}, f32[8,512]{1,0:T(8,128)S(1)}, u32[]{:S(2)}, u32[]{:S(2)}) collective-permute-start(f32[8,512]{1,0:T(8,128)S(1)} %maximum_maximum_fusion), channel_id=1, source_target_pairs={{0,4},{1,5},{2,6},{3,7},{4,0},{5,1},{6,2},{7,3},{8,12},{9,13},{10,... | collective-permute-start | bytes 49160 | tf_op jit(solution)/shard_map/ppermute | solution.py:485
  12.6 2.7 %cotangent_order.1.refs_6_.refs_4_ = bf16[1024,512]{1,0:T(8,128)(2,1)} custom-call(bf16[4,256,512]{2,1,0:T(8,128)(2,1)} %bitcast.63), custom_call_target="tpu_custom_call" | custom-call | flops 2200000000 | bytes 6000000 | tf_op jit(solution)/shard_map/cotangent_order/pallas_call | solution.py:664
  15.4 2.8 %collective-permute-done.1 = f32[8,512]{1,0:T(8,128)S(1)} collective-permute-done((f32[8,512]{1,0:T(8,128)S(1)}, f32[8,512]{1,0:T(8,128)S(1)}, u32[]{:S(2)}, u32[]{:S(2)}) %collective-permute-start.1) | collective-permute-done | bytes 16416 | tf_op jit(solution)/shard_map/ppermute | solution.py:485
  18.3 9.6 %block.1 = (bf16[1024,512]{1,0:T(8,128)(2,1)}, f32[1024,512]{1,0:T(8,128)}, f32[1024,512]{1,0:T(8,128)}, f32[1024,512]{1,0:T(8,128)}, f32[32,512]{1,0:T(8,128)},...) custom-call(bf16[512,1024]{1,0:T(8,128)(2,1)} %refs_0_.1, ...), custom_call_target="tpu_custom_call" | custom-call | flops 11000000512 | bytes 30000000 | tf_op jit(solution)/shard_map/block/pallas_call | solution.py:664
  28.0 1.9 %own_grads.1 = (f32[256,512]{1,0:T(8,128)}, f32[256,1024]{1,0:T(8,128)S(1)}, f32[256,512]{1,0:T(8,128)S(1)}) custom-call(bf16[1024,512]{1,0:T(8,128)(2,1)S(1)} %get-tuple-element.76.refs_0_, bf16[1024,1024]{1,0:T(8,128)(2,1)S(1)} %get-tuple-element.77.refs_1_, bf16[1024,512]{1,0:T(8,128)(2,1)S(1)} %get-tuple-element.78.refs_2_, ...), custom_call_target="tpu_custom_call" | custom-call | flops 2200000000 | bytes 6000000 | tf_op jit(solution)/shard_map/own_grads/pallas_call | solution.py:664
  29.9 0.7 collective-permute-done.4.refs_1_
  31.0 0.4 collective-permute-start.9
  31.3 1.5 %collective-permute-start.10 = (f32[128,1024]{1,0:T(8,128)S(1)}, f32[128,1024]{1,0:T(8,128)S(1)}, u32[]{:S(2)}, u32[]{:S(2)}) collective-permute-start(f32[128,1024]{1,0:T(8,128)S(1)} %get-tuple-element.92), channel_id=1, source_target_pairs={{0,8},{1,17},{2,10},{3,19},{4,12},{5,21},{6,14},{7,23},{8,0},{9,25... | collective-permute-start | bytes 1572872 | tf_op jit(solution)/shard_map/ppermute | solution.py:524
  33.0 1.6 %collective-permute-start.7 = (f32[8,512]{1,0:T(8,128)S(1)}, f32[8,512]{1,0:T(8,128)S(1)}, u32[]{:S(2)}, u32[]{:S(2)}) collective-permute-start(f32[8,512]{1,0:T(8,128)S(1)} %maximum_maximum_fusion.2), channel_id=1, source_target_pairs={{0,4},{1,5},{2,6},{3,7},{4,0},{5,1},{6,2},{7,3},{8,12},{9,13},{10,... | collective-permute-start | bytes 49160 | tf_op jit(solution)/shard_map/ppermute | solution.py:485
  34.6 2.8 %collective-permute-start.6 = (f32[8,512]{1,0:T(8,128)S(1)}, f32[8,512]{1,0:T(8,128)S(1)}, u32[]{:S(2)}, u32[]{:S(2)}) collective-permute-start(f32[8,512]{1,0:T(8,128)S(1)} %maximum_maximum_fusion.2), channel_id=1, source_target_pairs={{0,6},{1,7},{2,4},{3,5},{4,2},{5,3},{6,0},{7,1},{8,14},{9,15},{10,... | collective-permute-start | bytes 49160 | tf_op jit(solution)/shard_map/ppermute | solution.py:485
  37.4 0.5 collective-permute-done.7
  37.9 2.3 %collective-permute-done.6 = f32[8,512]{1,0:T(8,128)S(1)} collective-permute-done((f32[8,512]{1,0:T(8,128)S(1)}, f32[8,512]{1,0:T(8,128)S(1)}, u32[]{:S(2)}, u32[]{:S(2)}) %collective-permute-start.6) | collective-permute-done | bytes 16416 | tf_op jit(solution)/shard_map/ppermute | solution.py:485
  40.6 1.6 %collective-permute-start.15 = (f32[64,1024]{1,0:T(8,128)S(1)}, f32[64,1024]{1,0:T(8,128)S(1)}, u32[]{:S(2)}, u32[]{:S(2)}) collective-permute-start(f32[64,1024]{1,0:T(8,128)S(1)} %get-tuple-element.101), channel_id=1, source_target_pairs={{0,16},{1,9},{2,18},{3,11},{4,20},{5,13},{6,22},{7,15},{8,24},{9,1... | collective-permute-start | bytes 786440 | tf_op jit(solution)/shard_map/ppermute | solution.py:524
  42.2 3.7 %adjoint_states.1 = (bf16[1024,512]{1,0:T(8,128)(2,1)}, f32[264,512]{1,0:T(8,128)S(1)}, f32[264,512]{1,0:T(8,128)S(1)}, f32[256,512]{1,0:T(8,128)S(1)}) custom-call(f32[256,512]{1,0:T(8,128)} %get-tuple-element.80.refs_0_, f32[1024,512]{1,0:T(8,128)} %get-tuple-element.81.refs_1_, f32[1024,512]{1,0:T(8,128)} %get-tuple-element.82.refs_2_, ...), custom_call_target="tpu_custom_call" | custom-call | flops 3300000000 | bytes 9000000 | tf_op jit(solution)/shard_map/adjoint_states/pallas_call | solution.py:664
  46.0 1.1 %collective-permute-done.15.refs_1_ = f32[64,1024]{1,0:T(8,128)S(1)} collective-permute-done((f32[64,1024]{1,0:T(8,128)S(1)}, f32[64,1024]{1,0:T(8,128)S(1)}, u32[]{:S(2)}, u32[]{:S(2)}) %collective-permute-start.15) | collective-permute-done | bytes 262176 | tf_op jit(solution)/shard_map/ppermute | solution.py:524
  47.3 1.6 %collective-permute-start.11 = (f32[1,64,512]{2,1,0:T(8,128)S(1)}, f32[1,64,512]{2,1,0:T(8,128)S(1)}, u32[]{:S(2)}, u32[]{:S(2)}) collective-permute-start(f32[1,64,512]{2,1,0:T(8,128)S(1)} %bitcast.45), channel_id=1, source_target_pairs={{0,8},{8,0},{16,24},{24,16},{1,9},{9,1},{17,25},{25,17},{2,10},{10... | collective-permute-start | bytes 393224 | tf_op jit(solution)/shard_map/ppermute | solution.py:586
  48.9 1.5 %collective-permute-start.12 = (f32[1,64,512]{2,1,0:T(8,128)S(1)}, f32[1,64,512]{2,1,0:T(8,128)S(1)}, u32[]{:S(2)}, u32[]{:S(2)}) collective-permute-start(f32[1,64,512]{2,1,0:T(8,128)S(1)} %bitcast.44), channel_id=1, source_target_pairs={{0,16},{8,24},{16,0},{24,8},{1,17},{9,25},{17,1},{25,9},{2,18},{10... | collective-permute-start | bytes 393224 | tf_op jit(solution)/shard_map/ppermute | solution.py:586
  50.4 0.5 collective-permute-start.13
  50.8 1.3 %collective-permute-done.22 = f32[32,1024]{1,0:T(8,128)S(1)} collective-permute-done((f32[32,1024]{1,0:T(8,128)S(1)}, f32[32,1024]{1,0:T(8,128)S(1)}, u32[]{:S(2)}, u32[]{:S(2)}) %collective-permute-start.22) | collective-permute-done | bytes 131104 | tf_op jit(solution)/shard_map/ppermute | solution.py:524
  52.1 1.9 %collective-permute-start.23 = (f32[1,32,1024]{2,1,0:T(8,128)S(1)}, f32[1,32,1024]{2,1,0:T(8,128)S(1)}, u32[]{:S(2)}, u32[]{:S(2)}) collective-permute-start(f32[1,32,1024]{2,1,0:T(8,128)S(1)} %add_bitcast_fusion), channel_id=1, source_target_pairs={{0,4},{1,5},{2,6},{3,7},{4,0},{5,1},{6,2},{7,3},{8,12},{9,13},{10,... | collective-permute-start | bytes 393224 | tf_op jit(solution)/shard_map/ppermute | solution.py:524
  54.1 0.7 collective-permute-start.16
  54.8 1.5 %collective-permute-start.17 = (f32[72,512]{1,0:T(8,128)S(1)}, f32[72,512]{1,0:T(8,128)S(1)}, u32[]{:S(2)}, u32[]{:S(2)}) collective-permute-start(f32[72,512]{1,0:T(8,128)S(1)} %get-tuple-element.105), channel_id=1, source_target_pairs={{0,16},{8,24},{16,0},{24,8},{1,17},{9,25},{17,1},{25,9},{2,18},{10... | collective-permute-start | bytes 442376 | tf_op jit(solution)/shard_map/ppermute | solution.py:586
  56.3 1.3 %collective-permute-start.18 = (f32[72,512]{1,0:T(8,128)S(1)}, f32[72,512]{1,0:T(8,128)S(1)}, u32[]{:S(2)}, u32[]{:S(2)}) collective-permute-start(f32[72,512]{1,0:T(8,128)S(1)} %get-tuple-element.106), channel_id=1, source_target_pairs={{0,24},{8,16},{16,8},{24,0},{1,25},{9,17},{17,9},{25,1},{2,26},{10... | collective-permute-start | bytes 442376 | tf_op jit(solution)/shard_map/ppermute | solution.py:586
  57.7 1.9 %collective-permute-done.23 = f32[1,32,1024]{2,1,0:T(8,128)S(1)} collective-permute-done((f32[1,32,1024]{2,1,0:T(8,128)S(1)}, f32[1,32,1024]{2,1,0:T(8,128)S(1)}, u32[]{:S(2)}, u32[]{:S(2)}) %collective-permute-start.23) | collective-permute-done | bytes 131104 | tf_op jit(solution)/shard_map/ppermute | solution.py:524
  59.7 0.3 collective-permute-done.16
  60.0 2.7 %collective-permute-done.17 = f32[72,512]{1,0:T(8,128)S(1)} collective-permute-done((f32[72,512]{1,0:T(8,128)S(1)}, f32[72,512]{1,0:T(8,128)S(1)}, u32[]{:S(2)}, u32[]{:S(2)}) %collective-permute-start.17) | collective-permute-done | bytes 147488 | tf_op jit(solution)/shard_map/ppermute | solution.py:586
  62.8 1.6 %collective-permute-start.19 = (f32[72,512]{1,0:T(8,128)S(1)}, f32[72,512]{1,0:T(8,128)S(1)}, u32[]{:S(2)}, u32[]{:S(2)}) collective-permute-start(f32[72,512]{1,0:T(8,128)S(1)} %pad_maximum_fusion.1), channel_id=1, source_target_pairs={{0,2},{1,3},{2,0},{3,1},{4,6},{5,7},{6,4},{7,5},{8,10},{9,11},{10,... | collective-permute-start | bytes 442376 | tf_op jit(solution)/shard_map/ppermute | solution.py:524
  64.4 1.1 %collective-permute-done.24 = f32[1,32,1024]{2,1,0:T(8,128)S(1)} collective-permute-done((f32[1,32,1024]{2,1,0:T(8,128)S(1)}, f32[1,32,1024]{2,1,0:T(8,128)S(1)}, u32[]{:S(2)}, u32[]{:S(2)}) %collective-permute-start.24) | collective-permute-done | bytes 131104 | tf_op jit(solution)/shard_map/ppermute | solution.py:524
  65.5 3.2 %collective-permute-start.25 = (f32[1,64,1024]{2,1,0:T(8,128)S(1)}, f32[1,64,1024]{2,1,0:T(8,128)S(1)}, u32[]{:S(2)}, u32[]{:S(2)}) collective-permute-start(f32[1,64,1024]{2,1,0:T(8,128)S(1)} %maximum_select_fusion.8), channel_id=1, source_target_pairs={{0,16},{1,9},{2,18},{3,11},{4,20},{5,13},{6,22},{7,15},{8,24},{9,1... | collective-permute-start | bytes 786440 | tf_op jit(solution)/shard_map/ppermute | solution.py:524
  68.8 3.9 %collective-permute-start.20 = (f32[72,512]{1,0:T(8,128)S(1)}, f32[72,512]{1,0:T(8,128)S(1)}, u32[]{:S(2)}, u32[]{:S(2)}) collective-permute-start(f32[72,512]{1,0:T(8,128)S(1)} %pad_maximum_fusion.2), channel_id=1, source_target_pairs={{0,4},{1,5},{2,6},{3,7},{4,0},{5,1},{6,2},{7,3},{8,12},{9,13},{10,... | collective-permute-start | bytes 442376 | tf_op jit(solution)/shard_map/ppermute | solution.py:524
  72.6 3.1 %collective-permute-done.25 = f32[1,64,1024]{2,1,0:T(8,128)S(1)} collective-permute-done((f32[1,64,1024]{2,1,0:T(8,128)S(1)}, f32[1,64,1024]{2,1,0:T(8,128)S(1)}, u32[]{:S(2)}, u32[]{:S(2)}) %collective-permute-start.25) | collective-permute-done | bytes 262176 | tf_op jit(solution)/shard_map/ppermute | solution.py:524
  75.9 0.8 collective-permute-done.20
  76.8 1.3 %collective-permute-start.21 = (f32[2,32,512]{2,1,0:T(8,128)S(1)}, f32[2,32,512]{2,1,0:T(8,128)S(1)}, u32[]{:S(2)}, u32[]{:S(2)}) collective-permute-start(f32[2,32,512]{2,1,0:T(8,128)S(1)} %fusion.9), channel_id=1, source_target_pairs={{0,2},{1,3},{2,0},{3,1},{4,6},{5,7},{6,4},{7,5},{8,10},{9,11},{10,... | collective-permute-start | bytes 393224 | tf_op jit(solution)/shard_map/ppermute | solution.py:524
  78.1 1.3 %finish.1 = (f32[1,512]{1,0:T(1,128)}, f32[1,256]{1,0:T(1,128)}, f32[1,256]{1,0:T(1,128)}, f32[1,256]{1,0:T(1,128)}, f32[1,512]{1,0:T(1,128)}) custom-call(f32[1,256]{1,0:T(1,128)} %bitcast.69, f32[1,256]{1,0:T(1,128)} %bitcast.71, f32[1,512]{1,0:T(1,128)} %bitcast.66, f32[16,512]{1,0:T(8,128)S(1)} %maximum_select_fusion.9.refs_3_, ...), custom_call_target="tpu_custom_call" | custom-call | flops 1100000000 | bytes 3000000 | tf_op jit(solution)/shard_map/finish/pallas_call | solution.py:664
  79.5 3.3 %collective-permute-done.21 = f32[2,32,512]{2,1,0:T(8,128)S(1)} collective-permute-done((f32[2,32,512]{2,1,0:T(8,128)S(1)}, f32[2,32,512]{2,1,0:T(8,128)S(1)}, u32[]{:S(2)}, u32[]{:S(2)}) %collective-permute-start.21) | collective-permute-done | bytes 131104 | tf_op jit(solution)/shard_map/ppermute | solution.py:524
  82.8 2.3 %collective-permute-done.26 = f32[1,128,1024]{2,1,0:T(8,128)S(1)} collective-permute-done((f32[1,128,1024]{2,1,0:T(8,128)S(1)}, f32[1,128,1024]{2,1,0:T(8,128)S(1)}, u32[]{:S(2)}, u32[]{:S(2)}) %collective-permute-start.26) | collective-permute-done | bytes 524320 | tf_op jit(solution)/shard_map/ppermute | solution.py:524
  85.2 2.1 %collective-permute-start.28 = (f32[2,64,512]{2,1,0:T(8,128)S(1)}, f32[2,64,512]{2,1,0:T(8,128)S(1)}, u32[]{:S(2)}, u32[]{:S(2)}) collective-permute-start(f32[2,64,512]{2,1,0:T(8,128)S(1)} %maximum_select_fusion.6.refs_8_), channel_id=1, source_target_pairs={{0,16},{8,24},{16,0},{24,8},{1,17},{9,25},{17,1},{25,9},{2,18},{10... | collective-permute-start | bytes 786440 | tf_op jit(solution)/shard_map/ppermute | solution.py:586
  87.4 1.5 %collective-permute-start.27 = (f32[2,64,512]{2,1,0:T(8,128)S(1)}, f32[2,64,512]{2,1,0:T(8,128)S(1)}, u32[]{:S(2)}, u32[]{:S(2)}) collective-permute-start(f32[2,64,512]{2,1,0:T(8,128)S(1)} %maximum_select_fusion.6.refs_8_), channel_id=1, source_target_pairs={{0,8},{8,0},{16,24},{24,16},{1,9},{9,1},{17,25},{25,17},{2,10},{10... | collective-permute-start | bytes 786440 | tf_op jit(solution)/shard_map/ppermute | solution.py:586
  88.9 5.7 %back_input.1 = (bf16[4,256,512]{2,1,0:T(8,128)(2,1)}, bf16[4,256,512]{2,1,0:T(8,128)(2,1)}) custom-call(f32[1,512]{1,0:T(1,128)} %bitcast.67, bf16[512,512]{1,0:T(8,128)(2,1)} %refs_1_.5, f32[1,512]{1,0:T(1,128)} %bitcast.47, bf16[1024,512]{1,0:T(8,128)(2,1)} %get-tuple-element.68.refs_3_, bf16[1024,512]{1,0:T(8,128)(2,1)} %cotangent_order.1.refs_6_.refs_4_, ...), custom_call_target="tpu_custom_call" | custom-call | flops 4400000000 | bytes 12000000 | tf_op jit(solution)/shard_map/back_input/pallas_call | solution.py:664
  94.5 4.1 %collective-permute-done.27 = f32[2,64,512]{2,1,0:T(8,128)S(1)} collective-permute-done((f32[2,64,512]{2,1,0:T(8,128)S(1)}, f32[2,64,512]{2,1,0:T(8,128)S(1)}, u32[]{:S(2)}, u32[]{:S(2)}) %collective-permute-start.27) | collective-permute-done | bytes 262176 | tf_op jit(solution)/shard_map/ppermute | solution.py:586
  99.1 1.0 copy-done.3
  100.1 1.3 %assemble.3 = f32[512,1024]{1,0:T(8,128)} custom-call(f32[256,1024]{1,0:T(8,128)S(1)} %bitcast.42, f32[256,1024]{1,0:T(8,128)S(1)} %collective-permute-done.32.refs_1_, bf16[4,256,512]{2,1,0:T(8,128)(2,1)S(1)} %copy-done.3), custom_call_target="tpu_custom_call" | custom-call | flops 2200000000 | bytes 6000000 | tf_op jit(solution)/shard_map/assemble/pallas_call | solution.py:664
  101.4 0.3 collective-permute-done.31.refs_1_
  101.8 1.3 %assemble.2 = (f32[512,512]{1,0:T(8,128)}, f32[512,512]{1,0:T(8,128)}) custom-call(f32[256,1024]{1,0:T(8,128)S(1)} %pad_maximum_fusion.refs_0_, f32[256,1024]{1,0:T(8,128)S(1)} %collective-permute-done.31.refs_1_), custom_call_target="tpu_custom_call" | custom-call | flops 2200000000 | bytes 6000000 | tf_op jit(solution)/shard_map/assemble/pallas_call | solution.py:664
  (108 shorter events, 2.6 us)
Async XLA Ops:
  0.6 12.0 %copy-start.6 = (f32[4,512]{1,0:T(4,128)S(1)}, f32[4,512]{1,0:T(4,128)}, u32[]{:S(2)}) copy-start(f32[4,512]{1,0:T(4,128)} %constant.184.clone.1) | copy-start | bytes 24580
  5.6 1.3 %collective-permute-start = (f32[8,512]{1,0:T(8,128)S(1)}, f32[8,512]{1,0:T(8,128)S(1)}, u32[]{:S(2)}, u32[]{:S(2)}) collective-permute-start(f32[8,512]{1,0:T(8,128)S(1)} %get-tuple-element.71), channel_id=1, source_target_pairs={{0,1},{1,0},{2,3},{3,2},{4,5},{5,4},{6,7},{7,6},{8,9},{9,8},{10,11... | collective-permute-start | bytes 49160 | tf_op jit(solution)/shard_map/ppermute | solution.py:485
  7.0 8.3 %collective-permute-start.3 = (f32[8,512]{1,0:T(8,128)S(1)}, f32[8,512]{1,0:T(8,128)S(1)}, u32[]{:S(2)}, u32[]{:S(2)}) collective-permute-start(f32[8,512]{1,0:T(8,128)S(1)} %maximum_maximum_fusion), channel_id=1, source_target_pairs={{0,2},{1,3},{2,0},{3,1},{4,6},{5,7},{6,4},{7,5},{8,10},{9,11},{10,... | collective-permute-start | bytes 49160 | tf_op jit(solution)/shard_map/ppermute | solution.py:485
  10.0 5.3 %collective-permute-start.2 = (f32[8,512]{1,0:T(8,128)S(1)}, f32[8,512]{1,0:T(8,128)S(1)}, u32[]{:S(2)}, u32[]{:S(2)}) collective-permute-start(f32[8,512]{1,0:T(8,128)S(1)} %maximum_maximum_fusion), channel_id=1, source_target_pairs={{0,4},{1,5},{2,6},{3,7},{4,0},{5,1},{6,2},{7,3},{8,12},{9,13},{10,... | collective-permute-start | bytes 49160 | tf_op jit(solution)/shard_map/ppermute | solution.py:485
  12.6 5.5 %collective-permute-start.1 = (f32[8,512]{1,0:T(8,128)S(1)}, f32[8,512]{1,0:T(8,128)S(1)}, u32[]{:S(2)}, u32[]{:S(2)}) collective-permute-start(f32[8,512]{1,0:T(8,128)S(1)} %maximum_maximum_fusion), channel_id=1, source_target_pairs={{0,6},{1,7},{2,4},{3,5},{4,2},{5,3},{6,0},{7,1},{8,14},{9,15},{10,... | collective-permute-start | bytes 49160 | tf_op jit(solution)/shard_map/ppermute | solution.py:485
  27.9 2.7 %collective-permute-start.4 = (f32[256,1024]{1,0:T(8,128)S(1)}, f32[256,1024]{1,0:T(8,128)S(1)}, u32[]{:S(2)}, u32[]{:S(2)}) collective-permute-start(f32[256,1024]{1,0:T(8,128)S(1)} %get-tuple-element.86), channel_id=1, source_target_pairs={{0,1},{1,0},{2,3},{3,2},{4,5},{5,4},{6,7},{7,6},{8,9},{9,8},{10,11... | collective-permute-start | bytes 3145736 | tf_op jit(solution)/shard_map/ppermute | solution.py:462
  30.6 11.6 %copy-start = (bf16[512,512]{1,0:T(8,128)(2,1)S(1)}, bf16[512,512]{1,0:T(8,128)(2,1)}, u32[]{:S(2)}) copy-start(bf16[512,512]{1,0:T(8,128)(2,1)} %refs_1_.5) | copy-start | bytes 1572868
  30.6 11.6 %copy-start.1 = (f32[512]{0:T(512)S(1)}, f32[512]{0:T(512)}, u32[]{:S(2)}) copy-start(f32[512]{0:T(512)} %param.22) | copy-start | bytes 6148
  30.6 11.6 %copy-start.2 = (f32[256]{0:T(256)S(1)}, f32[256]{0:T(256)}, u32[]{:S(2)}) copy-start(f32[256]{0:T(256)} %param.18) | copy-start | bytes 3076
  30.6 11.6 %copy-start.5 = (f32[32,512]{1,0:T(8,128)S(1)}, f32[32,512]{1,0:T(8,128)}, u32[]{:S(2)}) copy-start(f32[32,512]{1,0:T(8,128)} %get-tuple-element.83.refs_4_) | copy-start | bytes 196612
  30.8 2.1 %collective-permute-start.5 = (f32[8,512]{1,0:T(8,128)S(1)}, f32[8,512]{1,0:T(8,128)S(1)}, u32[]{:S(2)}, u32[]{:S(2)}) collective-permute-start(f32[8,512]{1,0:T(8,128)S(1)} %maximum_maximum_fusion.1), channel_id=1, source_target_pairs={{0,1},{1,0},{2,3},{3,2},{4,5},{5,4},{6,7},{7,6},{8,9},{9,8},{10,11... | collective-permute-start | bytes 49160 | tf_op jit(solution)/shard_map/ppermute | solution.py:485
  31.0 11.2 %collective-permute-start.9 = (f32[256,512]{1,0:T(8,128)S(1)}, f32[256,512]{1,0:T(8,128)S(1)}, u32[]{:S(2)}, u32[]{:S(2)}) collective-permute-start(f32[256,512]{1,0:T(8,128)S(1)} %get-tuple-element.90), channel_id=1, source_target_pairs={{0,1},{1,0},{2,3},{3,2},{4,5},{5,4},{6,7},{7,6},{8,9},{9,8},{10,11... | collective-permute-start | bytes 1572872 | tf_op jit(solution)/shard_map/ppermute | solution.py:462
  31.3 9.2 %collective-permute-start.10 = (f32[128,1024]{1,0:T(8,128)S(1)}, f32[128,1024]{1,0:T(8,128)S(1)}, u32[]{:S(2)}, u32[]{:S(2)}) collective-permute-start(f32[128,1024]{1,0:T(8,128)S(1)} %get-tuple-element.92), channel_id=1, source_target_pairs={{0,8},{1,17},{2,10},{3,19},{4,12},{5,21},{6,14},{7,23},{8,0},{9,25... | collective-permute-start | bytes 1572872 | tf_op jit(solution)/shard_map/ppermute | solution.py:524
  32.9 4.5 %collective-permute-start.8 = (f32[8,512]{1,0:T(8,128)S(1)}, f32[8,512]{1,0:T(8,128)S(1)}, u32[]{:S(2)}, u32[]{:S(2)}) collective-permute-start(f32[8,512]{1,0:T(8,128)S(1)} %maximum_maximum_fusion.2), channel_id=1, source_target_pairs={{0,2},{1,3},{2,0},{3,1},{4,6},{5,7},{6,4},{7,5},{8,10},{9,11},{10,... | collective-permute-start | bytes 49160 | tf_op jit(solution)/shard_map/ppermute | solution.py:485
  33.0 4.9 %collective-permute-start.7 = (f32[8,512]{1,0:T(8,128)S(1)}, f32[8,512]{1,0:T(8,128)S(1)}, u32[]{:S(2)}, u32[]{:S(2)}) collective-permute-start(f32[8,512]{1,0:T(8,128)S(1)} %maximum_maximum_fusion.2), channel_id=1, source_target_pairs={{0,4},{1,5},{2,6},{3,7},{4,0},{5,1},{6,2},{7,3},{8,12},{9,13},{10,... | collective-permute-start | bytes 49160 | tf_op jit(solution)/shard_map/ppermute | solution.py:485
  34.6 5.5 %collective-permute-start.6 = (f32[8,512]{1,0:T(8,128)S(1)}, f32[8,512]{1,0:T(8,128)S(1)}, u32[]{:S(2)}, u32[]{:S(2)}) collective-permute-start(f32[8,512]{1,0:T(8,128)S(1)} %maximum_maximum_fusion.2), channel_id=1, source_target_pairs={{0,6},{1,7},{2,4},{3,5},{4,2},{5,3},{6,0},{7,1},{8,14},{9,15},{10,... | collective-permute-start | bytes 49160 | tf_op jit(solution)/shard_map/ppermute | solution.py:485
  40.6 6.4 %collective-permute-start.15 = (f32[64,1024]{1,0:T(8,128)S(1)}, f32[64,1024]{1,0:T(8,128)S(1)}, u32[]{:S(2)}, u32[]{:S(2)}) collective-permute-start(f32[64,1024]{1,0:T(8,128)S(1)} %get-tuple-element.101), channel_id=1, source_target_pairs={{0,16},{1,9},{2,18},{3,11},{4,20},{5,13},{6,22},{7,15},{8,24},{9,1... | collective-permute-start | bytes 786440 | tf_op jit(solution)/shard_map/ppermute | solution.py:524
  45.9 8.1 %collective-permute-start.14 = (f32[264,512]{1,0:T(8,128)S(1)}, f32[264,512]{1,0:T(8,128)S(1)}, u32[]{:S(2)}, u32[]{:S(2)}) collective-permute-start(f32[264,512]{1,0:T(8,128)S(1)} %get-tuple-element.100), channel_id=1, source_target_pairs={{0,1},{1,0},{2,3},{3,2},{4,5},{5,4},{6,7},{7,6},{8,9},{9,8},{10,11... | collective-permute-start | bytes 1622024 | tf_op jit(solution)/shard_map/ppermute | solution.py:462
  47.1 5.0 %collective-permute-start.22 = (f32[32,1024]{1,0:T(8,128)S(1)}, f32[32,1024]{1,0:T(8,128)S(1)}, u32[]{:S(2)}, u32[]{:S(2)}) collective-permute-start(f32[32,1024]{1,0:T(8,128)S(1)} %get-tuple-element.108), channel_id=1, source_target_pairs={{0,2},{1,3},{2,0},{3,1},{4,6},{5,7},{6,4},{7,5},{8,10},{9,11},{10,... | collective-permute-start | bytes 393224 | tf_op jit(solution)/shard_map/ppermute | solution.py:524
  47.3 7.5 %collective-permute-start.11 = (f32[1,64,512]{2,1,0:T(8,128)S(1)}, f32[1,64,512]{2,1,0:T(8,128)S(1)}, u32[]{:S(2)}, u32[]{:S(2)}) collective-permute-start(f32[1,64,512]{2,1,0:T(8,128)S(1)} %bitcast.45), channel_id=1, source_target_pairs={{0,8},{8,0},{16,24},{24,16},{1,9},{9,1},{17,25},{25,17},{2,10},{10... | collective-permute-start | bytes 393224 | tf_op jit(solution)/shard_map/ppermute | solution.py:586
  48.9 7.5 %collective-permute-start.12 = (f32[1,64,512]{2,1,0:T(8,128)S(1)}, f32[1,64,512]{2,1,0:T(8,128)S(1)}, u32[]{:S(2)}, u32[]{:S(2)}) collective-permute-start(f32[1,64,512]{2,1,0:T(8,128)S(1)} %bitcast.44), channel_id=1, source_target_pairs={{0,16},{8,24},{16,0},{24,8},{1,17},{9,25},{17,1},{25,9},{2,18},{10... | collective-permute-start | bytes 393224 | tf_op jit(solution)/shard_map/ppermute | solution.py:586
  50.4 7.3 %collective-permute-start.13 = (f32[1,64,512]{2,1,0:T(8,128)S(1)}, f32[1,64,512]{2,1,0:T(8,128)S(1)}, u32[]{:S(2)}, u32[]{:S(2)}) collective-permute-start(f32[1,64,512]{2,1,0:T(8,128)S(1)} %bitcast.43), channel_id=1, source_target_pairs={{0,24},{8,16},{16,8},{24,0},{1,25},{9,17},{17,9},{25,1},{2,26},{10... | collective-permute-start | bytes 393224 | tf_op jit(solution)/shard_map/ppermute | solution.py:586
  52.1 7.5 %collective-permute-start.23 = (f32[1,32,1024]{2,1,0:T(8,128)S(1)}, f32[1,32,1024]{2,1,0:T(8,128)S(1)}, u32[]{:S(2)}, u32[]{:S(2)}) collective-permute-start(f32[1,32,1024]{2,1,0:T(8,128)S(1)} %add_bitcast_fusion), channel_id=1, source_target_pairs={{0,4},{1,5},{2,6},{3,7},{4,0},{5,1},{6,2},{7,3},{8,12},{9,13},{10,... | collective-permute-start | bytes 393224 | tf_op jit(solution)/shard_map/ppermute | solution.py:524
  54.1 6.0 %collective-permute-start.16 = (f32[72,512]{1,0:T(8,128)S(1)}, f32[72,512]{1,0:T(8,128)S(1)}, u32[]{:S(2)}, u32[]{:S(2)}) collective-permute-start(f32[72,512]{1,0:T(8,128)S(1)} %get-tuple-element.104), channel_id=1, source_target_pairs={{0,8},{8,0},{16,24},{24,16},{1,9},{9,1},{17,25},{25,17},{2,10},{10... | collective-permute-start | bytes 442376 | tf_op jit(solution)/shard_map/ppermute | solution.py:586
  54.8 7.9 %collective-permute-start.17 = (f32[72,512]{1,0:T(8,128)S(1)}, f32[72,512]{1,0:T(8,128)S(1)}, u32[]{:S(2)}, u32[]{:S(2)}) collective-permute-start(f32[72,512]{1,0:T(8,128)S(1)} %get-tuple-element.105), channel_id=1, source_target_pairs={{0,16},{8,24},{16,0},{24,8},{1,17},{9,25},{17,1},{25,9},{2,18},{10... | collective-permute-start | bytes 442376 | tf_op jit(solution)/shard_map/ppermute | solution.py:586
  56.3 6.4 %collective-permute-start.18 = (f32[72,512]{1,0:T(8,128)S(1)}, f32[72,512]{1,0:T(8,128)S(1)}, u32[]{:S(2)}, u32[]{:S(2)}) collective-permute-start(f32[72,512]{1,0:T(8,128)S(1)} %get-tuple-element.106), channel_id=1, source_target_pairs={{0,24},{8,16},{16,8},{24,0},{1,25},{9,17},{17,9},{25,1},{2,26},{10... | collective-permute-start | bytes 442376 | tf_op jit(solution)/shard_map/ppermute | solution.py:586
  59.6 5.8 %collective-permute-start.24 = (f32[1,32,1024]{2,1,0:T(8,128)S(1)}, f32[1,32,1024]{2,1,0:T(8,128)S(1)}, u32[]{:S(2)}, u32[]{:S(2)}) collective-permute-start(f32[1,32,1024]{2,1,0:T(8,128)S(1)} %add.263), channel_id=1, source_target_pairs={{0,2},{1,3},{2,0},{3,1},{4,6},{5,7},{6,4},{7,5},{8,10},{9,11},{10,... | collective-permute-start | bytes 393224 | tf_op jit(solution)/shard_map/ppermute | solution.py:524
  62.8 5.9 %collective-permute-start.19 = (f32[72,512]{1,0:T(8,128)S(1)}, f32[72,512]{1,0:T(8,128)S(1)}, u32[]{:S(2)}, u32[]{:S(2)}) collective-permute-start(f32[72,512]{1,0:T(8,128)S(1)} %pad_maximum_fusion.1), channel_id=1, source_target_pairs={{0,2},{1,3},{2,0},{3,1},{4,6},{5,7},{6,4},{7,5},{8,10},{9,11},{10,... | collective-permute-start | bytes 442376 | tf_op jit(solution)/shard_map/ppermute | solution.py:524
  65.5 10.3 %collective-permute-start.25 = (f32[1,64,1024]{2,1,0:T(8,128)S(1)}, f32[1,64,1024]{2,1,0:T(8,128)S(1)}, u32[]{:S(2)}, u32[]{:S(2)}) collective-permute-start(f32[1,64,1024]{2,1,0:T(8,128)S(1)} %maximum_select_fusion.8), channel_id=1, source_target_pairs={{0,16},{1,9},{2,18},{3,11},{4,20},{5,13},{6,22},{7,15},{8,24},{9,1... | collective-permute-start | bytes 786440 | tf_op jit(solution)/shard_map/ppermute | solution.py:524
  68.8 8.0 %collective-permute-start.20 = (f32[72,512]{1,0:T(8,128)S(1)}, f32[72,512]{1,0:T(8,128)S(1)}, u32[]{:S(2)}, u32[]{:S(2)}) collective-permute-start(f32[72,512]{1,0:T(8,128)S(1)} %pad_maximum_fusion.2), channel_id=1, source_target_pairs={{0,4},{1,5},{2,6},{3,7},{4,0},{5,1},{6,2},{7,3},{8,12},{9,13},{10,... | collective-permute-start | bytes 442376 | tf_op jit(solution)/shard_map/ppermute | solution.py:524
  75.8 9.2 %collective-permute-start.26 = (f32[1,128,1024]{2,1,0:T(8,128)S(1)}, f32[1,128,1024]{2,1,0:T(8,128)S(1)}, u32[]{:S(2)}, u32[]{:S(2)}) collective-permute-start(f32[1,128,1024]{2,1,0:T(8,128)S(1)} %maximum_select_fusion.3), channel_id=1, source_target_pairs={{0,8},{1,17},{2,10},{3,19},{4,12},{5,21},{6,14},{7,23},{8,0},{9,25... | collective-permute-start | bytes 1572872 | tf_op jit(solution)/shard_map/ppermute | solution.py:524
  76.7 1.4 %collective-permute-start.30 = (f32[8,512]{1,0:T(8,128)S(1)}, f32[8,512]{1,0:T(8,128)S(1)}, u32[]{:S(2)}, u32[]{:S(2)}) collective-permute-start(f32[8,512]{1,0:T(8,128)S(1)} %slice_add_fusion.2), channel_id=1, source_target_pairs={{0,1},{1,0},{2,3},{3,2},{4,5},{5,4},{6,7},{7,6},{8,9},{9,8},{10,11... | collective-permute-start | bytes 49160 | tf_op jit(solution)/shard_map/ppermute | solution.py:462
  76.8 6.0 %collective-permute-start.21 = (f32[2,32,512]{2,1,0:T(8,128)S(1)}, f32[2,32,512]{2,1,0:T(8,128)S(1)}, u32[]{:S(2)}, u32[]{:S(2)}) collective-permute-start(f32[2,32,512]{2,1,0:T(8,128)S(1)} %fusion.9), channel_id=1, source_target_pairs={{0,2},{1,3},{2,0},{3,1},{4,6},{5,7},{6,4},{7,5},{8,10},{9,11},{10,... | collective-permute-start | bytes 393224 | tf_op jit(solution)/shard_map/ppermute | solution.py:524
  79.5 9.4 %copy-start.4 = (f32[1,512]{1,0:T(1,128)S(1)}, f32[1,512]{1,0:T(1,128)}, u32[]{:S(2)}) copy-start(f32[1,512]{1,0:T(1,128)} %get-tuple-element.113.refs_9_) | copy-start | bytes 6148
  85.2 13.5 %collective-permute-start.28 = (f32[2,64,512]{2,1,0:T(8,128)S(1)}, f32[2,64,512]{2,1,0:T(8,128)S(1)}, u32[]{:S(2)}, u32[]{:S(2)}) collective-permute-start(f32[2,64,512]{2,1,0:T(8,128)S(1)} %maximum_select_fusion.6.refs_8_), channel_id=1, source_target_pairs={{0,16},{8,24},{16,0},{24,8},{1,17},{9,25},{17,1},{25,9},{2,18},{10... | collective-permute-start | bytes 786440 | tf_op jit(solution)/shard_map/ppermute | solution.py:586
  87.3 11.4 %collective-permute-start.29 = (f32[2,64,512]{2,1,0:T(8,128)S(1)}, f32[2,64,512]{2,1,0:T(8,128)S(1)}, u32[]{:S(2)}, u32[]{:S(2)}) collective-permute-start(f32[2,64,512]{2,1,0:T(8,128)S(1)} %maximum_select_fusion.6.refs_8_), channel_id=1, source_target_pairs={{0,24},{8,16},{16,8},{24,0},{1,25},{9,17},{17,9},{25,1},{2,26},{10... | collective-permute-start | bytes 786440 | tf_op jit(solution)/shard_map/ppermute | solution.py:586
  87.4 11.3 %collective-permute-start.27 = (f32[2,64,512]{2,1,0:T(8,128)S(1)}, f32[2,64,512]{2,1,0:T(8,128)S(1)}, u32[]{:S(2)}, u32[]{:S(2)}) collective-permute-start(f32[2,64,512]{2,1,0:T(8,128)S(1)} %maximum_select_fusion.6.refs_8_), channel_id=1, source_target_pairs={{0,8},{8,0},{16,24},{24,16},{1,9},{9,1},{17,25},{25,17},{2,10},{10... | collective-permute-start | bytes 786440 | tf_op jit(solution)/shard_map/ppermute | solution.py:586
  88.9 10.3 %collective-permute-start.32 = (f32[256,1024]{1,0:T(8,128)S(1)}, f32[256,1024]{1,0:T(8,128)S(1)}, u32[]{:S(2)}, u32[]{:S(2)}) collective-permute-start(f32[256,1024]{1,0:T(8,128)S(1)} %bitcast.41), channel_id=1, source_target_pairs={{0,1},{1,0},{2,3},{3,2},{4,5},{5,4},{6,7},{7,6},{8,9},{9,8},{10,11... | collective-permute-start | bytes 3145736 | tf_op jit(solution)/shard_map/ppermute | solution.py:462
  98.9 1.2 %copy-start.3 = (bf16[4,256,512]{2,1,0:T(8,128)(2,1)S(1)}, bf16[4,256,512]{2,1,0:T(8,128)(2,1)}, u32[]{:S(2)}) copy-start(bf16[4,256,512]{2,1,0:T(8,128)(2,1)} %get-tuple-element.117.refs_2_) | copy-start | bytes 3145732
  99.1 2.7 %collective-permute-start.31 = (f32[256,1024]{1,0:T(8,128)S(1)}, f32[256,1024]{1,0:T(8,128)S(1)}, u32[]{:S(2)}, u32[]{:S(2)}) collective-permute-start(f32[256,1024]{1,0:T(8,128)S(1)} %pad_maximum_fusion.refs_0_), channel_id=1, source_target_pairs={{0,1},{1,0},{2,3},{3,2},{4,5},{5,4},{6,7},{7,6},{8,9},{9,8},{10,11... | collective-permute-start | bytes 3145736 | tf_op jit(solution)/shard_map/ppermute | solution.py:462
